TPU v7x, 32 devices: a whole 2x2x4 slice. The times are simulated.
32 devices in a mesh: row: 4 (over y, core), col: 8 (over z, x).
Axes of the slice: x: 2, y: 2, z: 4, core: 2. Of those that a mesh axis runs over, the one named last changes fastest.
Arguments:
- prolong: bfloat16 [6144, 2048], P('col', 'row'), may hold values from -0.21875 to 0.21875
- applied: bfloat16 [6144, 2048], P('row', 'col'), may hold values from -6 to 6
- prolong_pattern: int32 [48, 16], P('col', 'row'), may hold values from 0 to 1, as said below
- applied_pattern: int32 [48, 16], P('row', 'col'), may hold values from 0 to 1, as said below
Outputs:
- coarse_operator: float32 [2048, 2048], P('row', 'col')
Inputs may be any that keep to these rules, and one draw needn't show every extreme that they name: In each fine tile row a, the nonzero tiles of prolong_pattern are one run of 1 to 3 consecutive coarse tiles that holds tile a * 16 // 48 (cut at the ends of the range), and the tile (a * 16 // 48 + 16 // 2) mod 16. In each fine tile row a, the nonzero tiles of applied_pattern are one run of 3 to 5 consecutive coarse tiles that holds tile a * 16 // 48 (cut at the ends of the range), and the tile (a * 16 // 48 + 16 // 2) mod 16.
All inputs are finite; a program needn't handle non-finite values.
Results may differ from a plain program's by a relative error of at most 0.0003.
Values may be sent and summed in bfloat16 or wider, within the bound.
No kernel may reach another device: no remote copies, remote signals or barrier semaphores. Data moves between devices by JAX's collectives and lax.ppermute only.
A program may use at most 64 MiB of HBM per device.

v0:
```python
import jax
import jax.numpy as jnp
from jax import lax
from jax.sharding import PartitionSpec as P


def from_root(value, axis, source):
    kept = jnp.where(lax.axis_index(axis) == source, value, 0).astype(value.dtype)
    return lax.psum(kept, axis)


def apply_pattern(matrix, pattern):
    height, width = matrix.shape
    tile_rows, tile_cols = pattern.shape
    weights = pattern.astype(matrix.dtype)
    shaped = matrix.reshape(tile_rows, height // tile_rows, tile_cols, width // tile_cols)
    return (shaped * weights[:, None, :, None]).reshape(height, width)


def accumulate(running, r_piece, ap_piece):
    return running + lax.dot_general(
        r_piece, ap_piece, (((0,), (0,)), ((), ())), preferred_element_type=jnp.float32
    )


def on_device(prolong, applied, prolong_pattern, applied_pattern):
    masked_p = apply_pattern(prolong, prolong_pattern)
    masked_ap = apply_pattern(applied, applied_pattern)
    col_count = lax.axis_size("col")
    col_ratio = col_count // lax.axis_size("row")
    section_rows = masked_p.shape[0]
    initial = jnp.zeros((masked_p.shape[1], masked_ap.shape[1]), jnp.float32)

    def run_section(section_index, running):
        r_piece = from_root(masked_p, "col", section_index)
        ap_slice = lax.dynamic_slice_in_dim(
            masked_ap, section_index % col_ratio * section_rows, section_rows, 0
        )
        ap_piece = from_root(ap_slice, "row", section_index // col_ratio)
        return accumulate(running, r_piece, ap_piece)

    coarse_operator = lax.fori_loop(0, col_count, run_section, initial)
    return coarse_operator


def solution(mesh):
    in_specs = (P("col", "row"), P("row", "col"), P("col", "row"), P("row", "col"))
    out_specs = P("row", "col")
    return jax.shard_map(
        on_device, mesh=mesh, in_specs=in_specs, out_specs=out_specs, check_vma=False
    )
```

profile of v0, /device:TPU:0, one launch (start us, length us, event | category | flops | bytes accessed | tf_op | source)
XLA Modules:
  0.0 939.3 jit_solution(2318507751109120620)
XLA Ops:
  9.7 922.3 %while.16 = (s32[]{:T(128)}, f32[512,256]{1,0:T(8,128)S(1)}, bf16[768,512]{1,0:T(8,128)(2,1)S(1)}, bf16[1536,256]{1,0:T(8,128)(2,1)S(1)}, s32[]{:T(128)}, /*inde...) while((s32[]{:T(128)}, f32[512,256]{1,0:T(8,128)S(1)}, ...), condition=%wide.region_3.4_spmd.clone, body=%wide.region_0.3_spmd.clone.sunk | while | flops 202768416 | bytes 11665860 | solution.py:42
  11.6 36.7 %all-reduce.5.cloned.1.call-done = bf16[768,256]{1,0:T(8,128)(2,1)} async-done(((bf16[768,256]{1,0:T(8,128)(2,1)}), bf16[768,256]{1,0:T(8,128)(2,1)}) %all-reduce.5.cloned.1.call-update) | async-done | bytes 393232 | tf_op jit(solution)/shard_map/while/body/eval_jaxpr/psum | solution.py:9
  48.3 78.2 %all-reduce.3.cloned.1.call-done = bf16[768,512]{1,0:T(8,128)(2,1)} async-done(((bf16[768,512]{1,0:T(8,128)(2,1)}), bf16[768,512]{1,0:T(8,128)(2,1)}) %all-reduce.3.cloned.1.call-update) | async-done | bytes 786448 | tf_op jit(solution)/shard_map/while/body/eval_jaxpr/psum | solution.py:9
  126.5 1.7 convolution_add_fusion.2
  130.2 33.1 %all-reduce.5.cloned.1.call-done = bf16[768,256]{1,0:T(8,128)(2,1)} async-done(((bf16[768,256]{1,0:T(8,128)(2,1)}), bf16[768,256]{1,0:T(8,128)(2,1)}) %all-reduce.5.cloned.1.call-update) | async-done | bytes 393232 | tf_op jit(solution)/shard_map/while/body/eval_jaxpr/psum | solution.py:9
  163.3 78.0 %all-reduce.3.cloned.1.call-done = bf16[768,512]{1,0:T(8,128)(2,1)} async-done(((bf16[768,512]{1,0:T(8,128)(2,1)}), bf16[768,512]{1,0:T(8,128)(2,1)}) %all-reduce.3.cloned.1.call-update) | async-done | bytes 786448 | tf_op jit(solution)/shard_map/while/body/eval_jaxpr/psum | solution.py:9
  245.1 32.8 %all-reduce.5.cloned.1.call-done = bf16[768,256]{1,0:T(8,128)(2,1)} async-done(((bf16[768,256]{1,0:T(8,128)(2,1)}), bf16[768,256]{1,0:T(8,128)(2,1)}) %all-reduce.5.cloned.1.call-update) | async-done | bytes 393232 | tf_op jit(solution)/shard_map/while/body/eval_jaxpr/psum | solution.py:9
  277.9 78.0 %all-reduce.3.cloned.1.call-done = bf16[768,512]{1,0:T(8,128)(2,1)} async-done(((bf16[768,512]{1,0:T(8,128)(2,1)}), bf16[768,512]{1,0:T(8,128)(2,1)}) %all-reduce.3.cloned.1.call-update) | async-done | bytes 786448 | tf_op jit(solution)/shard_map/while/body/eval_jaxpr/psum | solution.py:9
  355.9 1.7 convolution_add_fusion.2
  359.7 33.1 %all-reduce.5.cloned.1.call-done = bf16[768,256]{1,0:T(8,128)(2,1)} async-done(((bf16[768,256]{1,0:T(8,128)(2,1)}), bf16[768,256]{1,0:T(8,128)(2,1)}) %all-reduce.5.cloned.1.call-update) | async-done | bytes 393232 | tf_op jit(solution)/shard_map/while/body/eval_jaxpr/psum | solution.py:9
  392.8 78.2 %all-reduce.3.cloned.1.call-done = bf16[768,512]{1,0:T(8,128)(2,1)} async-done(((bf16[768,512]{1,0:T(8,128)(2,1)}), bf16[768,512]{1,0:T(8,128)(2,1)}) %all-reduce.3.cloned.1.call-update) | async-done | bytes 786448 | tf_op jit(solution)/shard_map/while/body/eval_jaxpr/psum | solution.py:9
  471.0 1.7 convolution_add_fusion.2
  474.7 33.1 %all-reduce.5.cloned.1.call-done = bf16[768,256]{1,0:T(8,128)(2,1)} async-done(((bf16[768,256]{1,0:T(8,128)(2,1)}), bf16[768,256]{1,0:T(8,128)(2,1)}) %all-reduce.5.cloned.1.call-update) | async-done | bytes 393232 | tf_op jit(solution)/shard_map/while/body/eval_jaxpr/psum | solution.py:9
  507.8 78.0 %all-reduce.3.cloned.1.call-done = bf16[768,512]{1,0:T(8,128)(2,1)} async-done(((bf16[768,512]{1,0:T(8,128)(2,1)}), bf16[768,512]{1,0:T(8,128)(2,1)}) %all-reduce.3.cloned.1.call-update) | async-done | bytes 786448 | tf_op jit(solution)/shard_map/while/body/eval_jaxpr/psum | solution.py:9
  585.8 1.7 convolution_add_fusion.2
  589.5 33.1 %all-reduce.5.cloned.1.call-done = bf16[768,256]{1,0:T(8,128)(2,1)} async-done(((bf16[768,256]{1,0:T(8,128)(2,1)}), bf16[768,256]{1,0:T(8,128)(2,1)}) %all-reduce.5.cloned.1.call-update) | async-done | bytes 393232 | tf_op jit(solution)/shard_map/while/body/eval_jaxpr/psum | solution.py:9
  622.7 78.0 %all-reduce.3.cloned.1.call-done = bf16[768,512]{1,0:T(8,128)(2,1)} async-done(((bf16[768,512]{1,0:T(8,128)(2,1)}), bf16[768,512]{1,0:T(8,128)(2,1)}) %all-reduce.3.cloned.1.call-update) | async-done | bytes 786448 | tf_op jit(solution)/shard_map/while/body/eval_jaxpr/psum | solution.py:9
  700.7 1.7 convolution_add_fusion.2
  704.4 33.1 %all-reduce.5.cloned.1.call-done = bf16[768,256]{1,0:T(8,128)(2,1)} async-done(((bf16[768,256]{1,0:T(8,128)(2,1)}), bf16[768,256]{1,0:T(8,128)(2,1)}) %all-reduce.5.cloned.1.call-update) | async-done | bytes 393232 | tf_op jit(solution)/shard_map/while/body/eval_jaxpr/psum | solution.py:9
  737.6 78.0 %all-reduce.3.cloned.1.call-done = bf16[768,512]{1,0:T(8,128)(2,1)} async-done(((bf16[768,512]{1,0:T(8,128)(2,1)}), bf16[768,512]{1,0:T(8,128)(2,1)}) %all-reduce.3.cloned.1.call-update) | async-done | bytes 786448 | tf_op jit(solution)/shard_map/while/body/eval_jaxpr/psum | solution.py:9
  815.6 1.7 convolution_add_fusion.2
  819.3 32.8 %all-reduce.5.cloned.1.call-done = bf16[768,256]{1,0:T(8,128)(2,1)} async-done(((bf16[768,256]{1,0:T(8,128)(2,1)}), bf16[768,256]{1,0:T(8,128)(2,1)}) %all-reduce.5.cloned.1.call-update) | async-done | bytes 393232 | tf_op jit(solution)/shard_map/while/body/eval_jaxpr/psum | solution.py:9
  852.1 78.0 %all-reduce.3.cloned.1.call-done = bf16[768,512]{1,0:T(8,128)(2,1)} async-done(((bf16[768,512]{1,0:T(8,128)(2,1)}), bf16[768,512]{1,0:T(8,128)(2,1)}) %all-reduce.3.cloned.1.call-update) | async-done | bytes 786448 | tf_op jit(solution)/shard_map/while/body/eval_jaxpr/psum | solution.py:9
  930.2 1.7 convolution_add_fusion.2
  (66 shorter events, 20.7 us)
Async XLA Ops:
  6.5 1.2 copy-start.1
  7.7 0.7 copy-start.3
  8.4 1.1 copy-start.2
  9.7 38.7 %all-reduce.5.cloned.1.call-start = ((), (), s32[]{:S(2)}) async-start(), calls=%async_computation.1 | async-start | bytes 786432 | tf_op jit(solution)/shard_map/while/body/eval_jaxpr/psum | solution.py:9
  10.6 115.9 %all-reduce.3.cloned.1.call-start = ((), (), s32[]{:S(2)}) async-start(), calls=%async_computation | async-start | bytes 1572864 | tf_op jit(solution)/shard_map/while/body/eval_jaxpr/psum | solution.py:9
  128.3 35.1 %all-reduce.5.cloned.1.call-start = ((), (), s32[]{:S(2)}) async-start(), calls=%async_computation.1 | async-start | bytes 786432 | tf_op jit(solution)/shard_map/while/body/eval_jaxpr/psum | solution.py:9
  129.2 112.2 %all-reduce.3.cloned.1.call-start = ((), (), s32[]{:S(2)}) async-start(), calls=%async_computation | async-start | bytes 1572864 | tf_op jit(solution)/shard_map/while/body/eval_jaxpr/psum | solution.py:9
  243.1 34.8 %all-reduce.5.cloned.1.call-start = ((), (), s32[]{:S(2)}) async-start(), calls=%async_computation.1 | async-start | bytes 786432 | tf_op jit(solution)/shard_map/while/body/eval_jaxpr/psum | solution.py:9
  244.0 111.9 %all-reduce.3.cloned.1.call-start = ((), (), s32[]{:S(2)}) async-start(), calls=%async_computation | async-start | bytes 1572864 | tf_op jit(solution)/shard_map/while/body/eval_jaxpr/psum | solution.py:9
  357.7 35.1 %all-reduce.5.cloned.1.call-start = ((), (), s32[]{:S(2)}) async-start(), calls=%async_computation.1 | async-start | bytes 786432 | tf_op jit(solution)/shard_map/while/body/eval_jaxpr/psum | solution.py:9
  358.6 112.3 %all-reduce.3.cloned.1.call-start = ((), (), s32[]{:S(2)}) async-start(), calls=%async_computation | async-start | bytes 1572864 | tf_op jit(solution)/shard_map/while/body/eval_jaxpr/psum | solution.py:9
  472.7 35.1 %all-reduce.5.cloned.1.call-start = ((), (), s32[]{:S(2)}) async-start(), calls=%async_computation.1 | async-start | bytes 786432 | tf_op jit(solution)/shard_map/while/body/eval_jaxpr/psum | solution.py:9
  473.6 112.2 %all-reduce.3.cloned.1.call-start = ((), (), s32[]{:S(2)}) async-start(), calls=%async_computation | async-start | bytes 1572864 | tf_op jit(solution)/shard_map/while/body/eval_jaxpr/psum | solution.py:9
  587.6 35.1 %all-reduce.5.cloned.1.call-start = ((), (), s32[]{:S(2)}) async-start(), calls=%async_computation.1 | async-start | bytes 786432 | tf_op jit(solution)/shard_map/while/body/eval_jaxpr/psum | solution.py:9
  588.5 112.2 %all-reduce.3.cloned.1.call-start = ((), (), s32[]{:S(2)}) async-start(), calls=%async_computation | async-start | bytes 1572864 | tf_op jit(solution)/shard_map/while/body/eval_jaxpr/psum | solution.py:9
  702.5 35.1 %all-reduce.5.cloned.1.call-start = ((), (), s32[]{:S(2)}) async-start(), calls=%async_computation.1 | async-start | bytes 786432 | tf_op jit(solution)/shard_map/while/body/eval_jaxpr/psum | solution.py:9
  703.4 112.2 %all-reduce.3.cloned.1.call-start = ((), (), s32[]{:S(2)}) async-start(), calls=%async_computation | async-start | bytes 1572864 | tf_op jit(solution)/shard_map/while/body/eval_jaxpr/psum | solution.py:9
  817.4 34.8 %all-reduce.5.cloned.1.call-start = ((), (), s32[]{:S(2)}) async-start(), calls=%async_computation.1 | async-start | bytes 786432 | tf_op jit(solution)/shard_map/while/body/eval_jaxpr/psum | solution.py:9
  818.3 111.9 %all-reduce.3.cloned.1.call-start = ((), (), s32[]{:S(2)}) async-start(), calls=%async_computation | async-start | bytes 1572864 | tf_op jit(solution)/shard_map/while/body/eval_jaxpr/psum | solution.py:9
  931.9 0.8 copy-start
Sparse Core Ops, SparseCore 0:
  13.0 35.2 all-reduce.4
  51.7 74.7 all-reduce.2
  131.6 31.7 all-reduce.4
  166.6 74.7 all-reduce.2
  246.1 31.7 all-reduce.4
  281.2 74.7 all-reduce.2
  361.0 31.7 all-reduce.4
  396.2 74.7 all-reduce.2
  476.0 31.7 all-reduce.4
  511.1 74.7 all-reduce.2
  590.9 31.7 all-reduce.4
  626.0 74.7 all-reduce.2
  705.8 31.7 all-reduce.4
  740.8 74.7 all-reduce.2
  820.4 31.7 all-reduce.4
  855.4 74.7 all-reduce.2
where the time goes:
time: 940 us; the launch traced here: 939 us
  waiting for transfers between devices  893 us (95%)
  other arithmetic  15.2 us (2%)
  matrix products  13.9 us (1%)
  between operations  13.1 us (1%)
    psum x16, waiting for transfers between devices, from_root(): return lax.psum(kept, axis)  893 us
  transfers between devices with their start and end apart: 16, of which 16 were waited for; matrix products, arithmetic and copies ran while one was open for 1% of the time, Pallas kernels for 0%

commit v1 on v0

v1 whole, which is shorter than its diff:
```python
import functools

import jax
import jax.numpy as jnp
from jax import lax
from jax.experimental import pallas as pl
from jax.experimental.pallas import tpu as pltpu
from jax.sharding import PartitionSpec as P

TILE = 128
AXES = ("row", "col")
OWN, SIDE, IN, OUT, FAR, DIAG_IN, DIAG_OUT = range(7)


def inward(source, cols):
    return source + 2 if source < cols // 2 else source - 2


def outward(source, cols):
    target = source - 2 if source < cols // 2 else source + 2
    return target if 0 <= target < cols else None


def diagonal(source, cols):
    target = source - 1 if source % 2 == 0 else source + 1
    return target if 0 <= target < cols else None


def routes(sources, cols):
    pairs = {kind: [] for kind in (SIDE, IN, OUT, FAR, DIAG_IN, DIAG_OUT)}
    for s in sources:
        pairs[SIDE].append((s, s ^ 1))
        a, b, d = inward(s, cols), outward(s, cols), diagonal(s, cols)
        pairs[IN].append((s, a))
        pairs[FAR].append((a, (s + cols // 2) % cols))
        if b is not None:
            pairs[OUT].append((s, b))
        if d is not None:
            relay = s - 2 if s % 2 == 0 else s + 2
            pairs[DIAG_IN if relay == a else DIAG_OUT].append((relay, d))
    return pairs


def main_sources(r, cols):
    return [2 * r, 2 * r + 1]


def small_sources(r, cols):
    near = [s for s in (2 * r - 1, 2 * r + 2) if 0 <= s < cols]
    return near + [(2 * r + cols // 2) % cols, (2 * r + 1 + cols // 2) % cols]


def all_pairs(sources_of, rows, cols):
    total = {}
    for r in range(rows):
        for kind, pairs in routes(sources_of(r, cols), cols).items():
            assert len({d for _, d in pairs}) == len(pairs)
            assert len({s for s, _ in pairs}) == len(pairs)
            total.setdefault(kind, []).extend((r * cols + s, r * cols + d) for s, d in pairs)
    return total


def spread(block, pairs):
    move = lambda x, kind: lax.ppermute(x, AXES, pairs[kind])
    got = {OWN: block}
    got[IN] = move(block, IN)
    got[SIDE] = move(block, SIDE)
    got[OUT] = move(block, OUT)
    got[FAR] = move(got[IN], FAR)
    got[DIAG_IN] = move(got[IN], DIAG_IN)
    got[DIAG_OUT] = move(got[OUT], DIAG_OUT)
    return [got[kind] for kind in range(7)]


def arrival(source, c, cols):
    diff = c - source
    low = source < cols // 2
    even = source % 2 == 0
    side = jnp.where(even, 1, -1)
    is_in = diff == jnp.where(low, 2, -2)
    is_out = diff == jnp.where(low, -2, 2)
    diag_kind = jnp.where(even == low, DIAG_OUT, DIAG_IN)
    kind = jnp.where(diff == 0, OWN, -1)
    kind = jnp.where(diff == side, SIDE, kind)
    kind = jnp.where(diff == -side, diag_kind, kind)
    kind = jnp.where((diff == cols // 2) | (diff == -(cols // 2)), FAR, kind)
    kind = jnp.where(is_out, OUT, kind)
    kind = jnp.where(is_in, IN, kind)
    return kind


def prepare_kernel(cols, p_ref, ap_ref, pp_ref, app_ref, pm_ref, apm_ref, small_ref):
    r, c = lax.axis_index("row"), lax.axis_index("col")
    fine = p_ref.shape[0] // TILE
    for a in range(fine):
        for b in range(p_ref.shape[1] // TILE):
            at = (pl.ds(a * TILE, TILE), pl.ds(b * TILE, TILE))
            pm_ref[at] = jnp.where(pp_ref[a, b] > 0, p_ref[at], jnp.zeros((TILE, TILE), p_ref.dtype))
    for a in range(ap_ref.shape[0] // TILE):
        for b in range(ap_ref.shape[1] // TILE):
            at = (pl.ds(a * TILE, TILE), pl.ds(b * TILE, TILE))
            apm_ref[at] = jnp.where(app_ref[a, b] > 0, ap_ref[at], jnp.zeros((TILE, TILE), ap_ref.dtype))
    half = p_ref.shape[0] // 2

    def pack(units):
        for u, (m, i) in enumerate(units):
            small_ref[pl.ds(u * half, half), :] = pm_ref[pl.ds(m * half, half), pl.ds(i * TILE, TILE)]

    @pl.when(c == 2 * r - 1)
    def _():
        pack(BEFORE)

    @pl.when(c == 2 * r + 2)
    def _():
        pack(AFTER)

    @pl.when(c == lax.rem(2 * r + cols // 2, cols))
    def _():
        pack(FAR_FIRST)

    @pl.when(c == lax.rem(2 * r + 1 + cols // 2, cols))
    def _():
        pack(FAR_SECOND)


BEFORE = ((0, 0), (1, 0), (1, 1))
AFTER = ((0, 2), (0, 3), (1, 3))
FAR_FIRST = ((0, 0), (1, 1))
FAR_SECOND = ((0, 2), (1, 3))


def product(p, ap):
    return lax.dot_general(p, ap, (((0,), (0,)), ((), ())), preferred_element_type=jnp.float32)


def combine_kernel(cols, own_ap, far_ap, core_ap, cross_ap, *refs):
    mains, smalls, c_ref = refs[:7], refs[7:14], refs[14]
    main_scratch, small_scratch = refs[15], refs[16]
    r, c = lax.axis_index("row"), lax.axis_index("col")
    depth = mains[0].shape[0]
    half = depth // 2
    odd = r % 2 == 1
    c_ref[...] = jnp.zeros_like(c_ref)

    def fetch(kind, buffers, scratch):
        for k in range(7):
            @pl.when(kind == k)
            def _(k=k):
                scratch[...] = buffers[k][...]

    for e in range(2):
        kind = arrival(2 * r + e, c, cols)

        @pl.when(kind >= 0)
        def _(kind=kind, e=e):
            fetch(kind, mains, main_scratch)
            c_ref[...] += product(main_scratch[...], own_ap[pl.ds(e * depth, depth), :])

    def small(source, valid, units, ap_rows):
        kind = arrival(source, c, cols)

        @pl.when(valid & (kind >= 0))
        def _():
            fetch(kind, smalls, small_scratch)
            for u, (m, i) in enumerate(units):
                rows = pl.ds(i * TILE, TILE)
                c_ref[rows, :] += product(small_scratch[pl.ds(u * half, half), :], ap_rows(m))

    within = lambda ref, start: (lambda m: ref[pl.ds(start + m * half, half), :])
    small(lax.rem(2 * r + cols // 2, cols), True, FAR_FIRST, within(far_ap, 0))
    small(lax.rem(2 * r + 1 + cols // 2, cols), True, FAR_SECOND, within(far_ap, depth))
    small(2 * r - 1, odd, BEFORE, within(core_ap, 0))
    small(2 * r - 1, (r > 0) & ~odd, BEFORE, within(cross_ap, 0))
    small(2 * r + 2, ~odd, AFTER, within(core_ap, 0))
    small(2 * r + 2, (2 * r + 2 < cols) & odd, AFTER, within(cross_ap, 0))


def on_device(rows, cols, prolong, applied, prolong_pattern, applied_pattern):
    depth = prolong.shape[0]
    half = depth // 2
    vmem = pl.BlockSpec(memory_space=pltpu.VMEM)
    smem = pl.BlockSpec(memory_space=pltpu.SMEM)
    shape = lambda h, w: jax.ShapeDtypeStruct((h, w), prolong.dtype)
    masked_p, masked_ap, small = pl.pallas_call(
        functools.partial(prepare_kernel, cols),
        out_shape=(shape(*prolong.shape), shape(*applied.shape), shape(3 * half, TILE)),
        in_specs=[vmem, vmem, smem, smem],
        out_specs=(vmem, vmem, vmem),
        compiler_params=pltpu.CompilerParams(vmem_limit_bytes=16 << 20),
    )(prolong, applied, prolong_pattern, applied_pattern)

    device = lambda r, c: r * cols + c
    across = [(device(r, c), device((r + rows // 2) % rows, c)) for r in range(rows) for c in range(cols)]
    partner = [(device(r, c), device(r ^ 1, c)) for r in range(rows) for c in range(cols)]
    beyond = [
        (device(r, c), device(t, c))
        for r in range(rows)
        for t in [r + 1 if r % 2 == 1 else r - 1]
        if 0 <= t < rows
        for c in range(cols)
    ]
    odd = lax.axis_index("row") % 2 == 1
    lower, upper = masked_ap[:depth], masked_ap[depth:]
    far_ap = lax.ppermute(masked_ap, AXES, across)
    mains = spread(masked_p, all_pairs(main_sources, rows, cols))
    core_ap = lax.ppermute(jnp.where(odd, lower, upper), AXES, partner)
    cross_ap = lax.ppermute(jnp.where(odd, upper, lower), AXES, beyond)
    smalls = spread(small, all_pairs(small_sources, rows, cols))

    return pl.pallas_call(
        functools.partial(combine_kernel, cols),
        out_shape=jax.ShapeDtypeStruct((prolong.shape[1], applied.shape[1]), jnp.float32),
        in_specs=[vmem] * 18,
        out_specs=vmem,
        scratch_shapes=[pltpu.VMEM(prolong.shape, prolong.dtype), pltpu.VMEM((3 * half, TILE), prolong.dtype)],
        compiler_params=pltpu.CompilerParams(vmem_limit_bytes=32 << 20),
    )(masked_ap, far_ap, core_ap, cross_ap, *mains, *smalls)


def solution(mesh):
    in_specs = (P("col", "row"), P("row", "col"), P("col", "row"), P("row", "col"))
    return jax.shard_map(
        functools.partial(on_device, mesh.shape["row"], mesh.shape["col"]),
        mesh=mesh, in_specs=in_specs, out_specs=P("row", "col"), check_vma=False,
    )
```

time: 940 us -> 58.3 us (0.06)
  the two profiles are of different devices: /device:TPU:0 before, /device:TPU:23 now
where the time goes in v1:
time: 58.3 us; the launch traced here: 57.9 us
  waiting for transfers between devices  27.5 us (47%)
  starting transfers between devices  22.2 us (38%)
  Pallas kernels  4.78 us (8%)
  local copies, waits for them, and re-layouts  3.14 us (5%)
    ppermute x12, starting transfers between devices, spread(): move = lambda x, kind: lax.ppermute(x, AXES, pairs[kind])  18.9 us
    ppermute x12, waiting for transfers between devices, spread(): move = lambda x, kind: lax.ppermute(x, AXES, pairs[kind])  16.5 us
    ppermute x1, waiting for transfers between devices, on_device(): far_ap = lax.ppermute(masked_ap, AXES, across)  11 us
    pallas_call x1, Pallas kernels, on_device(): pl.pallas_call(functools.partial(combine_kernel, cols), out_shape=jax.Sha...  3.62 us
    unnamed x8, local copies, waits for them, and re-layouts  3.14 us
    ppermute x1, starting transfers between devices, on_device(): core_ap = lax.ppermute(jnp.where(odd, lower, upper), AXES, partner)  2.27 us
  transfers between devices with their start and end apart: 15, of which 5 were waited for; matrix products, arithmetic and copies ran while one was open for 0% of the time, Pallas kernels for 0%

profile of v1, /device:TPU:23, one launch (start us, length us, event | category | flops | bytes accessed | tf_op | source)
XLA Modules:
  0.0 57.9 jit_solution(17894224039595209259)
XLA Ops:
  0.0 0.8 %copy.5.pp_ref = s32[6,4]{1,0:T(8,128)S(1)} copy(s32[6,4]{0,1:T(4,128)} %param.6) | data formatting | bytes 192 | tf_op args[2]
  0.9 1.1 %copy-done = bf16[768,512]{1,0:T(8,128)(2,1)S(1)} copy-done((bf16[768,512]{1,0:T(8,128)(2,1)S(1)}, bf16[768,512]{1,0:T(8,128)(2,1)}, u32[]{:S(2)}) %copy-start) | copy-done | bytes 786456
  2.0 1.1 %copy-done.1 = bf16[1536,256]{1,0:T(8,128)(2,1)S(1)} copy-done((bf16[1536,256]{1,0:T(8,128)(2,1)S(1)}, bf16[1536,256]{1,0:T(8,128)(2,1)}, u32[]{:S(2)}) %copy-start.1) | copy-done | bytes 786456
  3.1 1.2 %shard_map.46 = (bf16[768,512]{1,0:T(8,128)(2,1)S(1)}, bf16[1536,256]{1,0:T(8,128)(2,1)S(1)}, bf16[1152,128]{1,0:T(8,128)(2,1)S(1)}) custom-call(bf16[768,512]{1,0:T(8,128)(2,1)S(1)} %copy-done, bf16[1536,256]{1,0:T(8,128)(2,1)S(1)} %copy-done.1, s32[6,4]{1,0:T(8,128)S(1)} %copy.5.pp_ref, s32[12,2]{1,0:T(8,128)S(1)} %copy.6.app_ref), custom_call_target="tpu_custom_call" | custom-call | tf_op jit(solution)/shard_map/pallas_call | solution.py:184
  4.3 3.9 %collective-permute-start.11 = (bf16[1152,128]{1,0:T(8,128)(2,1)S(1)}, bf16[1152,128]{1,0:T(8,128)(2,1)}, u32[]{:S(2)}, u32[]{:S(2)}) collective-permute-start(bf16[1152,128]{1,0:T(8,128)(2,1)S(1)} %get-tuple-element.10.refs_7_), channel_id=1, source_target_pairs={{2,0},{4,6},{5,7},{12,14},{19,17},{29,31},{26,24},{27,25}} | collective-permute-start | bytes 884744 | tf_op jit(solution)/shard_map/ppermute | solution.py:64
  8.2 1.9 %collective-permute-start.10 = (bf16[1152,128]{1,0:T(8,128)(2,1)S(1)}, bf16[1152,128]{1,0:T(8,128)(2,1)}, u32[]{:S(2)}, u32[]{:S(2)}) collective-permute-start(bf16[1152,128]{1,0:T(8,128)(2,1)S(1)} %get-tuple-element.10.refs_7_), channel_id=1, source_target_pairs={{2,4},{4,2},{5,3},{9,11},{12,10},{14,12},{15,13},{19,21},{22,20},{... | collective-permute-start | bytes 884744 | tf_op jit(solution)/shard_map/ppermute | solution.py:64
  10.1 0.7 %collective-permute-start.5 = (bf16[768,512]{1,0:T(8,128)(2,1)S(1)}, bf16[768,512]{1,0:T(8,128)(2,1)S(1)}, u32[]{:S(2)}, u32[]{:S(2)}) collective-permute-start(bf16[768,512]{1,0:T(8,128)(2,1)S(1)} %get-tuple-element.9.refs_0_), channel_id=1, source_target_pairs={{10,8},{11,9},{20,22},{21,23}} | collective-permute-start | bytes 2359304 | tf_op jit(solution)/shard_map/ppermute | solution.py:64
  10.8 1.3 %collective-permute-start.4 = (bf16[768,512]{1,0:T(8,128)(2,1)S(1)}, bf16[768,512]{1,0:T(8,128)(2,1)S(1)}, u32[]{:S(2)}, u32[]{:S(2)}) collective-permute-start(bf16[768,512]{1,0:T(8,128)(2,1)S(1)} %get-tuple-element.9.refs_0_), channel_id=1, source_target_pairs={{0,2},{1,3},{10,12},{11,13},{20,18},{21,19},{30,28},{31,29}} | collective-permute-start | bytes 2359304 | tf_op jit(solution)/shard_map/ppermute | solution.py:64
  12.2 0.7 %collective-permute-start.2 = (bf16[768,256]{1,0:T(8,128)(2,1)S(1)}, bf16[768,256]{1,0:T(8,128)(2,1)S(1)}, u32[]{:S(2)}, u32[]{:S(2)}) collective-permute-start(bf16[768,256]{1,0:T(8,128)(2,1)S(1)} %get-tuple-element.11), channel_id=1, source_target_pairs={{8,16},{9,17},{10,18},{11,19},{12,20},{13,21},{14,22},{15,23},{16,... | collective-permute-start | bytes 1179656 | tf_op jit(solution)/shard_map/ppermute | solution.py:207
  12.9 2.3 %collective-permute-start.1 = (bf16[768,256]{1,0:T(8,128)(2,1)S(1)}, bf16[768,256]{1,0:T(8,128)(2,1)S(1)}, u32[]{:S(2)}, u32[]{:S(2)}) collective-permute-start(bf16[768,256]{1,0:T(8,128)(2,1)S(1)} %get-tuple-element.12), channel_id=1, source_target_pairs={{0,8},{1,9},{2,10},{3,11},{4,12},{5,13},{6,14},{7,15},{8,0},{9,1},... | collective-permute-start | bytes 1179656 | tf_op jit(solution)/shard_map/ppermute | solution.py:206
  15.2 2.7 %collective-permute-done.10.refs_9_ = bf16[1152,128]{1,0:T(8,128)(2,1)} collective-permute-done((bf16[1152,128]{1,0:T(8,128)(2,1)S(1)}, bf16[1152,128]{1,0:T(8,128)(2,1)}, u32[]{:S(2)}, u32[]{:S(2)}) %collective-permute-start.10) | collective-permute-done | bytes 294944 | tf_op jit(solution)/shard_map/ppermute | solution.py:64
  17.9 1.3 %collective-permute-start.9 = (bf16[1152,128]{1,0:T(8,128)(2,1)S(1)}, bf16[1152,128]{1,0:T(8,128)(2,1)S(1)}, u32[]{:S(2)}, u32[]{:S(2)}) collective-permute-start(bf16[1152,128]{1,0:T(8,128)(2,1)S(1)} %get-tuple-element.10.refs_7_), channel_id=1, source_target_pairs={{2,3},{4,5},{5,4},{9,8},{12,13},{14,15},{15,14},{19,18},{22,23},{1... | collective-permute-start | bytes 884744 | tf_op jit(solution)/shard_map/ppermute | solution.py:64
  19.2 3.6 %collective-permute-done.9.refs_8_ = bf16[1152,128]{1,0:T(8,128)(2,1)S(1)} collective-permute-done((bf16[1152,128]{1,0:T(8,128)(2,1)S(1)}, bf16[1152,128]{1,0:T(8,128)(2,1)S(1)}, u32[]{:S(2)}, u32[]{:S(2)}) %collective-permute-start.9) | collective-permute-done | bytes 294944 | tf_op jit(solution)/shard_map/ppermute | solution.py:64
  22.8 0.7 %collective-permute-start.14 = (bf16[1152,128]{1,0:T(8,128)(2,1)}, bf16[1152,128]{1,0:T(8,128)(2,1)S(1)}, u32[]{:S(2)}, u32[]{:S(2)}) collective-permute-start(bf16[1152,128]{1,0:T(8,128)(2,1)} %collective-permute-done.11.refs_10_), channel_id=1, source_target_pairs={{0,1},{7,6},{31,30},{24,25}} | collective-permute-start | bytes 884744 | tf_op jit(solution)/shard_map/ppermute | solution.py:64
  23.5 3.8 %collective-permute-start.13 = (bf16[1152,128]{1,0:T(8,128)(2,1)}, bf16[1152,128]{1,0:T(8,128)(2,1)S(1)}, u32[]{:S(2)}, u32[]{:S(2)}) collective-permute-start(bf16[1152,128]{1,0:T(8,128)(2,1)} %collective-permute-done.10.refs_9_), channel_id=1, source_target_pairs={{2,3},{11,10},{10,11},{12,13},{21,20},{20,21},{19,18},{29,28}} | collective-permute-start | bytes 884744 | tf_op jit(solution)/shard_map/ppermute | solution.py:64
  27.3 1.3 %collective-permute-start.12 = (bf16[1152,128]{1,0:T(8,128)(2,1)}, bf16[1152,128]{1,0:T(8,128)(2,1)S(1)}, u32[]{:S(2)}, u32[]{:S(2)}) collective-permute-start(bf16[1152,128]{1,0:T(8,128)(2,1)} %collective-permute-done.10.refs_9_), channel_id=1, source_target_pairs={{4,6},{2,0},{3,1},{11,13},{10,8},{12,10},{13,11},{21,23},{20,18},{... | collective-permute-start | bytes 884744 | tf_op jit(solution)/shard_map/ppermute | solution.py:64
  29.0 4.1 %collective-permute-done.13.refs_12_ = bf16[1152,128]{1,0:T(8,128)(2,1)S(1)} collective-permute-done((bf16[1152,128]{1,0:T(8,128)(2,1)}, bf16[1152,128]{1,0:T(8,128)(2,1)S(1)}, u32[]{:S(2)}, u32[]{:S(2)}) %collective-permute-start.13) | collective-permute-done | bytes 294944 | tf_op jit(solution)/shard_map/ppermute | solution.py:64
  33.2 0.7 %collective-permute-start.3 = (bf16[768,512]{1,0:T(8,128)(2,1)S(1)}, bf16[768,512]{1,0:T(8,128)(2,1)S(1)}, u32[]{:S(2)}, u32[]{:S(2)}) collective-permute-start(bf16[768,512]{1,0:T(8,128)(2,1)S(1)} %get-tuple-element.9.refs_0_), channel_id=1, source_target_pairs={{0,1},{1,0},{10,11},{11,10},{20,21},{21,20},{30,31},{31,30}} | collective-permute-start | bytes 2359304 | tf_op jit(solution)/shard_map/ppermute | solution.py:64
  33.9 0.7 %collective-permute-start.8 = (bf16[768,512]{1,0:T(8,128)(2,1)S(1)}, bf16[768,512]{1,0:T(8,128)(2,1)S(1)}, u32[]{:S(2)}, u32[]{:S(2)}) collective-permute-start(bf16[768,512]{1,0:T(8,128)(2,1)S(1)} %collective-permute-done.5.refs_3_), channel_id=1, source_target_pairs={{8,9},{23,22}} | collective-permute-start | bytes 2359304 | tf_op jit(solution)/shard_map/ppermute | solution.py:64
  34.6 1.3 %collective-permute-start.7 = (bf16[768,512]{1,0:T(8,128)(2,1)S(1)}, bf16[768,512]{1,0:T(8,128)(2,1)S(1)}, u32[]{:S(2)}, u32[]{:S(2)}) collective-permute-start(bf16[768,512]{1,0:T(8,128)(2,1)S(1)} %collective-permute-done.4.refs_2_), channel_id=1, source_target_pairs={{3,2},{13,12},{18,19},{28,29}} | collective-permute-start | bytes 2359304 | tf_op jit(solution)/shard_map/ppermute | solution.py:64
  35.9 1.3 %collective-permute-start.6 = (bf16[768,512]{1,0:T(8,128)(2,1)S(1)}, bf16[768,512]{1,0:T(8,128)(2,1)S(1)}, u32[]{:S(2)}, u32[]{:S(2)}) collective-permute-start(bf16[768,512]{1,0:T(8,128)(2,1)S(1)} %collective-permute-done.4.refs_2_), channel_id=1, source_target_pairs={{2,4},{3,5},{12,14},{13,15},{18,16},{19,17},{28,26},{29,27}} | collective-permute-start | bytes 2359304 | tf_op jit(solution)/shard_map/ppermute | solution.py:64
  37.3 11.0 %collective-permute-done.far_ap = bf16[1536,256]{1,0:T(8,128)(2,1)S(1)} collective-permute-done((bf16[1536,256]{1,0:T(8,128)(2,1)S(1)}, bf16[1536,256]{1,0:T(8,128)(2,1)S(1)}, u32[]{:S(2)}, u32[]{:S(2)}) %collective-permute-start) | collective-permute-done | bytes 786464 | tf_op jit(solution)/shard_map/ppermute | solution.py:204
  48.3 6.0 %collective-permute-done.7.refs_5_ = bf16[768,512]{1,0:T(8,128)(2,1)S(1)} collective-permute-done((bf16[768,512]{1,0:T(8,128)(2,1)S(1)}, bf16[768,512]{1,0:T(8,128)(2,1)S(1)}, u32[]{:S(2)}, u32[]{:S(2)}) %collective-permute-start.7) | collective-permute-done | bytes 786464 | tf_op jit(solution)/shard_map/ppermute | solution.py:64
  54.3 3.6 %shard_map.47 = f32[512,256]{1,0:T(8,128)} custom-call(bf16[1536,256]{1,0:T(8,128)(2,1)S(1)} %get-tuple-element.8.own_ap, bf16[1536,256]{1,0:T(8,128)(2,1)S(1)} %collective-permute-done.far_ap, bf16[768,256]{1,0:T(8,128)(2,1)S(1)} %collective-permute-done.1.core_ap, bf16[768,256]{1,0:T(8,128)(2,1)S(1)} %collective-permute-done.2.cross_ap, ...), custom_call_target="tpu_custom_call" | custom-call | tf_op jit(solution)/shard_map/pallas_call | solution.py:210
  (17 shorter events, 0.6 us)
Async XLA Ops:
  0.0 0.8 %copy-start.2 = (s32[12,2]{0,1:T(2,128)S(1)}, s32[12,2]{0,1:T(2,128)}, u32[]{:S(2)}) copy-start(s32[12,2]{0,1:T(2,128)} %param.7) | copy-start | bytes 292
  0.9 1.1 %copy-start = (bf16[768,512]{1,0:T(8,128)(2,1)S(1)}, bf16[768,512]{1,0:T(8,128)(2,1)}, u32[]{:S(2)}) copy-start(bf16[768,512]{1,0:T(8,128)(2,1)} %p_ref.1) | copy-start | bytes 2359300
  2.0 1.1 %copy-start.1 = (bf16[1536,256]{1,0:T(8,128)(2,1)S(1)}, bf16[1536,256]{1,0:T(8,128)(2,1)}, u32[]{:S(2)}) copy-start(bf16[1536,256]{1,0:T(8,128)(2,1)} %ap_ref.1) | copy-start | bytes 2359300
  4.3 8.6 %collective-permute-start.11 = (bf16[1152,128]{1,0:T(8,128)(2,1)S(1)}, bf16[1152,128]{1,0:T(8,128)(2,1)}, u32[]{:S(2)}, u32[]{:S(2)}) collective-permute-start(bf16[1152,128]{1,0:T(8,128)(2,1)S(1)} %get-tuple-element.10.refs_7_), channel_id=1, source_target_pairs={{2,0},{4,6},{5,7},{12,14},{19,17},{29,31},{26,24},{27,25}} | collective-permute-start | bytes 884744 | tf_op jit(solution)/shard_map/ppermute | solution.py:64
  8.2 9.7 %collective-permute-start.10 = (bf16[1152,128]{1,0:T(8,128)(2,1)S(1)}, bf16[1152,128]{1,0:T(8,128)(2,1)}, u32[]{:S(2)}, u32[]{:S(2)}) collective-permute-start(bf16[1152,128]{1,0:T(8,128)(2,1)S(1)} %get-tuple-element.10.refs_7_), channel_id=1, source_target_pairs={{2,4},{4,2},{5,3},{9,11},{12,10},{14,12},{15,13},{19,21},{22,20},{... | collective-permute-start | bytes 884744 | tf_op jit(solution)/shard_map/ppermute | solution.py:64
  10.1 23.8 %collective-permute-start.5 = (bf16[768,512]{1,0:T(8,128)(2,1)S(1)}, bf16[768,512]{1,0:T(8,128)(2,1)S(1)}, u32[]{:S(2)}, u32[]{:S(2)}) collective-permute-start(bf16[768,512]{1,0:T(8,128)(2,1)S(1)} %get-tuple-element.9.refs_0_), channel_id=1, source_target_pairs={{10,8},{11,9},{20,22},{21,23}} | collective-permute-start | bytes 2359304 | tf_op jit(solution)/shard_map/ppermute | solution.py:64
  10.8 23.8 %collective-permute-start.4 = (bf16[768,512]{1,0:T(8,128)(2,1)S(1)}, bf16[768,512]{1,0:T(8,128)(2,1)S(1)}, u32[]{:S(2)}, u32[]{:S(2)}) collective-permute-start(bf16[768,512]{1,0:T(8,128)(2,1)S(1)} %get-tuple-element.9.refs_0_), channel_id=1, source_target_pairs={{0,2},{1,3},{10,12},{11,13},{20,18},{21,19},{30,28},{31,29}} | collective-permute-start | bytes 2359304 | tf_op jit(solution)/shard_map/ppermute | solution.py:64
  12.2 11.3 %collective-permute-start.2 = (bf16[768,256]{1,0:T(8,128)(2,1)S(1)}, bf16[768,256]{1,0:T(8,128)(2,1)S(1)}, u32[]{:S(2)}, u32[]{:S(2)}) collective-permute-start(bf16[768,256]{1,0:T(8,128)(2,1)S(1)} %get-tuple-element.11), channel_id=1, source_target_pairs={{8,16},{9,17},{10,18},{11,19},{12,20},{13,21},{14,22},{15,23},{16,... | collective-permute-start | bytes 1179656 | tf_op jit(solution)/shard_map/ppermute | solution.py:207
  12.9 14.4 %collective-permute-start.1 = (bf16[768,256]{1,0:T(8,128)(2,1)S(1)}, bf16[768,256]{1,0:T(8,128)(2,1)S(1)}, u32[]{:S(2)}, u32[]{:S(2)}) collective-permute-start(bf16[768,256]{1,0:T(8,128)(2,1)S(1)} %get-tuple-element.12), channel_id=1, source_target_pairs={{0,8},{1,9},{2,10},{3,11},{4,12},{5,13},{6,14},{7,15},{8,0},{9,1},... | collective-permute-start | bytes 1179656 | tf_op jit(solution)/shard_map/ppermute | solution.py:206
  17.9 4.9 %collective-permute-start.9 = (bf16[1152,128]{1,0:T(8,128)(2,1)S(1)}, bf16[1152,128]{1,0:T(8,128)(2,1)S(1)}, u32[]{:S(2)}, u32[]{:S(2)}) collective-permute-start(bf16[1152,128]{1,0:T(8,128)(2,1)S(1)} %get-tuple-element.10.refs_7_), channel_id=1, source_target_pairs={{2,3},{4,5},{5,4},{9,8},{12,13},{14,15},{15,14},{19,18},{22,23},{1... | collective-permute-start | bytes 884744 | tf_op jit(solution)/shard_map/ppermute | solution.py:64
  22.8 5.8 %collective-permute-start.14 = (bf16[1152,128]{1,0:T(8,128)(2,1)}, bf16[1152,128]{1,0:T(8,128)(2,1)S(1)}, u32[]{:S(2)}, u32[]{:S(2)}) collective-permute-start(bf16[1152,128]{1,0:T(8,128)(2,1)} %collective-permute-done.11.refs_10_), channel_id=1, source_target_pairs={{0,1},{7,6},{31,30},{24,25}} | collective-permute-start | bytes 884744 | tf_op jit(solution)/shard_map/ppermute | solution.py:64
  23.5 9.7 %collective-permute-start.13 = (bf16[1152,128]{1,0:T(8,128)(2,1)}, bf16[1152,128]{1,0:T(8,128)(2,1)S(1)}, u32[]{:S(2)}, u32[]{:S(2)}) collective-permute-start(bf16[1152,128]{1,0:T(8,128)(2,1)} %collective-permute-done.10.refs_9_), channel_id=1, source_target_pairs={{2,3},{11,10},{10,11},{12,13},{21,20},{20,21},{19,18},{29,28}} | collective-permute-start | bytes 884744 | tf_op jit(solution)/shard_map/ppermute | solution.py:64
  27.3 8.6 %collective-permute-start.12 = (bf16[1152,128]{1,0:T(8,128)(2,1)}, bf16[1152,128]{1,0:T(8,128)(2,1)S(1)}, u32[]{:S(2)}, u32[]{:S(2)}) collective-permute-start(bf16[1152,128]{1,0:T(8,128)(2,1)} %collective-permute-done.10.refs_9_), channel_id=1, source_target_pairs={{4,6},{2,0},{3,1},{11,13},{10,8},{12,10},{13,11},{21,23},{20,18},{... | collective-permute-start | bytes 884744 | tf_op jit(solution)/shard_map/ppermute | solution.py:64
  28.6 19.6 %collective-permute-start = (bf16[1536,256]{1,0:T(8,128)(2,1)S(1)}, bf16[1536,256]{1,0:T(8,128)(2,1)S(1)}, u32[]{:S(2)}, u32[]{:S(2)}) collective-permute-start(bf16[1536,256]{1,0:T(8,128)(2,1)S(1)} %get-tuple-element.8.own_ap), channel_id=1, source_target_pairs={{0,16},{1,17},{2,18},{3,19},{4,20},{5,21},{6,22},{7,23},{8,24},{9,... | collective-permute-start | bytes 2359304 | tf_op jit(solution)/shard_map/ppermute | solution.py:204
  33.2 15.1 %collective-permute-start.3 = (bf16[768,512]{1,0:T(8,128)(2,1)S(1)}, bf16[768,512]{1,0:T(8,128)(2,1)S(1)}, u32[]{:S(2)}, u32[]{:S(2)}) collective-permute-start(bf16[768,512]{1,0:T(8,128)(2,1)S(1)} %get-tuple-element.9.refs_0_), channel_id=1, source_target_pairs={{0,1},{1,0},{10,11},{11,10},{20,21},{21,20},{30,31},{31,30}} | collective-permute-start | bytes 2359304 | tf_op jit(solution)/shard_map/ppermute | solution.py:64
  33.9 14.4 %collective-permute-start.8 = (bf16[768,512]{1,0:T(8,128)(2,1)S(1)}, bf16[768,512]{1,0:T(8,128)(2,1)S(1)}, u32[]{:S(2)}, u32[]{:S(2)}) collective-permute-start(bf16[768,512]{1,0:T(8,128)(2,1)S(1)} %collective-permute-done.5.refs_3_), channel_id=1, source_target_pairs={{8,9},{23,22}} | collective-permute-start | bytes 2359304 | tf_op jit(solution)/shard_map/ppermute | solution.py:64
  34.6 19.6 %collective-permute-start.7 = (bf16[768,512]{1,0:T(8,128)(2,1)S(1)}, bf16[768,512]{1,0:T(8,128)(2,1)S(1)}, u32[]{:S(2)}, u32[]{:S(2)}) collective-permute-start(bf16[768,512]{1,0:T(8,128)(2,1)S(1)} %collective-permute-done.4.refs_2_), channel_id=1, source_target_pairs={{3,2},{13,12},{18,19},{28,29}} | collective-permute-start | bytes 2359304 | tf_op jit(solution)/shard_map/ppermute | solution.py:64
  35.9 18.3 %collective-permute-start.6 = (bf16[768,512]{1,0:T(8,128)(2,1)S(1)}, bf16[768,512]{1,0:T(8,128)(2,1)S(1)}, u32[]{:S(2)}, u32[]{:S(2)}) collective-permute-start(bf16[768,512]{1,0:T(8,128)(2,1)S(1)} %collective-permute-done.4.refs_2_), channel_id=1, source_target_pairs={{2,4},{3,5},{12,14},{13,15},{18,16},{19,17},{28,26},{29,27}} | collective-permute-start | bytes 2359304 | tf_op jit(solution)/shard_map/ppermute | solution.py:64

commit v2 on v0

v2 whole, which is shorter than its diff:
```python
import functools

import jax
import jax.numpy as jnp
from jax import lax
from jax.experimental import pallas as pl
from jax.experimental.pallas import tpu as pltpu
from jax.sharding import PartitionSpec as P

TILE = 128
AXES = ("row", "col")
SLOTS = 3
META = 16
MAINS, NEARS, FARS = (0, 1), (2, 3), (4, 5)
UNITS = (
    ((0, 0), (0, 1), (0, 2), (1, 0), (1, 1), (1, 2), (1, 3)),
    ((0, 0), (0, 1), (0, 2), (0, 3), (1, 1), (1, 2), (1, 3)),
    ((0, 0), (1, 0), (1, 1)),
    ((0, 2), (0, 3), (1, 3)),
    ((0, 0), (1, 1)),
    ((0, 2), (1, 3)),
)
OWN, SIDE, UP, DOWN, FAR, DIAG = range(6)
FIRST, SECOND = (SIDE, UP, DOWN), (FAR, DIAG)


def class_sources(r, cols):
    rem = lambda x: lax.rem(x, cols)
    return (2 * r, 2 * r + 1, 2 * r - 1, 2 * r + 2, rem(2 * r + cols // 2), rem(2 * r + 1 + cols // 2))


def kind_sources(c, cols):
    even = c % 2 == 0
    near, past = jnp.where(even, c + 1, c - 1), jnp.where(even, c - 1, c + 1)
    return {OWN: c, SIDE: near, UP: c - 2, DOWN: c + 2, FAR: lax.rem(c + cols // 2, cols), DIAG: past}


def slot_of(name, i, odd, width):
    return 2 if name in FARS else (i + (width if odd else 0)) % SLOTS


def mask_tiles(out_ref, in_ref, pattern_ref, rows):
    for a, row in enumerate(rows):
        for b in range(in_ref.shape[1] // TILE):
            tile = in_ref[pl.ds(row * TILE, TILE), pl.ds(b * TILE, TILE)]
            kept = jnp.where(pattern_ref[b, row] > 0, tile, jnp.zeros_like(tile))
            out_ref[pl.ds(a * TILE, TILE), pl.ds(b * TILE, TILE)] = kept


def prepare_applied(ap_ref, pattern_ref, out_ref):
    odd = lax.axis_index("row") % 2 == 1
    count = ap_ref.shape[0] // TILE
    lower, upper = list(range(count // 2)), list(range(count // 2, count))

    @pl.when(odd)
    def _():
        mask_tiles(out_ref, ap_ref, pattern_ref, upper + lower)

    @pl.when(jnp.logical_not(odd))
    def _():
        mask_tiles(out_ref, ap_ref, pattern_ref, lower + upper)


def prepare_prolong(cols, p_ref, pattern_ref, keep_ref, send_ref):
    r, c = lax.axis_index("row"), lax.axis_index("col")
    tiles = p_ref.shape[0] // TILE // 2
    half = tiles * TILE
    width = p_ref.shape[1] // TILE
    sources = class_sources(r, cols)
    zeros = jnp.zeros((TILE, TILE), p_ref.dtype)
    line = lax.broadcasted_iota(jnp.int32, (META, TILE), 0)

    def pack(name, odd):
        for out_ref, m in ((keep_ref, int(odd)), (send_ref, 1 - int(odd))):
            for s in range(SLOTS):
                found = [i for mm, i in UNITS[name] if mm == m and slot_of(name, i, odd, width) == s]
                for a in range(tiles):
                    value, row = zeros, m * tiles + a
                    for i in found:
                        tile = p_ref[pl.ds(row * TILE, TILE), pl.ds(i * TILE, TILE)]
                        value = jnp.where(pattern_ref[i, row] > 0, tile, value)
                    out_ref[pl.ds(s * half + a * TILE, TILE), :] = value

    def note(odd):
        for out_ref, m in ((keep_ref, int(odd)), (send_ref, 1 - int(odd))):
            value = jnp.zeros((META, TILE), jnp.float32)
            for a in range(tiles):
                for i in range(width):
                    value = jnp.where(line == a * width + i, pattern_ref[i, m * tiles + a].astype(jnp.float32), value)
            out_ref[pl.ds(SLOTS * half, META), :] = value.astype(out_ref.dtype)

    for odd in (False, True):
        parity = (r % 2 == 1) == odd

        @pl.when(parity)
        def _(odd=odd):
            note(odd)

        for name in range(len(UNITS)):
            @pl.when(parity & (c == sources[name]))
            def _(name=name, odd=odd):
                pack(name, odd)

    @pl.when(functools.reduce(jnp.logical_and, [c != s for s in sources]))
    def _():
        for out_ref in (keep_ref, send_ref):
            out_ref[pl.ds(0, SLOTS * half), :] = jnp.zeros((SLOTS * half, TILE), p_ref.dtype)


def merge_kernel(keep_ref, got_ref, half_ref):
    odd = lax.axis_index("row") % 2 == 1
    size = keep_ref.shape[0] - META
    half_ref[pl.ds(0, size), :] = keep_ref[pl.ds(0, size), :] + got_ref[pl.ds(0, size), :]
    mine, theirs = keep_ref[pl.ds(size, META), :], got_ref[pl.ds(size, META), :]
    half_ref[pl.ds(size, META), :] = jnp.where(odd, theirs, mine)
    half_ref[pl.ds(size + META, META), :] = jnp.where(odd, mine, theirs)


def put_columns(out_ref, start, ap):
    rows = ap.shape[0]
    for b in range(ap.shape[1] // TILE):
        out_ref[pl.ds(start + b * rows, rows), :] = ap[:, b * TILE : (b + 1) * TILE]


def forward_kernel(cols, half, side, up, down, ap_ref, far_out, diag_out, swap_out):
    c = lax.axis_index("col")
    relays = cols == 8
    inner_low = relays & (c >= 2) & (c < 4)
    inner_high = relays & (c >= 4) & (c < 6)

    @pl.when(inner_low)
    def _():
        far_out[...] = down[...]

    @pl.when(inner_high)
    def _():
        far_out[...] = up[...]

    @pl.when(jnp.logical_not(inner_low | inner_high))
    def _():
        far_out[...] = half[...]

    @pl.when(c % 2 == 0)
    def _():
        diag_out[...] = down[...]

    @pl.when(c % 2 == 1)
    def _():
        diag_out[...] = up[...]

    size = half.shape[0]
    for j, buffer in enumerate((side, up, down)):
        swap_out[pl.ds(j * size, size), :] = buffer[...]
    depth = ap_ref.shape[0] // 2
    put_columns(swap_out, len(FIRST) * size, ap_ref[pl.ds(depth, depth), :])


def last_swap_kernel(far, diag, far_ap, swap_out):
    size = far.shape[0]
    for j, buffer in enumerate((far, diag)):
        swap_out[pl.ds(j * size, size), :] = buffer[...]
    depth = far_ap.shape[0] // 2
    put_columns(swap_out, len(SECOND) * size, far_ap[pl.ds(0, depth), :])


def product(p, ap):
    return lax.dot_general(p, ap, (((0,), (0,)), ((), ())), preferred_element_type=jnp.float32)


def accumulate(cols, name, valid, buffers, c_ref, block, read_ap, half, width):
    r, c = lax.axis_index("row"), lax.axis_index("col")
    odd = r % 2 == 1
    data = SLOTS * half
    stride = data + META
    source = class_sources(r, cols)[name]
    at = kind_sources(c, cols)
    inside = valid & (source >= 0) & (source < cols)
    here = [inside & (at[kind] == source) for kind in buffers]
    start = {True: pl.multiple_of(jnp.where(odd, stride, 0), META), False: pl.multiple_of(jnp.where(odd, 0, stride), META)}

    @pl.when(functools.reduce(jnp.logical_or, here))
    def _():
        for flag, (kind, (mine, theirs, row)) in zip(here, buffers.items()):
            @pl.when(flag)
            def _(kind=kind, mine=mine, theirs=theirs, row=row):
                for is_mine, ref, base in ((True, mine, 0), (False, theirs, row)):
                    note = data if kind == OWN else pl.multiple_of(data + jnp.where(odd, META, 0), META)
                    block[pl.ds(start[is_mine], data), :] = ref[pl.ds(base, data), :]
                    block[pl.ds(start[is_mine] + data, META), :] = ref[pl.ds(base + note, META), :]
        for m in sorted({m for m, _ in UNITS[name]}):
            pattern = block[pl.ds(m * stride + data, META), :].astype(jnp.float32)
            ap = read_ap(m)
            for i in [i for mm, i in UNITS[name] if mm == m]:
                slot = jnp.where(odd, slot_of(name, i, True, width), slot_of(name, i, False, width))
                first = pl.multiple_of(m * stride + slot * half, META)
                lhs = []
                for a in range(half // TILE):
                    line = a * width + i
                    weight = jnp.broadcast_to(pattern[line : line + 1, :], (TILE, TILE)).astype(block.dtype)
                    lhs.append(block[pl.ds(first + a * TILE, TILE), :] * weight)
                c_ref[pl.ds(i * TILE, TILE), :] += product(jnp.concatenate(lhs, axis=0), ap)


def readers(odd, half, own_ap, core, core_row, far_ap):
    depth = 2 * half

    def in_order(ref, upper):
        row = jnp.where(odd == upper, 0, depth)
        return lambda m: ref[pl.ds(pl.multiple_of(row + m * half, TILE), half), :]

    def columns(ref, start):
        return lambda m: jnp.concatenate([ref[pl.ds(start + b * depth + m * half, half), :] for b in range(2)], axis=1)

    return in_order, columns


def near_kernel(cols, half, width, own_ap, keep, send, side, up, down, swapped, c_ref, block):
    odd = lax.axis_index("row") % 2 == 1
    size = side.shape[0]
    buffers = {OWN: (keep, send, 0)}
    buffers |= {kind: (ref, swapped, j * size) for j, (kind, ref) in enumerate(zip(FIRST, (side, up, down)))}
    in_order, columns = readers(odd, half, own_ap, None, 0, None)
    c_ref[...] = jnp.zeros_like(c_ref)
    for name in MAINS:
        accumulate(cols, name, True, buffers, c_ref, block, in_order(own_ap, name == 1), half, width)
    for name, valid in zip(NEARS, (odd, jnp.logical_not(odd))):
        accumulate(cols, name, valid, buffers, c_ref, block, columns(swapped, len(FIRST) * size), half, width)


def far_kernel(cols, half, width, own_ap, far_ap, keep, send, side, up, down, swapped, far, diag, last, cross, partial, c_ref, block):
    odd = lax.axis_index("row") % 2 == 1
    size = side.shape[0]
    early = {OWN: (keep, send, 0)}
    early |= {kind: (ref, swapped, j * size) for j, (kind, ref) in enumerate(zip(FIRST, (side, up, down)))}
    late = {kind: (ref, last, j * size) for j, (kind, ref) in enumerate(zip(SECOND, (far, diag)))}
    in_order, columns = readers(odd, half, own_ap, None, 0, None)
    c_ref[...] = partial[...]
    for name in MAINS:
        accumulate(cols, name, True, late, c_ref, block, in_order(own_ap, name == 1), half, width)
    for name, valid in zip(NEARS, (odd, jnp.logical_not(odd))):
        accumulate(cols, name, valid, late, c_ref, block, columns(swapped, len(FIRST) * size), half, width)
        cross_row = cross.shape[0] - own_ap.shape[0]
        accumulate(cols, name, jnp.logical_not(valid), early | late, c_ref, block, columns(cross, cross_row), half, width)
    for name in FARS:
        accumulate(cols, name, True, early | late, c_ref, block, in_order(far_ap, name == 5), half, width)


def on_device(rows, cols, prolong, applied, prolong_pattern, applied_pattern):
    depth, width = prolong.shape[0], prolong.shape[1] // TILE
    half = depth // 2
    data = SLOTS * half
    size = data + 2 * META
    vmem = pl.BlockSpec(memory_space=pltpu.VMEM)
    smem = pl.BlockSpec(memory_space=pltpu.SMEM)
    params = pltpu.CompilerParams(vmem_limit_bytes=24 << 20)
    shape = lambda *s: jax.ShapeDtypeStruct(s, prolong.dtype)

    def call(kernel, name, out_shape, *operands, specs=None, **more):
        out_specs = (vmem,) * len(out_shape) if isinstance(out_shape, tuple) else vmem
        return pl.pallas_call(
            kernel, out_shape=out_shape, in_specs=specs or [vmem] * len(operands), out_specs=out_specs,
            compiler_params=params, name=name, **more,
        )(*operands)

    def move(x, pairs):
        return lax.ppermute(x, AXES, pairs)

    def row_pairs(pairs):
        return [(a * cols + c, b * cols + c) for a, b in pairs for c in range(cols)]

    def col_pairs(pairs):
        return [(r * cols + a, r * cols + b) for r in range(rows) for a, b in pairs if 0 <= b < cols]

    partner = row_pairs([(r, r ^ 1) for r in range(rows)])
    opposite = [(r, (r + rows // 2) % rows) for r in range(rows)]

    own_ap = call(prepare_applied, "prepare_applied", shape(*applied.shape), applied, applied_pattern.T, specs=[vmem, smem])
    far_ap = move(own_ap, row_pairs(opposite))
    keep, send = call(
        functools.partial(prepare_prolong, cols), "prepare_prolong", (shape(data + META, TILE),) * 2,
        prolong, prolong_pattern.T, specs=[vmem, smem],
    )
    mine = call(merge_kernel, "merge", shape(size, TILE), keep, move(send, partner))
    side = move(mine, col_pairs([(c, c ^ 1) for c in range(cols)]))
    up = move(mine, col_pairs([(c, c + 2) for c in range(cols)]))
    down = move(mine, col_pairs([(c, c - 2) for c in range(cols)]))

    ap_rows = 2 * depth
    far_send, diag_send, swap = call(
        functools.partial(forward_kernel, cols), "forward",
        (shape(size, TILE), shape(size, TILE), shape(len(FIRST) * size + ap_rows, TILE)), mine, side, up, down, own_ap,
    )
    if cols == 8:
        far_pairs = [(0, 4), (1, 5), (2, 0), (3, 1), (4, 6), (5, 7), (6, 2), (7, 3)]
    else:
        far_pairs = [(c, (c + cols // 2) % cols) for c in range(cols)]
    far = move(far_send, col_pairs(far_pairs))
    diag = move(diag_send, col_pairs([(c, c + 1) for c in range(0, cols - 2, 2)] + [(c, c - 1) for c in range(3, cols, 2)]))
    swapped = move(swap, partner)
    last = move(
        call(last_swap_kernel, "last_swap", shape(len(SECOND) * size + ap_rows, TILE), far, diag, far_ap), partner
    )
    beyond = [(r, r + 1 if r % 2 == 1 else r - 1) for r in range(rows)]
    relay = [((r + rows // 2) % rows, t) for r, t in beyond if 0 <= t < rows]
    if all(h ^ 1 == t for h, t in relay):
        cross = last
    else:
        first = own_ap[:depth].reshape(depth, 2, TILE).transpose(1, 0, 2).reshape(ap_rows, TILE)
        cross = move(first, row_pairs([(r, t) for r, t in beyond if 0 <= t < rows]))

    result = jax.ShapeDtypeStruct((prolong.shape[1], applied.shape[1]), jnp.float32)
    scratch = dict(scratch_shapes=[pltpu.VMEM((2 * (data + META), TILE), prolong.dtype)])
    partial = call(
        functools.partial(near_kernel, cols, half, width), "near", result,
        own_ap, keep, send, side, up, down, swapped, **scratch,
    )
    return call(
        functools.partial(far_kernel, cols, half, width), "far", result,
        own_ap, far_ap, keep, send, side, up, down, swapped, far, diag, last, cross, partial, **scratch,
    )


def solution(mesh):
    in_specs = (P("col", "row"), P("row", "col"), P("col", "row"), P("row", "col"))
    return jax.shard_map(
        functools.partial(on_device, mesh.shape["row"], mesh.shape["col"]),
        mesh=mesh, in_specs=in_specs, out_specs=P("row", "col"), check_vma=False,
    )
```

time: 940 us -> 39.3 us (0.04)
  waiting for transfers between devices: 893 us -> 16.9 us
  other arithmetic: 15.2 us -> 0 us
  starting transfers between devices: 0.67 us -> 14.9 us
  matrix products: 13.9 us -> 0 us
  between operations: 13.1 us -> 0.11 us
    psum x16 -> x0, waiting for transfers between devices: 893 us -> none  [from_root(): return lax.psum(kept, axis)]
    ppermute x0 -> x9, waiting for transfers between devices: none -> 16.9 us  [move(): return lax.ppermute(x, AXES, pairs)]
    ppermute x0 -> x9, starting transfers between devices: none -> 14.9 us  [move(): return lax.ppermute(x, AXES, pairs)]
    select_n x16 -> x0, other arithmetic: 14.2 us -> none  [from_root(): jnp.where(lax.axis_index(axis) == source, value, 0).astype(value.dtype)]
    dot_general x8 -> x0, matrix products: 13.9 us -> none  [accumulate(): lax.dot_general(r_piece, ap_piece, (((0,), (0,)), ((), ())), preferred_el...]
  transfers between devices with their start and end apart: 16 -> 9, of which waited for: 16 -> 6; matrix products, arithmetic and copies ran while one was open for 1% -> 0% of each run, Pallas kernels for 0% -> 6%
where the time goes in v2:
time: 39.3 us; the launch traced here: 39 us
  waiting for transfers between devices  16.9 us (43%)
  starting transfers between devices  14.9 us (38%)
  Pallas kernels  4.58 us (12%)
  local copies, waits for them, and re-layouts  2.5 us (6%)
    ppermute x9, waiting for transfers between devices, move(): return lax.ppermute(x, AXES, pairs)  16.9 us
    ppermute x9, starting transfers between devices, move(): return lax.ppermute(x, AXES, pairs)  14.9 us
    pallas_call x7, Pallas kernels, call(): pl.pallas_call(kernel, out_shape=out_shape, in_specs=specs or [vmem] * le...  4.58 us
    unnamed x8, local copies, waits for them, and re-layouts  2.5 us
  transfers between devices with their start and end apart: 9, of which 6 were waited for; matrix products, arithmetic and copies ran while one was open for 0% of the time, Pallas kernels for 6%

profile of v2, /device:TPU:0, one launch (start us, length us, event | category | flops | bytes accessed | tf_op | source)
XLA Modules:
  0.0 39.0 jit_solution(6897121057554041976)
XLA Ops:
  0.0 1.1 %copy-done = bf16[768,512]{1,0:T(8,128)(2,1)S(1)} copy-done((bf16[768,512]{1,0:T(8,128)(2,1)S(1)}, bf16[768,512]{1,0:T(8,128)(2,1)}, u32[]{:S(2)}) %copy-start) | copy-done | bytes 786456
  1.1 0.7 %copy-done.2 = s32[6,4]{0,1:T(4,128)S(1)} copy-done((s32[6,4]{0,1:T(4,128)S(1)}, s32[6,4]{0,1:T(4,128)}, u32[]{:S(2)}) %copy-start.2) | copy-done | bytes 120
  1.8 0.8 %prepare_prolong.1 = (bf16[1168,128]{1,0:T(8,128)(2,1)S(1)}, bf16[1168,128]{1,0:T(8,128)(2,1)S(1)}) custom-call(bf16[768,512]{1,0:T(8,128)(2,1)S(1)} %copy-done, s32[4,6]{1,0:T(4,128)S(1)} %bitcast.2), custom_call_target="tpu_custom_call" | custom-call | tf_op jit(solution)/shard_map/prepare_prolong/pallas_call | solution.py:260
  2.6 0.5 %collective-permute-start.1 = (bf16[1168,128]{1,0:T(8,128)(2,1)S(1)}, bf16[1168,128]{1,0:T(8,128)(2,1)S(1)}, u32[]{:S(2)}, u32[]{:S(2)}) collective-permute-start(bf16[1168,128]{1,0:T(8,128)(2,1)S(1)} %get-tuple-element.11.send), channel_id=1, source_target_pairs={{0,8},{1,9},{2,10},{3,11},{4,12},{5,13},{6,14},{7,15},{8,0},{9,1},... | collective-permute-start | bytes 897032 | tf_op jit(solution)/shard_map/ppermute | solution.py:266
  3.1 0.7 %copy-done.3 = s32[12,2]{0,1:T(2,128)S(1)} copy-done((s32[12,2]{0,1:T(2,128)S(1)}, s32[12,2]{0,1:T(2,128)}, u32[]{:S(2)}) %copy-start.3) | copy-done | bytes 120
  3.8 0.7 %prepare_applied.1.ap_ref.own_ap = bf16[1536,256]{1,0:T(8,128)(2,1)S(1)} custom-call(bf16[1536,256]{1,0:T(8,128)(2,1)S(1)} %copy-done.1, s32[2,12]{1,0:T(2,128)S(1)} %bitcast.3), custom_call_target="tpu_custom_call" | custom-call | tf_op jit(solution)/shard_map/prepare_applied/pallas_call | solution.py:260
  4.5 2.9 %collective-permute-start = (bf16[1536,256]{1,0:T(8,128)(2,1)S(1)}, bf16[1536,256]{1,0:T(8,128)(2,1)S(1)}, u32[]{:S(2)}, u32[]{:S(2)}) collective-permute-start(bf16[1536,256]{1,0:T(8,128)(2,1)S(1)} %prepare_applied.1.ap_ref.own_ap), channel_id=1, source_target_pairs={{0,16},{1,17},{2,18},{3,19},{4,20},{5,21},{6,22},{7,23},{8,24},{9,... | collective-permute-start | bytes 2359304 | tf_op jit(solution)/shard_map/ppermute | solution.py:266
  7.5 1.6 %collective-permute-start.2 = (bf16[1184,128]{1,0:T(8,128)(2,1)S(1)}, bf16[1184,128]{1,0:T(8,128)(2,1)S(1)}, u32[]{:S(2)}, u32[]{:S(2)}) collective-permute-start(bf16[1184,128]{1,0:T(8,128)(2,1)S(1)} %merge.1.half), channel_id=1, source_target_pairs={{0,1},{1,0},{2,3},{3,2},{4,5},{5,4},{6,7},{7,6},{8,9},{9,8},{10,11... | collective-permute-start | bytes 909320 | tf_op jit(solution)/shard_map/ppermute | solution.py:266
  9.0 3.5 %collective-permute-start.3 = (bf16[1184,128]{1,0:T(8,128)(2,1)S(1)}, bf16[1184,128]{1,0:T(8,128)(2,1)S(1)}, u32[]{:S(2)}, u32[]{:S(2)}) collective-permute-start(bf16[1184,128]{1,0:T(8,128)(2,1)S(1)} %merge.1.half), channel_id=1, source_target_pairs={{0,2},{1,3},{2,4},{3,5},{4,6},{5,7},{8,10},{9,11},{10,12},{11,13},... | collective-permute-start | bytes 909320 | tf_op jit(solution)/shard_map/ppermute | solution.py:266
  12.5 1.3 %collective-permute-start.4 = (bf16[1184,128]{1,0:T(8,128)(2,1)S(1)}, bf16[1184,128]{1,0:T(8,128)(2,1)S(1)}, u32[]{:S(2)}, u32[]{:S(2)}) collective-permute-start(bf16[1184,128]{1,0:T(8,128)(2,1)S(1)} %merge.1.half), channel_id=1, source_target_pairs={{2,0},{3,1},{4,2},{5,3},{6,4},{7,5},{10,8},{11,9},{12,10},{13,11},... | collective-permute-start | bytes 909320 | tf_op jit(solution)/shard_map/ppermute | solution.py:266
  13.8 2.7 %collective-permute-done.2.side = bf16[1184,128]{1,0:T(8,128)(2,1)S(1)} collective-permute-done((bf16[1184,128]{1,0:T(8,128)(2,1)S(1)}, bf16[1184,128]{1,0:T(8,128)(2,1)S(1)}, u32[]{:S(2)}, u32[]{:S(2)}) %collective-permute-start.2) | collective-permute-done | bytes 303136 | tf_op jit(solution)/shard_map/ppermute | solution.py:266
  16.6 2.2 %collective-permute-done.3.up = bf16[1184,128]{1,0:T(8,128)(2,1)S(1)} collective-permute-done((bf16[1184,128]{1,0:T(8,128)(2,1)S(1)}, bf16[1184,128]{1,0:T(8,128)(2,1)S(1)}, u32[]{:S(2)}, u32[]{:S(2)}) %collective-permute-start.3) | collective-permute-done | bytes 303136 | tf_op jit(solution)/shard_map/ppermute | solution.py:266
  18.8 4.1 %collective-permute-done.4.down = bf16[1184,128]{1,0:T(8,128)(2,1)S(1)} collective-permute-done((bf16[1184,128]{1,0:T(8,128)(2,1)S(1)}, bf16[1184,128]{1,0:T(8,128)(2,1)S(1)}, u32[]{:S(2)}, u32[]{:S(2)}) %collective-permute-start.4) | collective-permute-done | bytes 303136 | tf_op jit(solution)/shard_map/ppermute | solution.py:266
  22.9 0.2 forward.1
  23.1 0.1 collective-permute-start.5
  23.2 2.6 %collective-permute-start.6 = (bf16[1184,128]{1,0:T(8,128)(2,1)S(1)}, bf16[1184,128]{1,0:T(8,128)(2,1)S(1)}, u32[]{:S(2)}, u32[]{:S(2)}) collective-permute-start(bf16[1184,128]{1,0:T(8,128)(2,1)S(1)} %get-tuple-element.13), channel_id=1, source_target_pairs={{0,4},{1,5},{2,0},{3,1},{4,6},{5,7},{6,2},{7,3},{8,12},{9,13},{10,... | collective-permute-start | bytes 909320 | tf_op jit(solution)/shard_map/ppermute | solution.py:266
  25.8 2.5 %collective-permute-start.7 = (bf16[1184,128]{1,0:T(8,128)(2,1)S(1)}, bf16[1184,128]{1,0:T(8,128)(2,1)S(1)}, u32[]{:S(2)}, u32[]{:S(2)}) collective-permute-start(bf16[1184,128]{1,0:T(8,128)(2,1)S(1)} %get-tuple-element.14), channel_id=1, source_target_pairs={{0,1},{2,3},{4,5},{3,2},{5,4},{7,6},{8,9},{10,11},{12,13},{11,10},... | collective-permute-start | bytes 909320 | tf_op jit(solution)/shard_map/ppermute | solution.py:266
  28.3 4.6 %collective-permute-done.6.far = bf16[1184,128]{1,0:T(8,128)(2,1)S(1)} collective-permute-done((bf16[1184,128]{1,0:T(8,128)(2,1)S(1)}, bf16[1184,128]{1,0:T(8,128)(2,1)S(1)}, u32[]{:S(2)}, u32[]{:S(2)}) %collective-permute-start.6) | collective-permute-done | bytes 303136 | tf_op jit(solution)/shard_map/ppermute | solution.py:266
  32.8 2.2 %collective-permute-done.7.diag = bf16[1184,128]{1,0:T(8,128)(2,1)S(1)} collective-permute-done((bf16[1184,128]{1,0:T(8,128)(2,1)S(1)}, bf16[1184,128]{1,0:T(8,128)(2,1)S(1)}, u32[]{:S(2)}, u32[]{:S(2)}) %collective-permute-start.7) | collective-permute-done | bytes 303136 | tf_op jit(solution)/shard_map/ppermute | solution.py:266
  35.0 0.1 last_swap.1
  35.1 0.1 collective-permute-start.8
  35.2 1.4 %near.1.partial = f32[512,256]{1,0:T(8,128)S(1)} custom-call(bf16[1536,256]{1,0:T(8,128)(2,1)S(1)} %prepare_applied.1.ap_ref.own_ap, bf16[1168,128]{1,0:T(8,128)(2,1)S(1)} %get-tuple-element.10.keep_ref.keep, bf16[1168,128]{1,0:T(8,128)(2,1)S(1)} %get-tuple-element.11.send, bf16[1184,128]{1,0:T(8,128)(2,1)S(1)} %collective-permute-done.2.side, ...), custom_call_target="tpu_custom_call" | custom-call | tf_op jit(solution)/shard_map/near/pallas_call | solution.py:260
  36.6 1.1 %collective-permute-done.8.last.cross = bf16[3904,128]{1,0:T(8,128)(2,1)S(1)} collective-permute-done((bf16[3904,128]{1,0:T(8,128)(2,1)S(1)}, bf16[3904,128]{1,0:T(8,128)(2,1)S(1)}, u32[]{:S(2)}, u32[]{:S(2)}) %collective-permute-start.8) | collective-permute-done | bytes 999456 | tf_op jit(solution)/shard_map/ppermute | solution.py:266
  37.7 1.3 %far.1 = f32[512,256]{1,0:T(8,128)} custom-call(bf16[1536,256]{1,0:T(8,128)(2,1)S(1)} %prepare_applied.1.ap_ref.own_ap, bf16[1536,256]{1,0:T(8,128)(2,1)S(1)} %collective-permute-done.far_ap, bf16[1168,128]{1,0:T(8,128)(2,1)S(1)} %get-tuple-element.10.keep_ref.keep, bf16[1168,128]{1,0:T(8,128)(2,1)S(1)} %get-tuple-element.11.send, ...), custom_call_target="tpu_custom_call" | custom-call | tf_op jit(solution)/shard_map/far/pallas_call | solution.py:260
  (9 shorter events, 0.1 us)
Async XLA Ops:
  0.0 1.1 %copy-start = (bf16[768,512]{1,0:T(8,128)(2,1)S(1)}, bf16[768,512]{1,0:T(8,128)(2,1)}, u32[]{:S(2)}) copy-start(bf16[768,512]{1,0:T(8,128)(2,1)} %p_ref.1) | copy-start | bytes 2359300
  1.1 0.7 %copy-start.2 = (s32[6,4]{0,1:T(4,128)S(1)}, s32[6,4]{0,1:T(4,128)}, u32[]{:S(2)}) copy-start(s32[6,4]{0,1:T(4,128)} %param.6) | copy-start | bytes 292
  1.8 1.3 %copy-start.1 = (bf16[1536,256]{1,0:T(8,128)(2,1)S(1)}, bf16[1536,256]{1,0:T(8,128)(2,1)}, u32[]{:S(2)}) copy-start(bf16[1536,256]{1,0:T(8,128)(2,1)} %ap_ref.1) | copy-start | bytes 2359300
  2.6 4.8 %collective-permute-start.1 = (bf16[1168,128]{1,0:T(8,128)(2,1)S(1)}, bf16[1168,128]{1,0:T(8,128)(2,1)S(1)}, u32[]{:S(2)}, u32[]{:S(2)}) collective-permute-start(bf16[1168,128]{1,0:T(8,128)(2,1)S(1)} %get-tuple-element.11.send), channel_id=1, source_target_pairs={{0,8},{1,9},{2,10},{3,11},{4,12},{5,13},{6,14},{7,15},{8,0},{9,1},... | collective-permute-start | bytes 897032 | tf_op jit(solution)/shard_map/ppermute | solution.py:266
  3.1 0.7 %copy-start.3 = (s32[12,2]{0,1:T(2,128)S(1)}, s32[12,2]{0,1:T(2,128)}, u32[]{:S(2)}) copy-start(s32[12,2]{0,1:T(2,128)} %param.7) | copy-start | bytes 292
  4.5 23.7 %collective-permute-start = (bf16[1536,256]{1,0:T(8,128)(2,1)S(1)}, bf16[1536,256]{1,0:T(8,128)(2,1)S(1)}, u32[]{:S(2)}, u32[]{:S(2)}) collective-permute-start(bf16[1536,256]{1,0:T(8,128)(2,1)S(1)} %prepare_applied.1.ap_ref.own_ap), channel_id=1, source_target_pairs={{0,16},{1,17},{2,18},{3,19},{4,20},{5,21},{6,22},{7,23},{8,24},{9,... | collective-permute-start | bytes 2359304 | tf_op jit(solution)/shard_map/ppermute | solution.py:266
  7.5 9.1 %collective-permute-start.2 = (bf16[1184,128]{1,0:T(8,128)(2,1)S(1)}, bf16[1184,128]{1,0:T(8,128)(2,1)S(1)}, u32[]{:S(2)}, u32[]{:S(2)}) collective-permute-start(bf16[1184,128]{1,0:T(8,128)(2,1)S(1)} %merge.1.half), channel_id=1, source_target_pairs={{0,1},{1,0},{2,3},{3,2},{4,5},{5,4},{6,7},{7,6},{8,9},{9,8},{10,11... | collective-permute-start | bytes 909320 | tf_op jit(solution)/shard_map/ppermute | solution.py:266
  9.0 9.7 %collective-permute-start.3 = (bf16[1184,128]{1,0:T(8,128)(2,1)S(1)}, bf16[1184,128]{1,0:T(8,128)(2,1)S(1)}, u32[]{:S(2)}, u32[]{:S(2)}) collective-permute-start(bf16[1184,128]{1,0:T(8,128)(2,1)S(1)} %merge.1.half), channel_id=1, source_target_pairs={{0,2},{1,3},{2,4},{3,5},{4,6},{5,7},{8,10},{9,11},{10,12},{11,13},... | collective-permute-start | bytes 909320 | tf_op jit(solution)/shard_map/ppermute | solution.py:266
  12.5 10.4 %collective-permute-start.4 = (bf16[1184,128]{1,0:T(8,128)(2,1)S(1)}, bf16[1184,128]{1,0:T(8,128)(2,1)S(1)}, u32[]{:S(2)}, u32[]{:S(2)}) collective-permute-start(bf16[1184,128]{1,0:T(8,128)(2,1)S(1)} %merge.1.half), channel_id=1, source_target_pairs={{2,0},{3,1},{4,2},{5,3},{6,4},{7,5},{10,8},{11,9},{12,10},{13,11},... | collective-permute-start | bytes 909320 | tf_op jit(solution)/shard_map/ppermute | solution.py:266
  23.1 12.1 %collective-permute-start.5 = (bf16[5088,128]{1,0:T(8,128)(2,1)S(1)}, bf16[5088,128]{1,0:T(8,128)(2,1)S(1)}, u32[]{:S(2)}, u32[]{:S(2)}) collective-permute-start(bf16[5088,128]{1,0:T(8,128)(2,1)S(1)} %get-tuple-element.12), channel_id=1, source_target_pairs={{0,8},{1,9},{2,10},{3,11},{4,12},{5,13},{6,14},{7,15},{8,0},{9,1},... | collective-permute-start | bytes 3907592 | tf_op jit(solution)/shard_map/ppermute | solution.py:266
  23.2 9.7 %collective-permute-start.6 = (bf16[1184,128]{1,0:T(8,128)(2,1)S(1)}, bf16[1184,128]{1,0:T(8,128)(2,1)S(1)}, u32[]{:S(2)}, u32[]{:S(2)}) collective-permute-start(bf16[1184,128]{1,0:T(8,128)(2,1)S(1)} %get-tuple-element.13), channel_id=1, source_target_pairs={{0,4},{1,5},{2,0},{3,1},{4,6},{5,7},{6,2},{7,3},{8,12},{9,13},{10,... | collective-permute-start | bytes 909320 | tf_op jit(solution)/shard_map/ppermute | solution.py:266
  25.8 9.2 %collective-permute-start.7 = (bf16[1184,128]{1,0:T(8,128)(2,1)S(1)}, bf16[1184,128]{1,0:T(8,128)(2,1)S(1)}, u32[]{:S(2)}, u32[]{:S(2)}) collective-permute-start(bf16[1184,128]{1,0:T(8,128)(2,1)S(1)} %get-tuple-element.14), channel_id=1, source_target_pairs={{0,1},{2,3},{4,5},{3,2},{5,4},{7,6},{8,9},{10,11},{12,13},{11,10},... | collective-permute-start | bytes 909320 | tf_op jit(solution)/shard_map/ppermute | solution.py:266
  35.1 2.7 %collective-permute-start.8 = (bf16[3904,128]{1,0:T(8,128)(2,1)S(1)}, bf16[3904,128]{1,0:T(8,128)(2,1)S(1)}, u32[]{:S(2)}, u32[]{:S(2)}) collective-permute-start(bf16[3904,128]{1,0:T(8,128)(2,1)S(1)} %last_swap.1), channel_id=1, source_target_pairs={{0,8},{1,9},{2,10},{3,11},{4,12},{5,13},{6,14},{7,15},{8,0},{9,1},... | collective-permute-start | bytes 2998280 | tf_op jit(solution)/shard_map/ppermute | solution.py:266

commit v3 on v2

v3 whole, which is shorter than its diff:
```python
import functools

import jax
import jax.numpy as jnp
from jax import lax
from jax.experimental import pallas as pl
from jax.experimental.pallas import tpu as pltpu
from jax.sharding import PartitionSpec as P

TILE = 128
AXES = ("row", "col")
LAST_WEIGHT = 20
SLOTS = 3
META = 16
MAINS, NEARS, FARS = (0, 1), (2, 3), (4, 5)
UNITS = (
    ((0, 0), (0, 1), (0, 2), (1, 0), (1, 1), (1, 2), (1, 3)),
    ((0, 0), (0, 1), (0, 2), (0, 3), (1, 1), (1, 2), (1, 3)),
    ((0, 0), (1, 0), (1, 1)),
    ((0, 2), (0, 3), (1, 3)),
    ((0, 0), (1, 1)),
    ((0, 2), (1, 3)),
)
OWN, SIDE, PAIR, CROSS, FAR, DIAG = range(6)
FIRST, SECOND = (SIDE, PAIR, CROSS), (FAR, DIAG)


def class_sources(r, cols):
    rem = lambda x: lax.rem(x, cols)
    return (2 * r, 2 * r + 1, 2 * r - 1, 2 * r + 2, rem(2 * r + cols // 2), rem(2 * r + 1 + cols // 2))


def kind_sources(c, cols):
    even, low = c % 2 == 0, (c // 2) % 2 == 0
    near, past = jnp.where(even, c + 1, c - 1), jnp.where(even, c - 1, c + 1)
    pair, across = jnp.where(low, c + 2, c - 2), jnp.where(low, c - 2, c + 2)
    return {OWN: c, SIDE: near, PAIR: pair, CROSS: across, FAR: lax.rem(c + cols // 2, cols), DIAG: past}


def slot_of(name, i, odd, width):
    return 2 if name in FARS else (i + (width if odd else 0)) % SLOTS


def prepare_kernel(cols, p_hbm, ap_hbm, p_pattern_hbm, ap_pattern_hbm, keep_ref, send_ref, out_ref, p_ref, ap_ref, p_pattern, ap_pattern, sems):
    copies = [
        pltpu.make_async_copy(source, target, sems.at[i])
        for i, (source, target) in enumerate(
            ((p_pattern_hbm, p_pattern), (p_hbm, p_ref), (ap_pattern_hbm, ap_pattern), (ap_hbm, ap_ref))
        )
    ]
    for copy in copies:
        copy.start()
    r, c = lax.axis_index("row"), lax.axis_index("col")
    tiles = p_ref.shape[0] // TILE // 2
    half = tiles * TILE
    width = p_ref.shape[1] // TILE
    sources = class_sources(r, cols)
    zeros = jnp.zeros((TILE, TILE), p_ref.dtype)
    line = lax.broadcasted_iota(jnp.int32, (META, TILE), 0)

    def pack(name, odd):
        for out_ref, m in ((keep_ref, int(odd)), (send_ref, 1 - int(odd))):
            for s in range(SLOTS):
                found = [i for mm, i in UNITS[name] if mm == m and slot_of(name, i, odd, width) == s]
                for a in range(tiles):
                    value, row = zeros, m * tiles + a
                    for i in found:
                        tile = p_ref[pl.ds(row * TILE, TILE), pl.ds(i * TILE, TILE)]
                        value = jnp.where(p_pattern[i, row] > 0, tile, value)
                    out_ref[pl.ds(s * half + a * TILE, TILE), :] = value

    def note(odd):
        for out_ref, m in ((keep_ref, int(odd)), (send_ref, 1 - int(odd))):
            value = jnp.zeros((META, TILE), jnp.float32)
            for a in range(tiles):
                for i in range(width):
                    value = jnp.where(line == a * width + i, p_pattern[i, m * tiles + a].astype(jnp.float32), value)
            out_ref[pl.ds(SLOTS * half, META), :] = value.astype(out_ref.dtype)

    copies[0].wait()
    copies[1].wait()
    for odd in (False, True):
        parity = (r % 2 == 1) == odd

        @pl.when(parity)
        def _(odd=odd):
            note(odd)

        for name in range(len(UNITS)):
            @pl.when(parity & (c == sources[name]))
            def _(name=name, odd=odd):
                pack(name, odd)

    @pl.when(functools.reduce(jnp.logical_and, [c != s for s in sources]))
    def _():
        for out in (keep_ref, send_ref):
            out[pl.ds(0, SLOTS * half), :] = jnp.zeros((SLOTS * half, TILE), p_ref.dtype)

    copies[2].wait()
    copies[3].wait()
    count = ap_ref.shape[0] // TILE
    shift = jnp.where(r % 2 == 1, count // 2, 0)
    for a in range(count):
        row = lax.rem(a + shift, count)
        rows = pl.ds(pl.multiple_of(row * TILE, TILE), TILE)
        for b in range(ap_ref.shape[1] // TILE):
            tile = ap_ref[rows, pl.ds(b * TILE, TILE)]
            out_ref[pl.ds(a * TILE, TILE), pl.ds(b * TILE, TILE)] = jnp.where(ap_pattern[b, row] > 0, tile, zeros)


def merge_kernel(keep_ref, got_ref, half_ref):
    odd = lax.axis_index("row") % 2 == 1
    size = keep_ref.shape[0] - META
    half_ref[pl.ds(0, size), :] = keep_ref[pl.ds(0, size), :] + got_ref[pl.ds(0, size), :]
    mine, theirs = keep_ref[pl.ds(size, META), :], got_ref[pl.ds(size, META), :]
    half_ref[pl.ds(size, META), :] = jnp.where(odd, theirs, mine)
    half_ref[pl.ds(size + META, META), :] = jnp.where(odd, mine, theirs)


def put_columns(out_ref, start, ap):
    rows = ap.shape[0]
    for b in range(ap.shape[1] // TILE):
        out_ref[pl.ds(start + b * rows, rows), :] = ap[:, b * TILE : (b + 1) * TILE]


def far_forward_kernel(cols, own, cross, out_ref):
    c = lax.axis_index("col")
    inner = (cols == 8) & (c >= 2) & (c < 6)

    @pl.when(inner)
    def _():
        out_ref[...] = cross[...]

    @pl.when(jnp.logical_not(inner))
    def _():
        out_ref[...] = own[...]


def diagonal_forward_kernel(pair, cross, out_ref):
    c = lax.axis_index("col")
    by_pair = (c % 2 == 0) == ((c // 2) % 2 == 0)

    @pl.when(by_pair)
    def _():
        out_ref[...] = pair[...]

    @pl.when(jnp.logical_not(by_pair))
    def _():
        out_ref[...] = cross[...]


def swap_kernel(side, pair, cross, own_ap, far_ap, out_ref):
    size = side.shape[0]
    for j, buffer in enumerate((side, pair, cross)):
        out_ref[pl.ds(j * size, size), :] = buffer[...]
    depth = own_ap.shape[0] // 2
    start = len(FIRST) * size
    put_columns(out_ref, start, own_ap[pl.ds(depth, depth), :])
    put_columns(out_ref, start + own_ap.shape[0], far_ap[pl.ds(0, depth), :])


def last_swap_kernel(far, diag, out_ref):
    size = far.shape[0]
    for j, buffer in enumerate((far, diag)):
        out_ref[pl.ds(j * size, size), :] = buffer[...]


def product(p, ap):
    return lax.dot_general(p, ap, (((0,), (0,)), ((), ())), preferred_element_type=jnp.float32)


def accumulate(cols, name, valid, buffers, c_ref, block, read_ap, half, width):
    r, c = lax.axis_index("row"), lax.axis_index("col")
    odd = r % 2 == 1
    data = SLOTS * half
    stride = data + META
    source = class_sources(r, cols)[name]
    at = kind_sources(c, cols)
    inside = valid & (source >= 0) & (source < cols)
    here = [inside & (at[kind] == source) for kind in buffers]
    start = {True: pl.multiple_of(jnp.where(odd, stride, 0), META), False: pl.multiple_of(jnp.where(odd, 0, stride), META)}

    @pl.when(functools.reduce(jnp.logical_or, here))
    def _():
        for flag, (kind, (mine, theirs, row)) in zip(here, buffers.items()):
            @pl.when(flag)
            def _(kind=kind, mine=mine, theirs=theirs, row=row):
                for is_mine, ref, base in ((True, mine, 0), (False, theirs, row)):
                    note = data if kind == OWN else pl.multiple_of(data + jnp.where(odd, META, 0), META)
                    block[pl.ds(start[is_mine], data), :] = ref[pl.ds(base, data), :]
                    block[pl.ds(start[is_mine] + data, META), :] = ref[pl.ds(base + note, META), :]
        for m in sorted({m for m, _ in UNITS[name]}):
            pattern = block[pl.ds(m * stride + data, META), :].astype(jnp.float32)
            ap = read_ap(m)
            for i in [i for mm, i in UNITS[name] if mm == m]:
                slot = jnp.where(odd, slot_of(name, i, True, width), slot_of(name, i, False, width))
                first = pl.multiple_of(m * stride + slot * half, META)
                lhs = []
                for a in range(half // TILE):
                    line = a * width + i
                    weight = jnp.broadcast_to(pattern[line : line + 1, :], (TILE, TILE)).astype(block.dtype)
                    lhs.append(block[pl.ds(first + a * TILE, TILE), :] * weight)
                c_ref[pl.ds(i * TILE, TILE), :] += product(jnp.concatenate(lhs, axis=0), ap)


def readers(odd, half):
    depth = 2 * half

    def in_order(ref, upper):
        row = jnp.where(odd == upper, 0, depth)
        return lambda m: ref[pl.ds(pl.multiple_of(row + m * half, TILE), half), :]

    def columns(ref, start):
        return lambda m: jnp.concatenate([ref[pl.ds(start + b * depth + m * half, half), :] for b in range(2)], axis=1)

    return in_order, columns


def add_all(cols, half, width, buffers, own_ap, far_ap, swapped, size, cross_ap, c_ref, block):
    odd = lax.axis_index("row") % 2 == 1
    in_order, columns = readers(odd, half)
    for name in MAINS:
        accumulate(cols, name, True, buffers, c_ref, block, in_order(own_ap, name == 1), half, width)
    core, cross = columns(swapped, len(FIRST) * size), columns(cross_ap, cross_ap.shape[0] - own_ap.shape[0])
    for name, valid in zip(NEARS, (odd, jnp.logical_not(odd))):
        accumulate(cols, name, valid, buffers, c_ref, block, core, half, width)
        accumulate(cols, name, jnp.logical_not(valid), buffers, c_ref, block, cross, half, width)
    for name in FARS:
        accumulate(cols, name, True, buffers, c_ref, block, in_order(far_ap, name == 5), half, width)


def near_kernel(cols, half, width, own_ap, far_ap, keep, send, side, pair, cross, swapped, cross_ap, c_ref, block):
    size = side.shape[0]
    buffers = {OWN: (keep, send, 0)}
    buffers |= {kind: (ref, swapped, j * size) for j, (kind, ref) in enumerate(zip(FIRST, (side, pair, cross)))}
    c_ref[...] = jnp.zeros_like(c_ref)
    add_all(cols, half, width, buffers, own_ap, far_ap, swapped, size, cross_ap, c_ref, block)


def far_kernel(cols, half, width, own_ap, far_ap, swapped, cross_ap, far, diag, last, partial, c_ref, block):
    size = far.shape[0]
    buffers = {kind: (ref, last, j * size) for j, (kind, ref) in enumerate(zip(SECOND, (far, diag)))}
    c_ref[...] = partial[...]
    add_all(cols, half, width, buffers, own_ap, far_ap, swapped, size, cross_ap, c_ref, block)


def on_device(rows, cols, prolong, applied, prolong_pattern, applied_pattern):
    depth, width = prolong.shape[0], prolong.shape[1] // TILE
    half = depth // 2
    data = SLOTS * half
    size = data + 2 * META
    vmem = pl.BlockSpec(memory_space=pltpu.VMEM)
    smem = pl.BlockSpec(memory_space=pltpu.SMEM)
    params = pltpu.CompilerParams(vmem_limit_bytes=24 << 20)
    shape = lambda *s: jax.ShapeDtypeStruct(s, prolong.dtype)

    def call(kernel, name, out_shape, *operands, specs=None, weight=0, **more):
        if weight:
            more["cost_estimate"] = pl.CostEstimate(flops=weight * 1_000_000_000, bytes_accessed=weight * 3_000_000, transcendentals=0)
        out_specs = (vmem,) * len(out_shape) if isinstance(out_shape, tuple) else vmem
        return pl.pallas_call(
            kernel, out_shape=out_shape, in_specs=specs or [vmem] * len(operands), out_specs=out_specs,
            compiler_params=params, name=name, **more,
        )(*operands)

    def move(x, pairs):
        return lax.ppermute(x, AXES, pairs)

    def row_pairs(pairs):
        return [(a * cols + c, b * cols + c) for a, b in pairs for c in range(cols)]

    def col_pairs(pairs):
        return [(r * cols + a, r * cols + b) for r in range(rows) for a, b in pairs if 0 <= b < cols]

    partner = row_pairs([(r, r ^ 1) for r in range(rows)])
    opposite = [(r, (r + rows // 2) % rows) for r in range(rows)]

    hbm = pl.BlockSpec(memory_space=pltpu.HBM)
    keep, send, own_ap = call(
        functools.partial(prepare_kernel, cols), "prepare", (shape(data + META, TILE),) * 2 + (shape(*applied.shape),),
        *[pltpu.with_memory_space_constraint(x, pltpu.HBM) for x in (prolong, applied, prolong_pattern.T, applied_pattern.T)],
        specs=[hbm] * 4,
        scratch_shapes=[
            pltpu.VMEM(prolong.shape, prolong.dtype),
            pltpu.VMEM(applied.shape, applied.dtype),
            pltpu.SMEM(prolong_pattern.shape[::-1], jnp.int32),
            pltpu.SMEM(applied_pattern.shape[::-1], jnp.int32),
            pltpu.SemaphoreType.DMA((4,)),
        ],
    )
    got = move(send, partner)
    far_ap = move(own_ap, row_pairs(opposite))
    mine = call(merge_kernel, "merge", shape(size, TILE), keep, got)
    middle = lambda c: 2 <= c < cols - 2
    step = lambda c: c - 2 if (c // 2) % 2 == 0 else c + 2
    cross = move(mine, [
        (r * cols + c, r * cols + step(c) if middle(c) else (r ^ 1) * cols + c) for r in range(rows) for c in range(cols)
    ])
    pair = move(mine, col_pairs([(c, c ^ 2) for c in range(cols)]))
    side = move(mine, col_pairs([(c, c ^ 1) for c in range(cols)]))

    ap_rows = 2 * depth
    if cols == 8:
        far_pairs = [(0, 4), (1, 5), (2, 0), (3, 1), (4, 6), (5, 7), (6, 2), (7, 3)]
    else:
        far_pairs = [(c, (c + cols // 2) % cols) for c in range(cols)]
    far_send = call(functools.partial(far_forward_kernel, cols), "far_forward", shape(size, TILE), mine, cross)
    far = move(far_send, col_pairs(far_pairs))
    diag_send = call(diagonal_forward_kernel, "diagonal_forward", shape(size, TILE), pair, cross)
    diag = move(diag_send, col_pairs([(c, c ^ 1) for c in range(cols)]))
    swap = call(swap_kernel, "swap", shape(len(FIRST) * size + 2 * ap_rows, TILE), side, pair, cross, own_ap, far_ap)
    swapped = move(swap, partner)
    last = move(call(last_swap_kernel, "last_swap", shape(len(SECOND) * size, TILE), far, diag, weight=LAST_WEIGHT), partner)
    beyond = [(r, r + 1 if r % 2 == 1 else r - 1) for r in range(rows)]
    relay = [((r + rows // 2) % rows, t) for r, t in beyond if 0 <= t < rows]
    if all(h ^ 1 == t for h, t in relay):
        cross_ap = swapped
    else:
        first = own_ap[:depth].reshape(depth, 2, TILE).transpose(1, 0, 2).reshape(ap_rows, TILE)
        cross_ap = move(first, row_pairs([(r, t) for r, t in beyond if 0 <= t < rows]))

    result = jax.ShapeDtypeStruct((prolong.shape[1], applied.shape[1]), jnp.float32)
    scratch = dict(scratch_shapes=[pltpu.VMEM((2 * (data + META), TILE), prolong.dtype)])
    partial = call(
        functools.partial(near_kernel, cols, half, width), "near", result,
        own_ap, far_ap, keep, send, side, pair, cross, swapped, cross_ap, **scratch,
    )
    return call(
        functools.partial(far_kernel, cols, half, width), "far", result,
        own_ap, far_ap, swapped, cross_ap, far, diag, last, partial, **scratch,
    )


def solution(mesh):
    in_specs = (P("col", "row"), P("row", "col"), P("col", "row"), P("row", "col"))
    return jax.shard_map(
        functools.partial(on_device, mesh.shape["row"], mesh.shape["col"]),
        mesh=mesh, in_specs=in_specs, out_specs=P("row", "col"), check_vma=False,
    )
```

time: 39.3 us -> 29.5 us (0.75)
  starting transfers between devices: 14.9 us -> 11.2 us
  waiting for transfers between devices: 16.9 us -> 13.5 us
  local copies, waits for them, and re-layouts: 2.5 us -> 0 us
    ppermute x9, starting transfers between devices: 14.9 us -> 11.2 us  [move(): return lax.ppermute(x, AXES, pairs)]
    ppermute x9, waiting for transfers between devices: 16.9 us -> 13.5 us  [move(): return lax.ppermute(x, AXES, pairs)]
    unnamed x8 -> x0, local copies, waits for them, and re-layouts: 2.5 us -> none
    pallas_call x7 -> x8, Pallas kernels: 4.58 us -> 4.59 us  [call(): pl.pallas_call(kernel, out_shape=out_shape, in_specs=specs or [vmem] * le...]
  transfers between devices with their start and end apart: 9 -> 9, of which waited for: 6 -> 5; matrix products, arithmetic and copies ran while one was open for 0% -> 0% of each run, Pallas kernels for 6% -> 6%
where the time goes in v3:
time: 29.5 us; the launch traced here: 29.4 us
  waiting for transfers between devices  13.5 us (46%)
  starting transfers between devices  11.2 us (38%)
  Pallas kernels  4.59 us (16%)
    ppermute x9, waiting for transfers between devices, move(): return lax.ppermute(x, AXES, pairs)  13.5 us
    ppermute x9, starting transfers between devices, move(): return lax.ppermute(x, AXES, pairs)  11.2 us
    pallas_call x8, Pallas kernels, call(): pl.pallas_call(kernel, out_shape=out_shape, in_specs=specs or [vmem] * le...  4.59 us
  transfers between devices with their start and end apart: 9, of which 5 were waited for; matrix products, arithmetic and copies ran while one was open for 0% of the time, Pallas kernels for 6%

profile of v3, /device:TPU:0, one launch (start us, length us, event | category | flops | bytes accessed | tf_op | source)
XLA Modules:
  0.0 29.4 jit_solution(7388042862986026251)
XLA Ops:
  0.0 1.6 %prepare.1 = (bf16[1168,128]{1,0:T(8,128)(2,1)S(1)}, bf16[1168,128]{1,0:T(8,128)(2,1)S(1)}, bf16[1536,256]{1,0:T(8,128)(2,1)S(1)}) custom-call(bf16[768,512]{1,0:T(8,128)(2,1)} %p_hbm.1, bf16[1536,256]{1,0:T(8,128)(2,1)} %ap_hbm.1, s32[4,6]{1,0:T(4,128)} %bitcast.2, s32[2,12]{1,0:T(2,128)} %bitcast.3), custom_call_target="tpu_custom_call" | custom-call | tf_op jit(solution)/shard_map/prepare/pallas_call | solution.py:261
  1.6 0.5 %collective-permute-start.1 = (bf16[1168,128]{1,0:T(8,128)(2,1)S(1)}, bf16[1168,128]{1,0:T(8,128)(2,1)S(1)}, u32[]{:S(2)}, u32[]{:S(2)}) collective-permute-start(bf16[1168,128]{1,0:T(8,128)(2,1)S(1)} %get-tuple-element.10.send), channel_id=1, source_target_pairs={{0,8},{1,9},{2,10},{3,11},{4,12},{5,13},{6,14},{7,15},{8,0},{9,1},... | collective-permute-start | bytes 897032 | tf_op jit(solution)/shard_map/ppermute | solution.py:267
  2.1 2.6 %collective-permute-start = (bf16[1536,256]{1,0:T(8,128)(2,1)S(1)}, bf16[1536,256]{1,0:T(8,128)(2,1)S(1)}, u32[]{:S(2)}, u32[]{:S(2)}) collective-permute-start(bf16[1536,256]{1,0:T(8,128)(2,1)S(1)} %get-tuple-element.8.own_ap), channel_id=1, source_target_pairs={{0,16},{1,17},{2,18},{3,19},{4,20},{5,21},{6,22},{7,23},{8,24},{9,... | collective-permute-start | bytes 2359304 | tf_op jit(solution)/shard_map/ppermute | solution.py:267
  4.7 0.0 collective-permute-done.1.got_ref
  4.7 0.1 merge.1.own
  4.8 0.2 collective-permute-start.4
  5.0 3.0 %collective-permute-start.3 = (bf16[1184,128]{1,0:T(8,128)(2,1)S(1)}, bf16[1184,128]{1,0:T(8,128)(2,1)S(1)}, u32[]{:S(2)}, u32[]{:S(2)}) collective-permute-start(bf16[1184,128]{1,0:T(8,128)(2,1)S(1)} %merge.1.own), channel_id=1, source_target_pairs={{0,2},{1,3},{2,0},{3,1},{4,6},{5,7},{6,4},{7,5},{8,10},{9,11},{10,... | collective-permute-start | bytes 909320 | tf_op jit(solution)/shard_map/ppermute | solution.py:267
  8.0 1.5 %collective-permute-start.2 = (bf16[1184,128]{1,0:T(8,128)(2,1)S(1)}, bf16[1184,128]{1,0:T(8,128)(2,1)S(1)}, u32[]{:S(2)}, u32[]{:S(2)}) collective-permute-start(bf16[1184,128]{1,0:T(8,128)(2,1)S(1)} %merge.1.own), channel_id=1, source_target_pairs={{0,1},{1,0},{2,3},{3,2},{4,5},{5,4},{6,7},{7,6},{8,9},{9,8},{10,11... | collective-permute-start | bytes 909320 | tf_op jit(solution)/shard_map/ppermute | solution.py:267
  9.5 0.0 collective-permute-done.4.cross
  9.5 5.7 %collective-permute-done.3.pair = bf16[1184,128]{1,0:T(8,128)(2,1)S(1)} collective-permute-done((bf16[1184,128]{1,0:T(8,128)(2,1)S(1)}, bf16[1184,128]{1,0:T(8,128)(2,1)S(1)}, u32[]{:S(2)}, u32[]{:S(2)}) %collective-permute-start.3) | collective-permute-done | bytes 303136 | tf_op jit(solution)/shard_map/ppermute | solution.py:267
  15.3 1.6 %collective-permute-start.7 = (bf16[1184,128]{1,0:T(8,128)(2,1)S(1)}, bf16[1184,128]{1,0:T(8,128)(2,1)S(1)}, u32[]{:S(2)}, u32[]{:S(2)}) collective-permute-start(bf16[1184,128]{1,0:T(8,128)(2,1)S(1)} %diagonal_forward.1), channel_id=1, source_target_pairs={{0,1},{1,0},{2,3},{3,2},{4,5},{5,4},{6,7},{7,6},{8,9},{9,8},{10,11... | collective-permute-start | bytes 909320 | tf_op jit(solution)/shard_map/ppermute | solution.py:267
  16.9 1.7 %collective-permute-start.6 = (bf16[1184,128]{1,0:T(8,128)(2,1)S(1)}, bf16[1184,128]{1,0:T(8,128)(2,1)S(1)}, u32[]{:S(2)}, u32[]{:S(2)}) collective-permute-start(bf16[1184,128]{1,0:T(8,128)(2,1)S(1)} %far_forward.1), channel_id=1, source_target_pairs={{0,4},{1,5},{2,0},{3,1},{4,6},{5,7},{6,2},{7,3},{8,12},{9,13},{10,... | collective-permute-start | bytes 909320 | tf_op jit(solution)/shard_map/ppermute | solution.py:267
  18.5 0.0 collective-permute-done.2.side
  18.5 4.3 %collective-permute-done.far_ap = bf16[1536,256]{1,0:T(8,128)(2,1)S(1)} collective-permute-done((bf16[1536,256]{1,0:T(8,128)(2,1)S(1)}, bf16[1536,256]{1,0:T(8,128)(2,1)S(1)}, u32[]{:S(2)}, u32[]{:S(2)}) %collective-permute-start) | collective-permute-done | bytes 786464 | tf_op jit(solution)/shard_map/ppermute | solution.py:267
  22.8 0.2 swap.1
  23.0 0.1 collective-permute-start.5
  23.1 0.7 %collective-permute-done.7.diag = bf16[1184,128]{1,0:T(8,128)(2,1)S(1)} collective-permute-done((bf16[1184,128]{1,0:T(8,128)(2,1)S(1)}, bf16[1184,128]{1,0:T(8,128)(2,1)S(1)}, u32[]{:S(2)}, u32[]{:S(2)}) %collective-permute-start.7) | collective-permute-done | bytes 303136 | tf_op jit(solution)/shard_map/ppermute | solution.py:267
  23.8 1.3 %collective-permute-done.6.far = bf16[1184,128]{1,0:T(8,128)(2,1)S(1)} collective-permute-done((bf16[1184,128]{1,0:T(8,128)(2,1)S(1)}, bf16[1184,128]{1,0:T(8,128)(2,1)S(1)}, u32[]{:S(2)}, u32[]{:S(2)}) %collective-permute-start.6) | collective-permute-done | bytes 303136 | tf_op jit(solution)/shard_map/ppermute | solution.py:267
  25.1 0.1 collective-permute-start.8
  25.2 1.5 %collective-permute-done.5.swapped.cross_ap = bf16[6624,128]{1,0:T(8,128)(2,1)S(1)} collective-permute-done((bf16[6624,128]{1,0:T(8,128)(2,1)S(1)}, bf16[6624,128]{1,0:T(8,128)(2,1)S(1)}, u32[]{:S(2)}, u32[]{:S(2)}) %collective-permute-start.5) | collective-permute-done | bytes 1695776 | tf_op jit(solution)/shard_map/ppermute | solution.py:267
  26.7 1.5 %near.1.partial = f32[512,256]{1,0:T(8,128)S(1)} custom-call(bf16[1536,256]{1,0:T(8,128)(2,1)S(1)} %get-tuple-element.8.own_ap, bf16[1536,256]{1,0:T(8,128)(2,1)S(1)} %collective-permute-done.far_ap, bf16[1168,128]{1,0:T(8,128)(2,1)S(1)} %get-tuple-element.9.keep_ref.keep, bf16[1168,128]{1,0:T(8,128)(2,1)S(1)} %get-tuple-element.10.send, ...), custom_call_target="tpu_custom_call" | custom-call | tf_op jit(solution)/shard_map/near/pallas_call | solution.py:261
  28.1 0.0 collective-permute-done.8.last
  28.1 1.2 %far.1 = f32[512,256]{1,0:T(8,128)} custom-call(bf16[1536,256]{1,0:T(8,128)(2,1)S(1)} %get-tuple-element.8.own_ap, bf16[1536,256]{1,0:T(8,128)(2,1)S(1)} %collective-permute-done.far_ap, bf16[6624,128]{1,0:T(8,128)(2,1)S(1)} %collective-permute-done.5.swapped.cross_ap, bf16[6624,128]{1,0:T(8,128)(2,1)S(1)} %collective-permute-done.5.swapped.cross_ap, ...), custom_call_target="tpu_custom_call" | custom-call | tf_op jit(solution)/shard_map/far/pallas_call | solution.py:261
  (3 shorter events, 0.1 us)
Async XLA Ops:
  1.6 3.1 %collective-permute-start.1 = (bf16[1168,128]{1,0:T(8,128)(2,1)S(1)}, bf16[1168,128]{1,0:T(8,128)(2,1)S(1)}, u32[]{:S(2)}, u32[]{:S(2)}) collective-permute-start(bf16[1168,128]{1,0:T(8,128)(2,1)S(1)} %get-tuple-element.10.send), channel_id=1, source_target_pairs={{0,8},{1,9},{2,10},{3,11},{4,12},{5,13},{6,14},{7,15},{8,0},{9,1},... | collective-permute-start | bytes 897032 | tf_op jit(solution)/shard_map/ppermute | solution.py:267
  2.1 20.7 %collective-permute-start = (bf16[1536,256]{1,0:T(8,128)(2,1)S(1)}, bf16[1536,256]{1,0:T(8,128)(2,1)S(1)}, u32[]{:S(2)}, u32[]{:S(2)}) collective-permute-start(bf16[1536,256]{1,0:T(8,128)(2,1)S(1)} %get-tuple-element.8.own_ap), channel_id=1, source_target_pairs={{0,16},{1,17},{2,18},{3,19},{4,20},{5,21},{6,22},{7,23},{8,24},{9,... | collective-permute-start | bytes 2359304 | tf_op jit(solution)/shard_map/ppermute | solution.py:267
  4.8 4.7 %collective-permute-start.4 = (bf16[1184,128]{1,0:T(8,128)(2,1)S(1)}, bf16[1184,128]{1,0:T(8,128)(2,1)S(1)}, u32[]{:S(2)}, u32[]{:S(2)}) collective-permute-start(bf16[1184,128]{1,0:T(8,128)(2,1)S(1)} %merge.1.own), channel_id=1, source_target_pairs={{0,8},{1,9},{2,4},{3,5},{4,2},{5,3},{6,14},{7,15},{8,0},{9,1},{10,... | collective-permute-start | bytes 909320 | tf_op jit(solution)/shard_map/ppermute | solution.py:267
  5.0 10.2 %collective-permute-start.3 = (bf16[1184,128]{1,0:T(8,128)(2,1)S(1)}, bf16[1184,128]{1,0:T(8,128)(2,1)S(1)}, u32[]{:S(2)}, u32[]{:S(2)}) collective-permute-start(bf16[1184,128]{1,0:T(8,128)(2,1)S(1)} %merge.1.own), channel_id=1, source_target_pairs={{0,2},{1,3},{2,0},{3,1},{4,6},{5,7},{6,4},{7,5},{8,10},{9,11},{10,... | collective-permute-start | bytes 909320 | tf_op jit(solution)/shard_map/ppermute | solution.py:267
  8.0 10.5 %collective-permute-start.2 = (bf16[1184,128]{1,0:T(8,128)(2,1)S(1)}, bf16[1184,128]{1,0:T(8,128)(2,1)S(1)}, u32[]{:S(2)}, u32[]{:S(2)}) collective-permute-start(bf16[1184,128]{1,0:T(8,128)(2,1)S(1)} %merge.1.own), channel_id=1, source_target_pairs={{0,1},{1,0},{2,3},{3,2},{4,5},{5,4},{6,7},{7,6},{8,9},{9,8},{10,11... | collective-permute-start | bytes 909320 | tf_op jit(solution)/shard_map/ppermute | solution.py:267
  15.3 8.5 %collective-permute-start.7 = (bf16[1184,128]{1,0:T(8,128)(2,1)S(1)}, bf16[1184,128]{1,0:T(8,128)(2,1)S(1)}, u32[]{:S(2)}, u32[]{:S(2)}) collective-permute-start(bf16[1184,128]{1,0:T(8,128)(2,1)S(1)} %diagonal_forward.1), channel_id=1, source_target_pairs={{0,1},{1,0},{2,3},{3,2},{4,5},{5,4},{6,7},{7,6},{8,9},{9,8},{10,11... | collective-permute-start | bytes 909320 | tf_op jit(solution)/shard_map/ppermute | solution.py:267
  16.9 8.2 %collective-permute-start.6 = (bf16[1184,128]{1,0:T(8,128)(2,1)S(1)}, bf16[1184,128]{1,0:T(8,128)(2,1)S(1)}, u32[]{:S(2)}, u32[]{:S(2)}) collective-permute-start(bf16[1184,128]{1,0:T(8,128)(2,1)S(1)} %far_forward.1), channel_id=1, source_target_pairs={{0,4},{1,5},{2,0},{3,1},{4,6},{5,7},{6,2},{7,3},{8,12},{9,13},{10,... | collective-permute-start | bytes 909320 | tf_op jit(solution)/shard_map/ppermute | solution.py:267
  23.0 3.7 %collective-permute-start.5 = (bf16[6624,128]{1,0:T(8,128)(2,1)S(1)}, bf16[6624,128]{1,0:T(8,128)(2,1)S(1)}, u32[]{:S(2)}, u32[]{:S(2)}) collective-permute-start(bf16[6624,128]{1,0:T(8,128)(2,1)S(1)} %swap.1), channel_id=1, source_target_pairs={{0,8},{1,9},{2,10},{3,11},{4,12},{5,13},{6,14},{7,15},{8,0},{9,1},... | collective-permute-start | bytes 5087240 | tf_op jit(solution)/shard_map/ppermute | solution.py:267
  25.1 3.0 %collective-permute-start.8 = (bf16[2368,128]{1,0:T(8,128)(2,1)S(1)}, bf16[2368,128]{1,0:T(8,128)(2,1)S(1)}, u32[]{:S(2)}, u32[]{:S(2)}) collective-permute-start(bf16[2368,128]{1,0:T(8,128)(2,1)S(1)} %last_swap.1), channel_id=1, source_target_pairs={{0,8},{1,9},{2,10},{3,11},{4,12},{5,13},{6,14},{7,15},{8,0},{9,1},... | collective-permute-start | bytes 1818632 | tf_op jit(solution)/shard_map/ppermute | solution.py:267

commit v4 on v3

v4 whole, which is shorter than its diff:
```python
import functools

import jax
import jax.numpy as jnp
from jax import lax
from jax.experimental import pallas as pl
from jax.experimental.pallas import tpu as pltpu
from jax.sharding import PartitionSpec as P

TILE = 128
AXES = ("row", "col")
LAST_WEIGHT, FIRST_WEIGHT = 20, 5
SLOTS = 3
META = 16
MAINS, NEARS, FARS = (0, 1), (2, 3), (4, 5)
UNITS = (
    ((0, 0), (0, 1), (0, 2), (1, 0), (1, 1), (1, 2), (1, 3)),
    ((0, 0), (0, 1), (0, 2), (0, 3), (1, 1), (1, 2), (1, 3)),
    ((0, 0), (1, 0), (1, 1)),
    ((0, 2), (0, 3), (1, 3)),
    ((0, 0), (1, 1)),
    ((0, 2), (1, 3)),
)
OWN, SIDE, PAIR, CROSS, FAR, DIAG = range(6)
FIRST, SECOND = (OWN, SIDE, PAIR, CROSS), (FAR, DIAG)


def class_sources(r, cols):
    rem = lambda x: lax.rem(x, cols)
    return (2 * r, 2 * r + 1, 2 * r - 1, 2 * r + 2, rem(2 * r + cols // 2), rem(2 * r + 1 + cols // 2))


def kind_sources(c, cols):
    even, low = c % 2 == 0, (c // 2) % 2 == 0
    near, past = jnp.where(even, c + 1, c - 1), jnp.where(even, c - 1, c + 1)
    pair, across = jnp.where(low, c + 2, c - 2), jnp.where(low, c - 2, c + 2)
    return {OWN: c, SIDE: near, PAIR: pair, CROSS: across, FAR: lax.rem(c + cols // 2, cols), DIAG: past}


def slot_of(name, i, odd, width):
    return 2 if name in FARS else (i + (width if odd else 0)) % SLOTS


def prepare_kernel(cols, p_hbm, ap_hbm, p_pattern_hbm, ap_pattern_hbm, keep_ref, send_ref, first_ref, second_ref, p_ref, ap_ref, p_pattern, ap_pattern, sems):
    copies = [
        pltpu.make_async_copy(source, target, sems.at[i])
        for i, (source, target) in enumerate(
            ((p_pattern_hbm, p_pattern), (p_hbm, p_ref), (ap_pattern_hbm, ap_pattern), (ap_hbm, ap_ref))
        )
    ]
    for copy in copies:
        copy.start()
    r, c = lax.axis_index("row"), lax.axis_index("col")
    tiles = p_ref.shape[0] // TILE // 2
    half = tiles * TILE
    width = p_ref.shape[1] // TILE
    sources = class_sources(r, cols)
    zeros = jnp.zeros((TILE, TILE), p_ref.dtype)
    line = lax.broadcasted_iota(jnp.int32, (META, TILE), 0)

    def pack(name, odd):
        for out_ref, m in ((keep_ref, int(odd)), (send_ref, 1 - int(odd))):
            for s in range(SLOTS):
                found = [i for mm, i in UNITS[name] if mm == m and slot_of(name, i, odd, width) == s]
                for a in range(tiles):
                    value, row = zeros, m * tiles + a
                    for i in found:
                        tile = p_ref[pl.ds(row * TILE, TILE), pl.ds(i * TILE, TILE)]
                        value = jnp.where(p_pattern[i, row] > 0, tile, value)
                    out_ref[pl.ds(s * half + a * TILE, TILE), :] = value

    def note(odd):
        for out_ref, m in ((keep_ref, int(odd)), (send_ref, 1 - int(odd))):
            value = jnp.zeros((META, TILE), jnp.float32)
            for a in range(tiles):
                for i in range(width):
                    value = jnp.where(line == a * width + i, p_pattern[i, m * tiles + a].astype(jnp.float32), value)
            out_ref[pl.ds(SLOTS * half, META), :] = value.astype(out_ref.dtype)

    copies[0].wait()
    copies[1].wait()
    for odd in (False, True):
        parity = (r % 2 == 1) == odd

        @pl.when(parity)
        def _(odd=odd):
            note(odd)

        for name in range(len(UNITS)):
            @pl.when(parity & (c == sources[name]))
            def _(name=name, odd=odd):
                pack(name, odd)

    @pl.when(functools.reduce(jnp.logical_and, [c != s for s in sources]))
    def _():
        for out in (keep_ref, send_ref):
            out[pl.ds(0, SLOTS * half), :] = jnp.zeros((SLOTS * half, TILE), p_ref.dtype)

    copies[2].wait()
    copies[3].wait()
    count = ap_ref.shape[0] // TILE
    shift = jnp.where(r % 2 == 1, count // 2, 0)
    for a in range(count):
        row = lax.rem(a + shift, count)
        rows = pl.ds(pl.multiple_of(row * TILE, TILE), TILE)
        for b in range(ap_ref.shape[1] // TILE):
            tile = ap_ref[rows, pl.ds(b * TILE, TILE)]
            out_ref = first_ref if 2 * a < count else second_ref
            out_ref[pl.ds(a % (count // 2) * TILE, TILE), pl.ds(b * TILE, TILE)] = jnp.where(ap_pattern[b, row] > 0, tile, zeros)


def merge_kernel(keep_ref, got_ref, half_ref):
    odd = lax.axis_index("row") % 2 == 1
    size = keep_ref.shape[0] - META
    half_ref[pl.ds(0, size), :] = keep_ref[pl.ds(0, size), :] + got_ref[pl.ds(0, size), :]
    mine, theirs = keep_ref[pl.ds(size, META), :], got_ref[pl.ds(size, META), :]
    half_ref[pl.ds(size, META), :] = jnp.where(odd, theirs, mine)
    half_ref[pl.ds(size + META, META), :] = jnp.where(odd, mine, theirs)


def far_forward_kernel(cols, own, cross, ordered_after, out_ref):
    c = lax.axis_index("col")
    inner = (cols == 8) & (c >= 2) & (c < 6)

    @pl.when(inner)
    def _():
        out_ref[...] = cross[...]

    @pl.when(jnp.logical_not(inner))
    def _():
        out_ref[...] = own[...]


def diagonal_forward_kernel(pair, cross, ordered_after, out_ref):
    c = lax.axis_index("col")
    by_pair = (c % 2 == 0) == ((c // 2) % 2 == 0)

    @pl.when(by_pair)
    def _():
        out_ref[...] = pair[...]

    @pl.when(jnp.logical_not(by_pair))
    def _():
        out_ref[...] = cross[...]


def swap_kernel(own, side, pair, cross, own_second, far_first, out_ref):
    size = side.shape[0]
    for j, buffer in enumerate((own, side, pair, cross)):
        for a in range(0, size - 2 * META, TILE):
            out_ref[pl.ds(j * size + a, TILE), :] = buffer[pl.ds(a, TILE), :].T
        out_ref[pl.ds((j + 1) * size - 2 * META, 2 * META), :] = buffer[pl.ds(size - 2 * META, 2 * META), :]
    start = len(FIRST) * size
    for ap in (own_second, far_first):
        for b in range(ap.shape[1] // TILE):
            out_ref[pl.ds(start, ap.shape[0]), :] = ap[:, b * TILE : (b + 1) * TILE]
            start += ap.shape[0]


def settle_kernel(ap_ref, ordered_after, out_ref):
    out_ref[...] = ap_ref[...]


def last_swap_kernel(far, diag, ordered_after, out_ref):
    size = far.shape[0]
    for j, buffer in enumerate((far, diag)):
        out_ref[pl.ds(j * size, size), :] = buffer[...]


def add_product(c_ref, ref, base, name, m, odd, half, width, ap, transposed):
    note = base + SLOTS * half + (META if odd else 0)
    pattern = ref[pl.ds(pl.multiple_of(note, META), META), :].astype(jnp.float32)
    found = [i for mm, i in UNITS[name] if mm == m]
    columns = []
    for i in found:
        tiles = []
        for a in range(half // TILE):
            k = a * width + i
            weight = jnp.broadcast_to(pattern[k : k + 1, :], (TILE, TILE)).astype(ref.dtype)
            first = base + slot_of(name, i, odd, width) * half + a * TILE
            tiles.append(ref[pl.ds(pl.multiple_of(first, META), TILE), :] * weight)
        columns.append(jnp.concatenate(tiles, axis=int(transposed)))
    lhs = jnp.concatenate(columns, axis=1 - int(transposed))
    product = lax.dot_general(lhs, ap, (((int(transposed),), (0,)), ((), ())), preferred_element_type=jnp.float32)
    c_ref[pl.ds(found[0] * TILE, len(found) * TILE), :] += product


def present(cols, name, kind, valid=True):
    r, c = lax.axis_index("row"), lax.axis_index("col")
    source = class_sources(r, cols)[name]
    return valid & (source >= 0) & (source < cols) & (kind_sources(c, cols)[kind] == source)


def read_applied(name, m, odd, half, size, own, far, swapped, cross_ap):
    depth, rows = 2 * half, pl.ds(m * half, half)
    if name in MAINS:
        return own[int(odd == (name == 0))][rows, :]
    if name in FARS:
        return far[int(odd == (name == 4))][rows, :]
    if odd == (name == 2):
        ref, start = swapped, len(FIRST) * size
    else:
        ref, start = cross_ap, cross_ap.shape[0] - 2 * depth
    return jnp.concatenate([ref[pl.ds(start + b * depth + m * half, half), :] for b in range(2)], axis=1)


def add_blocks(cols, half, width, c_ref, read, kinds, size, mine, theirs, transposed):
    row_odd = lax.axis_index("row") % 2 == 1
    for odd in (False, True):
        @pl.when(row_odd == odd)
        def _(odd=odd):
            for name in range(len(UNITS)):
                here = [present(cols, name, kind) for kind in kinds]
                base = sum(jnp.where(flag, j * size, 0) for j, flag in enumerate(here))

                @pl.when(functools.reduce(jnp.logical_or, here))
                def _(name=name, base=base):
                    for m in sorted({m for m, _ in UNITS[name]}):
                        ref = mine if odd == (m == 1) else theirs
                        if ref is not None:
                            add_product(c_ref, ref, base, name, m, odd, half, width, read(name, m, odd), transposed)


def near_kernel(cols, half, width, own_first, own_second, far_first, far_second, swapped, cross_ap, swap, last_swap, c_ref):
    size = last_swap.shape[0] // len(SECOND)
    read = lambda name, m, odd: read_applied(
        name, m, odd, half, size, (own_first, own_second), (far_first, far_second), swapped, cross_ap
    )
    c_ref[...] = jnp.zeros_like(c_ref)
    add_blocks(cols, half, width, c_ref, read, FIRST, size, swap, swapped, True)
    add_blocks(cols, half, width, c_ref, read, SECOND, size, last_swap, None, False)


def last_kernel(cols, half, width, own_first, own_second, far_first, far_second, swapped, cross_ap, last, partial, c_ref):
    size = last.shape[0] // len(SECOND)
    read = lambda name, m, odd: read_applied(
        name, m, odd, half, size, (own_first, own_second), (far_first, far_second), swapped, cross_ap
    )
    c_ref[...] = partial[...]
    add_blocks(cols, half, width, c_ref, read, SECOND, size, None, last, False)


def on_device(rows, cols, prolong, applied, prolong_pattern, applied_pattern):
    depth, width = prolong.shape[0], prolong.shape[1] // TILE
    half = depth // 2
    data = SLOTS * half
    size = data + 2 * META
    vmem = pl.BlockSpec(memory_space=pltpu.VMEM)
    smem = pl.BlockSpec(memory_space=pltpu.SMEM)
    params = pltpu.CompilerParams(vmem_limit_bytes=24 << 20)
    shape = lambda *s: jax.ShapeDtypeStruct(s, prolong.dtype)

    def call(kernel, name, out_shape, *operands, specs=None, weight=0, **more):
        if weight:
            more["cost_estimate"] = pl.CostEstimate(flops=weight * 1_000_000_000, bytes_accessed=weight * 3_000_000, transcendentals=0)
        out_specs = (vmem,) * len(out_shape) if isinstance(out_shape, tuple) else vmem
        return pl.pallas_call(
            kernel, out_shape=out_shape, in_specs=specs or [vmem] * len(operands), out_specs=out_specs,
            compiler_params=params, name=name, **more,
        )(*operands)

    def move(x, pairs):
        return lax.ppermute(x, AXES, pairs)

    def row_pairs(pairs):
        return [(a * cols + c, b * cols + c) for a, b in pairs for c in range(cols)]

    def col_pairs(pairs):
        return [(r * cols + a, r * cols + b) for r in range(rows) for a, b in pairs if 0 <= b < cols]

    partner = row_pairs([(r, r ^ 1) for r in range(rows)])
    opposite = [(r, (r + rows // 2) % rows) for r in range(rows)]

    hbm = pl.BlockSpec(memory_space=pltpu.HBM)
    half_ap = shape(depth, applied.shape[1])
    keep, send, own_first, own_second = call(
        functools.partial(prepare_kernel, cols), "prepare", (shape(data + META, TILE),) * 2 + (half_ap,) * 2,
        *[pltpu.with_memory_space_constraint(x, pltpu.HBM) for x in (prolong, applied, prolong_pattern.T, applied_pattern.T)],
        specs=[hbm] * 4,
        scratch_shapes=[
            pltpu.VMEM(prolong.shape, prolong.dtype),
            pltpu.VMEM(applied.shape, applied.dtype),
            pltpu.SMEM(prolong_pattern.shape[::-1], jnp.int32),
            pltpu.SMEM(applied_pattern.shape[::-1], jnp.int32),
            pltpu.SemaphoreType.DMA((4,)),
        ],
    )
    got = move(send, partner)
    far_first, far_second = move(own_first, row_pairs(opposite)), move(own_second, row_pairs(opposite))
    mine = call(merge_kernel, "merge", shape(size, TILE), keep, got)
    middle = lambda c: 2 <= c < cols - 2
    step = lambda c: c - 2 if (c // 2) % 2 == 0 else c + 2
    cross = move(mine, [
        (r * cols + c, r * cols + step(c) if middle(c) else (r ^ 1) * cols + c) for r in range(rows) for c in range(cols)
    ])
    pair = move(mine, col_pairs([(c, c ^ 2) for c in range(cols)]))
    side = move(mine, col_pairs([(c, c ^ 1) for c in range(cols)]))

    if cols == 8:
        far_pairs = [(0, 4), (1, 5), (2, 0), (3, 1), (4, 6), (5, 7), (6, 2), (7, 3)]
    else:
        far_pairs = [(c, (c + cols // 2) % cols) for c in range(cols)]
    diag_send = call(diagonal_forward_kernel, "diagonal_forward", shape(size, TILE), pair, cross, pair)
    diag = move(diag_send, col_pairs([(c, c ^ 1) for c in range(cols)]))
    far_send = call(
        functools.partial(far_forward_kernel, cols), "far_forward", shape(size, TILE), mine, cross, cross
    )
    far = move(far_send, col_pairs(far_pairs))
    far_first = call(settle_kernel, "settle_first", half_ap, far_first, mine, weight=FIRST_WEIGHT)
    swap = call(
        swap_kernel, "swap", shape(len(FIRST) * size + 4 * depth, TILE), mine, side, pair, cross, own_second, far_first
    )
    swapped = move(swap, partner)
    far_second = call(settle_kernel, "settle", half_ap, far_second, swap)
    last_swap = call(last_swap_kernel, "last_swap", shape(len(SECOND) * size, TILE), far, diag, far_second, weight=LAST_WEIGHT)
    last = move(last_swap, partner)
    beyond = [(r, r + 1 if r % 2 == 1 else r - 1) for r in range(rows)]
    relay = [((r + rows // 2) % rows, t) for r, t in beyond if 0 <= t < rows]
    if all(h ^ 1 == t for h, t in relay):
        cross_ap = swapped
    else:
        first = own_first.reshape(depth, 2, TILE).transpose(1, 0, 2).reshape(2 * depth, TILE)
        cross_ap = move(first, row_pairs([(r, t) for r, t in beyond if 0 <= t < rows]))

    result = jax.ShapeDtypeStruct((prolong.shape[1], applied.shape[1]), jnp.float32)
    sizes = (cols, half, width)
    aps = (own_first, own_second, far_first, far_second, swapped, cross_ap)
    partial = call(
        functools.partial(near_kernel, *sizes), "near", result, *aps, swap, last_swap,
    )
    return call(functools.partial(last_kernel, *sizes), "last", result, *aps, last, partial)


def solution(mesh):
    in_specs = (P("col", "row"), P("row", "col"), P("col", "row"), P("row", "col"))
    return jax.shard_map(
        functools.partial(on_device, mesh.shape["row"], mesh.shape["col"]),
        mesh=mesh, in_specs=in_specs, out_specs=P("row", "col"), check_vma=False,
    )
```

time: 29.5 us -> 28.5 us (0.966)
  waiting for transfers between devices: 13.5 us -> 10.7 us
  starting transfers between devices: 11.2 us -> 12.7 us
    ppermute x9 -> x10, waiting for transfers between devices: 13.5 us -> 10.7 us  [move(): return lax.ppermute(x, AXES, pairs)]
    ppermute x9 -> x10, starting transfers between devices: 11.2 us -> 12.7 us  [move(): return lax.ppermute(x, AXES, pairs)]
    pallas_call x8 -> x10, Pallas kernels: 4.59 us -> 4.85 us  [call(): pl.pallas_call(kernel, out_shape=out_shape, in_specs=specs or [vmem] * le...]
  transfers between devices with their start and end apart: 9 -> 10, of which waited for: 5 -> 5; matrix products, arithmetic and copies ran while one was open for 0% -> 0% of each run, Pallas kernels for 6% -> 7%
where the time goes in v4:
time: 28.5 us; the launch traced here: 28.3 us
  starting transfers between devices  12.7 us (45%)
  waiting for transfers between devices  10.7 us (38%)
  Pallas kernels  4.85 us (17%)
    ppermute x10, starting transfers between devices, move(): return lax.ppermute(x, AXES, pairs)  12.7 us
    ppermute x10, waiting for transfers between devices, move(): return lax.ppermute(x, AXES, pairs)  10.7 us
    pallas_call x10, Pallas kernels, call(): pl.pallas_call(kernel, out_shape=out_shape, in_specs=specs or [vmem] * le...  4.85 us
  transfers between devices with their start and end apart: 10, of which 5 were waited for; matrix products, arithmetic and copies ran while one was open for 0% of the time, Pallas kernels for 7%

profile of v4, /device:TPU:0, one launch (start us, length us, event | category | flops | bytes accessed | tf_op | source)
XLA Modules:
  0.0 28.3 jit_solution(1913653942602188818)
XLA Ops:
  0.0 1.6 %prepare.1 = (bf16[1168,128]{1,0:T(8,128)(2,1)S(1)}, bf16[1168,128]{1,0:T(8,128)(2,1)S(1)}, bf16[768,256]{1,0:T(8,128)(2,1)S(1)}, bf16[768,256]{1,0:T(8,128)(2,1)S(1)}) custom-call(bf16[768,512]{1,0:T(8,128)(2,1)} %p_hbm.1, bf16[1536,256]{1,0:T(8,128)(2,1)} %ap_hbm.1, s32[4,6]{1,0:T(4,128)} %bitcast.2, s32[2,12]{1,0:T(2,128)} %bitcast.3), custom_call_target="tpu_custom_call" | custom-call | tf_op jit(solution)/shard_map/prepare/pallas_call | solution.py:257
  1.6 0.5 %collective-permute-start.1 = (bf16[1168,128]{1,0:T(8,128)(2,1)S(1)}, bf16[1168,128]{1,0:T(8,128)(2,1)S(1)}, u32[]{:S(2)}, u32[]{:S(2)}) collective-permute-start(bf16[1168,128]{1,0:T(8,128)(2,1)S(1)} %get-tuple-element.12), channel_id=1, source_target_pairs={{0,8},{1,9},{2,10},{3,11},{4,12},{5,13},{6,14},{7,15},{8,0},{9,1},... | collective-permute-start | bytes 897032 | tf_op jit(solution)/shard_map/ppermute | solution.py:263
  2.1 2.6 %collective-permute-start = (bf16[768,256]{1,0:T(8,128)(2,1)S(1)}, bf16[768,256]{1,0:T(8,128)(2,1)S(1)}, u32[]{:S(2)}, u32[]{:S(2)}) collective-permute-start(bf16[768,256]{1,0:T(8,128)(2,1)S(1)} %get-tuple-element.9.own_first), channel_id=1, source_target_pairs={{0,16},{1,17},{2,18},{3,19},{4,20},{5,21},{6,22},{7,23},{8,24},{9,... | collective-permute-start | bytes 1179656 | tf_op jit(solution)/shard_map/ppermute | solution.py:263
  4.7 0.0 collective-permute-done.1.got_ref
  4.7 0.1 merge.1.ordered_after.own
  4.8 0.2 collective-permute-start.5
  5.0 3.0 %collective-permute-start.4 = (bf16[1184,128]{1,0:T(8,128)(2,1)S(1)}, bf16[1184,128]{1,0:T(8,128)(2,1)S(1)}, u32[]{:S(2)}, u32[]{:S(2)}) collective-permute-start(bf16[1184,128]{1,0:T(8,128)(2,1)S(1)} %merge.1.ordered_after.own), channel_id=1, source_target_pairs={{0,2},{1,3},{2,0},{3,1},{4,6},{5,7},{6,4},{7,5},{8,10},{9,11},{10,... | collective-permute-start | bytes 909320 | tf_op jit(solution)/shard_map/ppermute | solution.py:263
  8.0 1.5 %collective-permute-start.2 = (bf16[768,256]{1,0:T(8,128)(2,1)S(1)}, bf16[768,256]{1,0:T(8,128)(2,1)S(1)}, u32[]{:S(2)}, u32[]{:S(2)}) collective-permute-start(bf16[768,256]{1,0:T(8,128)(2,1)S(1)} %get-tuple-element.10.own_second), channel_id=1, source_target_pairs={{0,16},{1,17},{2,18},{3,19},{4,20},{5,21},{6,22},{7,23},{8,24},{9,... | collective-permute-start | bytes 1179656 | tf_op jit(solution)/shard_map/ppermute | solution.py:263
  9.5 1.5 %collective-permute-start.3 = (bf16[1184,128]{1,0:T(8,128)(2,1)S(1)}, bf16[1184,128]{1,0:T(8,128)(2,1)S(1)}, u32[]{:S(2)}, u32[]{:S(2)}) collective-permute-start(bf16[1184,128]{1,0:T(8,128)(2,1)S(1)} %merge.1.ordered_after.own), channel_id=1, source_target_pairs={{0,1},{1,0},{2,3},{3,2},{4,5},{5,4},{6,7},{7,6},{8,9},{9,8},{10,11... | collective-permute-start | bytes 909320 | tf_op jit(solution)/shard_map/ppermute | solution.py:263
  11.0 0.0 collective-permute-done.5.cross.ordered_after
  11.0 4.2 %collective-permute-done.4.pair.ordered_after = bf16[1184,128]{1,0:T(8,128)(2,1)S(1)} collective-permute-done((bf16[1184,128]{1,0:T(8,128)(2,1)S(1)}, bf16[1184,128]{1,0:T(8,128)(2,1)S(1)}, u32[]{:S(2)}, u32[]{:S(2)}) %collective-permute-start.4) | collective-permute-done | bytes 303136 | tf_op jit(solution)/shard_map/ppermute | solution.py:263
  15.3 1.6 %collective-permute-start.8 = (bf16[1184,128]{1,0:T(8,128)(2,1)S(1)}, bf16[1184,128]{1,0:T(8,128)(2,1)S(1)}, u32[]{:S(2)}, u32[]{:S(2)}) collective-permute-start(bf16[1184,128]{1,0:T(8,128)(2,1)S(1)} %diagonal_forward.1), channel_id=1, source_target_pairs={{0,1},{1,0},{2,3},{3,2},{4,5},{5,4},{6,7},{7,6},{8,9},{9,8},{10,11... | collective-permute-start | bytes 909320 | tf_op jit(solution)/shard_map/ppermute | solution.py:263
  16.9 1.7 %collective-permute-start.7 = (bf16[1184,128]{1,0:T(8,128)(2,1)S(1)}, bf16[1184,128]{1,0:T(8,128)(2,1)S(1)}, u32[]{:S(2)}, u32[]{:S(2)}) collective-permute-start(bf16[1184,128]{1,0:T(8,128)(2,1)S(1)} %far_forward.1), channel_id=1, source_target_pairs={{0,4},{1,5},{2,0},{3,1},{4,6},{5,7},{6,2},{7,3},{8,12},{9,13},{10,... | collective-permute-start | bytes 909320 | tf_op jit(solution)/shard_map/ppermute | solution.py:263
  18.5 0.0 collective-permute-done.ap_ref
  18.6 0.0 collective-permute-done.3.side
  18.6 0.4 %swap.1.ordered_after = bf16[7808,128]{1,0:T(8,128)(2,1)S(1)} custom-call(bf16[1184,128]{1,0:T(8,128)(2,1)S(1)} %merge.1.ordered_after.own, bf16[1184,128]{1,0:T(8,128)(2,1)S(1)} %collective-permute-done.3.side, bf16[1184,128]{1,0:T(8,128)(2,1)S(1)} %collective-permute-done.4.pair.ordered_after, ...), custom_call_target="tpu_custom_call" | custom-call | tf_op jit(solution)/shard_map/swap/pallas_call | solution.py:257
  19.0 0.1 collective-permute-start.6
  19.1 3.7 %collective-permute-done.2.ap_ref = bf16[768,256]{1,0:T(8,128)(2,1)S(1)} collective-permute-done((bf16[768,256]{1,0:T(8,128)(2,1)S(1)}, bf16[768,256]{1,0:T(8,128)(2,1)S(1)}, u32[]{:S(2)}, u32[]{:S(2)}) %collective-permute-start.2) | collective-permute-done | bytes 393248 | tf_op jit(solution)/shard_map/ppermute | solution.py:263
  22.9 1.5 %collective-permute-done.8.diag = bf16[1184,128]{1,0:T(8,128)(2,1)S(1)} collective-permute-done((bf16[1184,128]{1,0:T(8,128)(2,1)S(1)}, bf16[1184,128]{1,0:T(8,128)(2,1)S(1)}, u32[]{:S(2)}, u32[]{:S(2)}) %collective-permute-start.8) | collective-permute-done | bytes 303136 | tf_op jit(solution)/shard_map/ppermute | solution.py:263
  24.4 0.7 %collective-permute-done.7.far = bf16[1184,128]{1,0:T(8,128)(2,1)S(1)} collective-permute-done((bf16[1184,128]{1,0:T(8,128)(2,1)S(1)}, bf16[1184,128]{1,0:T(8,128)(2,1)S(1)}, u32[]{:S(2)}, u32[]{:S(2)}) %collective-permute-start.7) | collective-permute-done | bytes 303136 | tf_op jit(solution)/shard_map/ppermute | solution.py:263
  25.1 0.1 collective-permute-start.9
  25.2 1.5 %near.1.partial = f32[512,256]{1,0:T(8,128)S(1)} custom-call(bf16[768,256]{1,0:T(8,128)(2,1)S(1)} %get-tuple-element.9.own_first, bf16[768,256]{1,0:T(8,128)(2,1)S(1)} %get-tuple-element.10.own_second, bf16[768,256]{1,0:T(8,128)(2,1)S(1)} %settle_first.1.far_first, bf16[768,256]{1,0:T(8,128)(2,1)S(1)} %settle.1.ordered_after.far_second, ...), custom_call_target="tpu_custom_call" | custom-call | tf_op jit(solution)/shard_map/near/pallas_call | solution.py:257
  26.7 0.5 %collective-permute-done.9.last = bf16[2368,128]{1,0:T(8,128)(2,1)S(1)} collective-permute-done((bf16[2368,128]{1,0:T(8,128)(2,1)S(1)}, bf16[2368,128]{1,0:T(8,128)(2,1)S(1)}, u32[]{:S(2)}, u32[]{:S(2)}) %collective-permute-start.9) | collective-permute-done | bytes 606240 | tf_op jit(solution)/shard_map/ppermute | solution.py:263
  27.2 1.1 %last.1 = f32[512,256]{1,0:T(8,128)} custom-call(bf16[768,256]{1,0:T(8,128)(2,1)S(1)} %get-tuple-element.9.own_first, bf16[768,256]{1,0:T(8,128)(2,1)S(1)} %get-tuple-element.10.own_second, bf16[768,256]{1,0:T(8,128)(2,1)S(1)} %settle_first.1.far_first, bf16[768,256]{1,0:T(8,128)(2,1)S(1)} %settle.1.ordered_after.far_second, ...), custom_call_target="tpu_custom_call" | custom-call | tf_op jit(solution)/shard_map/last/pallas_call | solution.py:257
  (6 shorter events, 0.1 us)
Async XLA Ops:
  1.6 3.1 %collective-permute-start.1 = (bf16[1168,128]{1,0:T(8,128)(2,1)S(1)}, bf16[1168,128]{1,0:T(8,128)(2,1)S(1)}, u32[]{:S(2)}, u32[]{:S(2)}) collective-permute-start(bf16[1168,128]{1,0:T(8,128)(2,1)S(1)} %get-tuple-element.12), channel_id=1, source_target_pairs={{0,8},{1,9},{2,10},{3,11},{4,12},{5,13},{6,14},{7,15},{8,0},{9,1},... | collective-permute-start | bytes 897032 | tf_op jit(solution)/shard_map/ppermute | solution.py:263
  2.1 16.4 %collective-permute-start = (bf16[768,256]{1,0:T(8,128)(2,1)S(1)}, bf16[768,256]{1,0:T(8,128)(2,1)S(1)}, u32[]{:S(2)}, u32[]{:S(2)}) collective-permute-start(bf16[768,256]{1,0:T(8,128)(2,1)S(1)} %get-tuple-element.9.own_first), channel_id=1, source_target_pairs={{0,16},{1,17},{2,18},{3,19},{4,20},{5,21},{6,22},{7,23},{8,24},{9,... | collective-permute-start | bytes 1179656 | tf_op jit(solution)/shard_map/ppermute | solution.py:263
  4.8 6.2 %collective-permute-start.5 = (bf16[1184,128]{1,0:T(8,128)(2,1)S(1)}, bf16[1184,128]{1,0:T(8,128)(2,1)S(1)}, u32[]{:S(2)}, u32[]{:S(2)}) collective-permute-start(bf16[1184,128]{1,0:T(8,128)(2,1)S(1)} %merge.1.ordered_after.own), channel_id=1, source_target_pairs={{0,8},{1,9},{2,4},{3,5},{4,2},{5,3},{6,14},{7,15},{8,0},{9,1},{10,... | collective-permute-start | bytes 909320 | tf_op jit(solution)/shard_map/ppermute | solution.py:263
  5.0 10.2 %collective-permute-start.4 = (bf16[1184,128]{1,0:T(8,128)(2,1)S(1)}, bf16[1184,128]{1,0:T(8,128)(2,1)S(1)}, u32[]{:S(2)}, u32[]{:S(2)}) collective-permute-start(bf16[1184,128]{1,0:T(8,128)(2,1)S(1)} %merge.1.ordered_after.own), channel_id=1, source_target_pairs={{0,2},{1,3},{2,0},{3,1},{4,6},{5,7},{6,4},{7,5},{8,10},{9,11},{10,... | collective-permute-start | bytes 909320 | tf_op jit(solution)/shard_map/ppermute | solution.py:263
  8.0 14.8 %collective-permute-start.2 = (bf16[768,256]{1,0:T(8,128)(2,1)S(1)}, bf16[768,256]{1,0:T(8,128)(2,1)S(1)}, u32[]{:S(2)}, u32[]{:S(2)}) collective-permute-start(bf16[768,256]{1,0:T(8,128)(2,1)S(1)} %get-tuple-element.10.own_second), channel_id=1, source_target_pairs={{0,16},{1,17},{2,18},{3,19},{4,20},{5,21},{6,22},{7,23},{8,24},{9,... | collective-permute-start | bytes 1179656 | tf_op jit(solution)/shard_map/ppermute | solution.py:263
  9.5 9.0 %collective-permute-start.3 = (bf16[1184,128]{1,0:T(8,128)(2,1)S(1)}, bf16[1184,128]{1,0:T(8,128)(2,1)S(1)}, u32[]{:S(2)}, u32[]{:S(2)}) collective-permute-start(bf16[1184,128]{1,0:T(8,128)(2,1)S(1)} %merge.1.ordered_after.own), channel_id=1, source_target_pairs={{0,1},{1,0},{2,3},{3,2},{4,5},{5,4},{6,7},{7,6},{8,9},{9,8},{10,11... | collective-permute-start | bytes 909320 | tf_op jit(solution)/shard_map/ppermute | solution.py:263
  15.3 9.1 %collective-permute-start.8 = (bf16[1184,128]{1,0:T(8,128)(2,1)S(1)}, bf16[1184,128]{1,0:T(8,128)(2,1)S(1)}, u32[]{:S(2)}, u32[]{:S(2)}) collective-permute-start(bf16[1184,128]{1,0:T(8,128)(2,1)S(1)} %diagonal_forward.1), channel_id=1, source_target_pairs={{0,1},{1,0},{2,3},{3,2},{4,5},{5,4},{6,7},{7,6},{8,9},{9,8},{10,11... | collective-permute-start | bytes 909320 | tf_op jit(solution)/shard_map/ppermute | solution.py:263
  16.9 8.2 %collective-permute-start.7 = (bf16[1184,128]{1,0:T(8,128)(2,1)S(1)}, bf16[1184,128]{1,0:T(8,128)(2,1)S(1)}, u32[]{:S(2)}, u32[]{:S(2)}) collective-permute-start(bf16[1184,128]{1,0:T(8,128)(2,1)S(1)} %far_forward.1), channel_id=1, source_target_pairs={{0,4},{1,5},{2,0},{3,1},{4,6},{5,7},{6,2},{7,3},{8,12},{9,13},{10,... | collective-permute-start | bytes 909320 | tf_op jit(solution)/shard_map/ppermute | solution.py:263
  19.0 6.2 %collective-permute-start.6 = (bf16[7808,128]{1,0:T(8,128)(2,1)S(1)}, bf16[7808,128]{1,0:T(8,128)(2,1)S(1)}, u32[]{:S(2)}, u32[]{:S(2)}) collective-permute-start(bf16[7808,128]{1,0:T(8,128)(2,1)S(1)} %swap.1.ordered_after), channel_id=1, source_target_pairs={{0,8},{1,9},{2,10},{3,11},{4,12},{5,13},{6,14},{7,15},{8,0},{9,1},... | collective-permute-start | bytes 5996552 | tf_op jit(solution)/shard_map/ppermute | solution.py:263
  25.1 2.1 %collective-permute-start.9 = (bf16[2368,128]{1,0:T(8,128)(2,1)S(1)}, bf16[2368,128]{1,0:T(8,128)(2,1)S(1)}, u32[]{:S(2)}, u32[]{:S(2)}) collective-permute-start(bf16[2368,128]{1,0:T(8,128)(2,1)S(1)} %last_swap.1), channel_id=1, source_target_pairs={{0,8},{1,9},{2,10},{3,11},{4,12},{5,13},{6,14},{7,15},{8,0},{9,1},... | collective-permute-start | bytes 1818632 | tf_op jit(solution)/shard_map/ppermute | solution.py:263

commit v5 on v4

--- a/solution.py
+++ b/solution.py
@@ -157,32 +157,25 @@
             start += ap.shape[0]
 
 
-def settle_kernel(ap_ref, ordered_after, out_ref):
-    out_ref[...] = ap_ref[...]
-
-
-def last_swap_kernel(far, diag, ordered_after, out_ref):
-    size = far.shape[0]
-    for j, buffer in enumerate((far, diag)):
-        out_ref[pl.ds(j * size, size), :] = buffer[...]
-
-
-def add_product(c_ref, ref, base, name, m, odd, half, width, ap, transposed):
+def pass_kernel(ref, ordered_after, out_ref):
+    out_ref[...] = ref[...]
+
+
+def masked_product(ref, base, flag, odd, slots, half, width, ap, transposed):
     note = base + SLOTS * half + (META if odd else 0)
     pattern = ref[pl.ds(pl.multiple_of(note, META), META), :].astype(jnp.float32)
-    found = [i for mm, i in UNITS[name] if mm == m]
+    pattern = pattern * jnp.where(flag, 1.0, 0.0)
     columns = []
-    for i in found:
+    for i, slot in slots.items():
         tiles = []
         for a in range(half // TILE):
             k = a * width + i
             weight = jnp.broadcast_to(pattern[k : k + 1, :], (TILE, TILE)).astype(ref.dtype)
-            first = base + slot_of(name, i, odd, width) * half + a * TILE
-            tiles.append(ref[pl.ds(pl.multiple_of(first, META), TILE), :] * weight)
+            tiles.append(ref[pl.ds(pl.multiple_of(base + slot + a * TILE, META), TILE), :] * weight)
         columns.append(jnp.concatenate(tiles, axis=int(transposed)))
     lhs = jnp.concatenate(columns, axis=1 - int(transposed))
     product = lax.dot_general(lhs, ap, (((int(transposed),), (0,)), ((), ())), preferred_element_type=jnp.float32)
-    c_ref[pl.ds(found[0] * TILE, len(found) * TILE), :] += product
+    return pl.ds(min(slots) * TILE, len(slots) * TILE), product
 
 
 def present(cols, name, kind, valid=True):
@@ -204,40 +197,98 @@
     return jnp.concatenate([ref[pl.ds(start + b * depth + m * half, half), :] for b in range(2)], axis=1)
 
 
-def add_blocks(cols, half, width, c_ref, read, kinds, size, mine, theirs, transposed):
+def add_classes(cols, half, width, odd, c_ref, read, kinds, size, mine, theirs, names):
+    for name in names:
+        here = [present(cols, name, kind) for kind in kinds]
+        base = sum(jnp.where(flag, j * size, 0) for j, flag in enumerate(here))
+        there = functools.reduce(jnp.logical_or, here)
+        for m in sorted({m for m, _ in UNITS[name]}):
+            ref = mine if odd == (m == 1) else theirs
+            if ref is not None:
+                slots = {i: slot_of(name, i, odd, width) * half for mm, i in UNITS[name] if mm == m}
+                rows, product = masked_product(ref, base, there, odd, slots, half, width, read(name, m, odd), True)
+                c_ref[rows, :] += product
+
+
+def kind_product(cols, half, width, odd, read, kind, ref, m):
+    here = [present(cols, name, kind) for name in range(len(UNITS))]
+    there = functools.reduce(jnp.logical_or, here)
+    is_far = functools.reduce(jnp.logical_or, [here[name] for name in FARS])
+    ap = read(0, m, odd)
+    for name in range(1, len(UNITS)):
+        ap = jnp.where(here[name], read(name, m, odd), ap)
+    slots = {
+        i: jnp.where(is_far, slot_of(FARS[0], i, odd, width), slot_of(MAINS[0], i, odd, width)) * half for i in range(width)
+    }
+    return masked_product(ref, 0, there, odd, slots, half, width, ap, False)[1]
+
+
+def by_parity(body):
     row_odd = lax.axis_index("row") % 2 == 1
     for odd in (False, True):
         @pl.when(row_odd == odd)
         def _(odd=odd):
-            for name in range(len(UNITS)):
-                here = [present(cols, name, kind) for kind in kinds]
-                base = sum(jnp.where(flag, j * size, 0) for j, flag in enumerate(here))
-
-                @pl.when(functools.reduce(jnp.logical_or, here))
-                def _(name=name, base=base):
-                    for m in sorted({m for m, _ in UNITS[name]}):
-                        ref = mine if odd == (m == 1) else theirs
-                        if ref is not None:
-                            add_product(c_ref, ref, base, name, m, odd, half, width, read(name, m, odd), transposed)
-
-
-def near_kernel(cols, half, width, own_first, own_second, far_first, far_second, swapped, cross_ap, swap, last_swap, c_ref):
-    size = last_swap.shape[0] // len(SECOND)
+            body(odd)
+
+
+def own_kernel(cols, half, width, own_first, own_second, swap, side, c_ref):
+    size = side.shape[0]
+    read = lambda name, m, odd: read_applied(name, m, odd, half, size, (own_first, own_second), None, None, None)
+
+    def body(odd):
+        c_ref[...] = jnp.zeros_like(c_ref)
+        add_classes(cols, half, width, odd, c_ref, read, FIRST, size, swap, None, MAINS)
+
+    by_parity(body)
+
+
+def near_kernel(cols, half, width, own_first, own_second, far_first, far_second, swapped, cross_ap, swap, diag, far, partial, c_ref):
+    size = far.shape[0]
     read = lambda name, m, odd: read_applied(
         name, m, odd, half, size, (own_first, own_second), (far_first, far_second), swapped, cross_ap
     )
-    c_ref[...] = jnp.zeros_like(c_ref)
-    add_blocks(cols, half, width, c_ref, read, FIRST, size, swap, swapped, True)
-    add_blocks(cols, half, width, c_ref, read, SECOND, size, last_swap, None, False)
-
-
-def last_kernel(cols, half, width, own_first, own_second, far_first, far_second, swapped, cross_ap, last, partial, c_ref):
-    size = last.shape[0] // len(SECOND)
+
+    def body(odd):
+        mine = int(odd)
+        c_ref[...] = partial[...]
+        add_classes(cols, half, width, odd, c_ref, read, FIRST, size, None, swapped, MAINS)
+        add_classes(cols, half, width, odd, c_ref, read, FIRST, size, swap, swapped, NEARS + FARS)
+        c_ref[...] += kind_product(cols, half, width, odd, read, DIAG, diag, mine)
+        c_ref[...] += kind_product(cols, half, width, odd, read, FAR, far, mine)
+
+    by_parity(body)
+
+
+def diagonal_kernel(cols, half, width, own_first, own_second, far_first, far_second, swapped, cross_ap, diag_last, partial, c_ref):
+    size = diag_last.shape[0]
     read = lambda name, m, odd: read_applied(
         name, m, odd, half, size, (own_first, own_second), (far_first, far_second), swapped, cross_ap
     )
-    c_ref[...] = partial[...]
-    add_blocks(cols, half, width, c_ref, read, SECOND, size, None, last, False)
+
+    def body(odd):
+        c_ref[...] = partial[...] + kind_product(cols, half, width, odd, read, DIAG, diag_last, 1 - int(odd))
+
+    by_parity(body)
+
+
+def last_kernel(cols, half, width, own_first, own_second, far_first, far_second, swapped, cross_ap, far_last, partial, out_hbm, c_ref, sems):
+    size = far_last.shape[0]
+    read = lambda name, m, odd: read_applied(
+        name, m, odd, half, size, (own_first, own_second), (far_first, far_second), swapped, cross_ap
+    )
+
+    def body(odd):
+        product = kind_product(cols, half, width, odd, read, FAR, far_last, 1 - int(odd))
+        copies = []
+        for i in range(width):
+            rows = pl.ds(i * TILE, TILE)
+            c_ref[rows, :] = partial[rows, :] + product[i * TILE : (i + 1) * TILE, :]
+            copies.append(pltpu.make_async_copy(c_ref.at[rows, :], out_hbm.at[rows, :], sems.at[i]))
+            copies[-1].start()
+        for copy in copies:
+            copy.wait()
+
+    by_parity(body)
 
 
 def on_device(rows, cols, prolong, applied, prolong_pattern, applied_pattern):
@@ -306,14 +357,17 @@
         functools.partial(far_forward_kernel, cols), "far_forward", shape(size, TILE), mine, cross, cross
     )
     far = move(far_send, col_pairs(far_pairs))
-    far_first = call(settle_kernel, "settle_first", half_ap, far_first, mine, weight=FIRST_WEIGHT)
+    far_first = call(pass_kernel, "settle_first", half_ap, far_first, mine, weight=FIRST_WEIGHT)
     swap = call(
         swap_kernel, "swap", shape(len(FIRST) * size + 4 * depth, TILE), mine, side, pair, cross, own_second, far_first
     )
     swapped = move(swap, partner)
-    far_second = call(settle_kernel, "settle", half_ap, far_second, swap)
-    last_swap = call(last_swap_kernel, "last_swap", shape(len(SECOND) * size, TILE), far, diag, far_second, weight=LAST_WEIGHT)
-    last = move(last_swap, partner)
+    result = jax.ShapeDtypeStruct((prolong.shape[1], applied.shape[1]), jnp.float32)
+    sizes = (cols, half, width)
+    partial = call(functools.partial(own_kernel, *sizes), "own", result, own_first, own_second, swap, side)
+    far_second = call(pass_kernel, "settle", half_ap, far_second, partial)
+    diag_last = move(call(pass_kernel, "pass_diagonal", shape(size, TILE), diag, diag_send), partner)
+    far_last = move(call(pass_kernel, "pass_far", shape(size, TILE), far, far_second, weight=LAST_WEIGHT), partner)
     beyond = [(r, r + 1 if r % 2 == 1 else r - 1) for r in range(rows)]
     relay = [((r + rows // 2) % rows, t) for r, t in beyond if 0 <= t < rows]
     if all(h ^ 1 == t for h, t in relay):
@@ -322,13 +376,15 @@
         first = own_first.reshape(depth, 2, TILE).transpose(1, 0, 2).reshape(2 * depth, TILE)
         cross_ap = move(first, row_pairs([(r, t) for r, t in beyond if 0 <= t < rows]))
 
-    result = jax.ShapeDtypeStruct((prolong.shape[1], applied.shape[1]), jnp.float32)
-    sizes = (cols, half, width)
     aps = (own_first, own_second, far_first, far_second, swapped, cross_ap)
-    partial = call(
-        functools.partial(near_kernel, *sizes), "near", result, *aps, swap, last_swap,
-    )
-    return call(functools.partial(last_kernel, *sizes), "last", result, *aps, last, partial)
+    partial = call(functools.partial(near_kernel, *sizes), "near", result, *aps, swap, diag, far, partial)
+    partial = call(functools.partial(diagonal_kernel, *sizes), "diagonal", result, *aps, diag_last, partial)
+    operands = (*aps, far_last, partial)
+    return pl.pallas_call(
+        functools.partial(last_kernel, *sizes), out_shape=result, in_specs=[vmem] * len(operands), out_specs=hbm,
+        compiler_params=params, name="last",
+        scratch_shapes=[pltpu.VMEM(result.shape, jnp.float32), pltpu.SemaphoreType.DMA((width,))],
+    )(*operands)
 
 
 def solution(mesh):

time: 28.5 us -> 28 us (0.982)
  waiting for transfers between devices: 10.7 us -> 9.69 us
  Pallas kernels: 4.85 us -> 5.26 us
    pallas_call x0 -> x1, Pallas kernels: none -> 1.09 us  [on_device(): pl.pallas_call(functools.partial(last_kernel, *sizes), out_shape=result,...]
    ppermute x10 -> x11, waiting for transfers between devices: 10.7 us -> 9.69 us  [move(): return lax.ppermute(x, AXES, pairs)]
    pallas_call x10 -> x12, Pallas kernels: 4.85 us -> 4.16 us  [call(): pl.pallas_call(kernel, out_shape=out_shape, in_specs=specs or [vmem] * le...]
    ppermute x10 -> x11, starting transfers between devices: 12.7 us -> 12.8 us  [move(): return lax.ppermute(x, AXES, pairs)]
  transfers between devices with their start and end apart: 10 -> 11, of which waited for: 5 -> 5; matrix products, arithmetic and copies ran while one was open for 0% -> 0% of each run, Pallas kernels for 7% -> 9%
where the time goes in v5:
time: 28 us; the launch traced here: 27.8 us
  starting transfers between devices  12.8 us (46%)
  waiting for transfers between devices  9.69 us (35%)
  Pallas kernels  5.26 us (19%)
    ppermute x11, starting transfers between devices, move(): return lax.ppermute(x, AXES, pairs)  12.8 us
    ppermute x11, waiting for transfers between devices, move(): return lax.ppermute(x, AXES, pairs)  9.69 us
    pallas_call x12, Pallas kernels, call(): pl.pallas_call(kernel, out_shape=out_shape, in_specs=specs or [vmem] * le...  4.16 us
    pallas_call x1, Pallas kernels, on_device(): pl.pallas_call(functools.partial(last_kernel, *sizes), out_shape=result,...  1.09 us
  transfers between devices with their start and end apart: 11, of which 5 were waited for; matrix products, arithmetic and copies ran while one was open for 0% of the time, Pallas kernels for 9%

profile of v5, /device:TPU:0, one launch (start us, length us, event | category | flops | bytes accessed | tf_op | source)
XLA Modules:
  0.0 27.8 jit_solution(4251275330260512205)
XLA Ops:
  0.0 1.6 %prepare.1 = (bf16[1168,128]{1,0:T(8,128)(2,1)S(1)}, bf16[1168,128]{1,0:T(8,128)(2,1)S(1)}, bf16[768,256]{1,0:T(8,128)(2,1)S(1)}, bf16[768,256]{1,0:T(8,128)(2,1)S(1)}) custom-call(bf16[768,512]{1,0:T(8,128)(2,1)} %p_hbm.1, bf16[1536,256]{1,0:T(8,128)(2,1)} %ap_hbm.1, s32[4,6]{1,0:T(4,128)} %bitcast.2, s32[2,12]{1,0:T(2,128)} %bitcast.3), custom_call_target="tpu_custom_call" | custom-call | tf_op jit(solution)/shard_map/prepare/pallas_call | solution.py:308
  1.6 0.5 %collective-permute-start.1 = (bf16[1168,128]{1,0:T(8,128)(2,1)S(1)}, bf16[1168,128]{1,0:T(8,128)(2,1)S(1)}, u32[]{:S(2)}, u32[]{:S(2)}) collective-permute-start(bf16[1168,128]{1,0:T(8,128)(2,1)S(1)} %get-tuple-element.12), channel_id=1, source_target_pairs={{0,8},{1,9},{2,10},{3,11},{4,12},{5,13},{6,14},{7,15},{8,0},{9,1},... | collective-permute-start | bytes 897032 | tf_op jit(solution)/shard_map/ppermute | solution.py:314
  2.1 2.6 %collective-permute-start = (bf16[768,256]{1,0:T(8,128)(2,1)S(1)}, bf16[768,256]{1,0:T(8,128)(2,1)S(1)}, u32[]{:S(2)}, u32[]{:S(2)}) collective-permute-start(bf16[768,256]{1,0:T(8,128)(2,1)S(1)} %get-tuple-element.9.own_first), channel_id=1, source_target_pairs={{0,16},{1,17},{2,18},{3,19},{4,20},{5,21},{6,22},{7,23},{8,24},{9,... | collective-permute-start | bytes 1179656 | tf_op jit(solution)/shard_map/ppermute | solution.py:314
  4.7 0.0 collective-permute-done.1.got_ref
  4.7 0.1 merge.1.ordered_after.own
  4.8 0.2 collective-permute-start.5
  5.0 3.0 %collective-permute-start.4 = (bf16[1184,128]{1,0:T(8,128)(2,1)S(1)}, bf16[1184,128]{1,0:T(8,128)(2,1)S(1)}, u32[]{:S(2)}, u32[]{:S(2)}) collective-permute-start(bf16[1184,128]{1,0:T(8,128)(2,1)S(1)} %merge.1.ordered_after.own), channel_id=1, source_target_pairs={{0,2},{1,3},{2,0},{3,1},{4,6},{5,7},{6,4},{7,5},{8,10},{9,11},{10,... | collective-permute-start | bytes 909320 | tf_op jit(solution)/shard_map/ppermute | solution.py:314
  8.0 1.5 %collective-permute-start.2 = (bf16[768,256]{1,0:T(8,128)(2,1)S(1)}, bf16[768,256]{1,0:T(8,128)(2,1)S(1)}, u32[]{:S(2)}, u32[]{:S(2)}) collective-permute-start(bf16[768,256]{1,0:T(8,128)(2,1)S(1)} %get-tuple-element.10.own_second), channel_id=1, source_target_pairs={{0,16},{1,17},{2,18},{3,19},{4,20},{5,21},{6,22},{7,23},{8,24},{9,... | collective-permute-start | bytes 1179656 | tf_op jit(solution)/shard_map/ppermute | solution.py:314
  9.5 1.5 %collective-permute-start.3 = (bf16[1184,128]{1,0:T(8,128)(2,1)S(1)}, bf16[1184,128]{1,0:T(8,128)(2,1)S(1)}, u32[]{:S(2)}, u32[]{:S(2)}) collective-permute-start(bf16[1184,128]{1,0:T(8,128)(2,1)S(1)} %merge.1.ordered_after.own), channel_id=1, source_target_pairs={{0,1},{1,0},{2,3},{3,2},{4,5},{5,4},{6,7},{7,6},{8,9},{9,8},{10,11... | collective-permute-start | bytes 909320 | tf_op jit(solution)/shard_map/ppermute | solution.py:314
  11.0 4.2 %collective-permute-done.4.pair.ordered_after = bf16[1184,128]{1,0:T(8,128)(2,1)S(1)} collective-permute-done((bf16[1184,128]{1,0:T(8,128)(2,1)S(1)}, bf16[1184,128]{1,0:T(8,128)(2,1)S(1)}, u32[]{:S(2)}, u32[]{:S(2)}) %collective-permute-start.4) | collective-permute-done | bytes 303136 | tf_op jit(solution)/shard_map/ppermute | solution.py:314
  15.3 1.6 %collective-permute-start.9 = (bf16[1184,128]{1,0:T(8,128)(2,1)S(1)}, bf16[1184,128]{1,0:T(8,128)(2,1)S(1)}, u32[]{:S(2)}, u32[]{:S(2)}) collective-permute-start(bf16[1184,128]{1,0:T(8,128)(2,1)S(1)} %diagonal_forward.1.ordered_after), channel_id=1, source_target_pairs={{0,1},{1,0},{2,3},{3,2},{4,5},{5,4},{6,7},{7,6},{8,9},{9,8},{10,11... | collective-permute-start | bytes 909320 | tf_op jit(solution)/shard_map/ppermute | solution.py:314
  16.9 1.7 %collective-permute-start.7 = (bf16[1184,128]{1,0:T(8,128)(2,1)S(1)}, bf16[1184,128]{1,0:T(8,128)(2,1)S(1)}, u32[]{:S(2)}, u32[]{:S(2)}) collective-permute-start(bf16[1184,128]{1,0:T(8,128)(2,1)S(1)} %far_forward.1), channel_id=1, source_target_pairs={{0,4},{1,5},{2,0},{3,1},{4,6},{5,7},{6,2},{7,3},{8,12},{9,13},{10,... | collective-permute-start | bytes 909320 | tf_op jit(solution)/shard_map/ppermute | solution.py:314
  18.6 0.4 %swap.1 = bf16[7808,128]{1,0:T(8,128)(2,1)S(1)} custom-call(bf16[1184,128]{1,0:T(8,128)(2,1)S(1)} %merge.1.ordered_after.own, bf16[1184,128]{1,0:T(8,128)(2,1)S(1)} %collective-permute-done.3.side, bf16[1184,128]{1,0:T(8,128)(2,1)S(1)} %collective-permute-done.4.pair.ordered_after, bf16[1184,128]{1,0:T(8,128)(2,1)S(1)} %collective-permute-done.5.cross.ordered_after, ...), custom_call_target="tpu_custom_call" | custom-call | tf_op jit(solution)/shard_map/swap/pallas_call | solution.py:308
  19.0 0.1 collective-permute-start.6
  19.1 0.4 %own.1.ordered_after.partial = f32[512,256]{1,0:T(8,128)S(1)} custom-call(bf16[768,256]{1,0:T(8,128)(2,1)S(1)} %get-tuple-element.9.own_first, bf16[768,256]{1,0:T(8,128)(2,1)S(1)} %get-tuple-element.10.own_second, bf16[7808,128]{1,0:T(8,128)(2,1)S(1)} %swap.1, bf16[1184,128]{1,0:T(8,128)(2,1)S(1)} %collective-permute-done.3.side), custom_call_target="tpu_custom_call" | custom-call | tf_op jit(solution)/shard_map/own/pallas_call | solution.py:308
  19.5 3.3 %collective-permute-done.2.ref = bf16[768,256]{1,0:T(8,128)(2,1)S(1)} collective-permute-done((bf16[768,256]{1,0:T(8,128)(2,1)S(1)}, bf16[768,256]{1,0:T(8,128)(2,1)S(1)}, u32[]{:S(2)}, u32[]{:S(2)}) %collective-permute-start.2) | collective-permute-done | bytes 393248 | tf_op jit(solution)/shard_map/ppermute | solution.py:314
  22.9 1.5 %collective-permute-done.9.ref.diag = bf16[1184,128]{1,0:T(8,128)(2,1)S(1)} collective-permute-done((bf16[1184,128]{1,0:T(8,128)(2,1)S(1)}, bf16[1184,128]{1,0:T(8,128)(2,1)S(1)}, u32[]{:S(2)}, u32[]{:S(2)}) %collective-permute-start.9) | collective-permute-done | bytes 303136 | tf_op jit(solution)/shard_map/ppermute | solution.py:314
  24.4 0.1 collective-permute-start.10
  24.5 0.5 %collective-permute-done.7.ref.far = bf16[1184,128]{1,0:T(8,128)(2,1)S(1)} collective-permute-done((bf16[1184,128]{1,0:T(8,128)(2,1)S(1)}, bf16[1184,128]{1,0:T(8,128)(2,1)S(1)}, u32[]{:S(2)}, u32[]{:S(2)}) %collective-permute-start.7) | collective-permute-done | bytes 303136 | tf_op jit(solution)/shard_map/ppermute | solution.py:314
  25.1 0.1 collective-permute-start.8
  25.2 1.1 %near.1.partial = f32[512,256]{1,0:T(8,128)S(1)} custom-call(bf16[768,256]{1,0:T(8,128)(2,1)S(1)} %get-tuple-element.9.own_first, bf16[768,256]{1,0:T(8,128)(2,1)S(1)} %get-tuple-element.10.own_second, bf16[768,256]{1,0:T(8,128)(2,1)S(1)} %settle_first.1.far_first, bf16[768,256]{1,0:T(8,128)(2,1)S(1)} %settle.1.ordered_after.far_second, ...), custom_call_target="tpu_custom_call" | custom-call | tf_op jit(solution)/shard_map/near/pallas_call | solution.py:308
  26.3 0.4 %diagonal.1.partial = f32[512,256]{1,0:T(8,128)S(1)} custom-call(bf16[768,256]{1,0:T(8,128)(2,1)S(1)} %get-tuple-element.9.own_first, bf16[768,256]{1,0:T(8,128)(2,1)S(1)} %get-tuple-element.10.own_second, bf16[768,256]{1,0:T(8,128)(2,1)S(1)} %settle_first.1.far_first, bf16[768,256]{1,0:T(8,128)(2,1)S(1)} %settle.1.ordered_after.far_second, ...), custom_call_target="tpu_custom_call" | custom-call | tf_op jit(solution)/shard_map/diagonal/pallas_call | solution.py:308
  26.7 0.1 collective-permute-done.8.far_last
  26.7 1.1 %last.1 = f32[512,256]{1,0:T(8,128)} custom-call(bf16[768,256]{1,0:T(8,128)(2,1)S(1)} %get-tuple-element.9.own_first, bf16[768,256]{1,0:T(8,128)(2,1)S(1)} %get-tuple-element.10.own_second, bf16[768,256]{1,0:T(8,128)(2,1)S(1)} %settle_first.1.far_first, bf16[768,256]{1,0:T(8,128)(2,1)S(1)} %settle.1.ordered_after.far_second, ...), custom_call_target="tpu_custom_call" | custom-call | tf_op jit(solution)/shard_map/last/pallas_call | solution.py:383
  (11 shorter events, 0.1 us)
Async XLA Ops:
  1.6 3.1 %collective-permute-start.1 = (bf16[1168,128]{1,0:T(8,128)(2,1)S(1)}, bf16[1168,128]{1,0:T(8,128)(2,1)S(1)}, u32[]{:S(2)}, u32[]{:S(2)}) collective-permute-start(bf16[1168,128]{1,0:T(8,128)(2,1)S(1)} %get-tuple-element.12), channel_id=1, source_target_pairs={{0,8},{1,9},{2,10},{3,11},{4,12},{5,13},{6,14},{7,15},{8,0},{9,1},... | collective-permute-start | bytes 897032 | tf_op jit(solution)/shard_map/ppermute | solution.py:314
  2.1 16.4 %collective-permute-start = (bf16[768,256]{1,0:T(8,128)(2,1)S(1)}, bf16[768,256]{1,0:T(8,128)(2,1)S(1)}, u32[]{:S(2)}, u32[]{:S(2)}) collective-permute-start(bf16[768,256]{1,0:T(8,128)(2,1)S(1)} %get-tuple-element.9.own_first), channel_id=1, source_target_pairs={{0,16},{1,17},{2,18},{3,19},{4,20},{5,21},{6,22},{7,23},{8,24},{9,... | collective-permute-start | bytes 1179656 | tf_op jit(solution)/shard_map/ppermute | solution.py:314
  4.8 6.2 %collective-permute-start.5 = (bf16[1184,128]{1,0:T(8,128)(2,1)S(1)}, bf16[1184,128]{1,0:T(8,128)(2,1)S(1)}, u32[]{:S(2)}, u32[]{:S(2)}) collective-permute-start(bf16[1184,128]{1,0:T(8,128)(2,1)S(1)} %merge.1.ordered_after.own), channel_id=1, source_target_pairs={{0,8},{1,9},{2,4},{3,5},{4,2},{5,3},{6,14},{7,15},{8,0},{9,1},{10,... | collective-permute-start | bytes 909320 | tf_op jit(solution)/shard_map/ppermute | solution.py:314
  5.0 10.2 %collective-permute-start.4 = (bf16[1184,128]{1,0:T(8,128)(2,1)S(1)}, bf16[1184,128]{1,0:T(8,128)(2,1)S(1)}, u32[]{:S(2)}, u32[]{:S(2)}) collective-permute-start(bf16[1184,128]{1,0:T(8,128)(2,1)S(1)} %merge.1.ordered_after.own), channel_id=1, source_target_pairs={{0,2},{1,3},{2,0},{3,1},{4,6},{5,7},{6,4},{7,5},{8,10},{9,11},{10,... | collective-permute-start | bytes 909320 | tf_op jit(solution)/shard_map/ppermute | solution.py:314
  8.0 14.8 %collective-permute-start.2 = (bf16[768,256]{1,0:T(8,128)(2,1)S(1)}, bf16[768,256]{1,0:T(8,128)(2,1)S(1)}, u32[]{:S(2)}, u32[]{:S(2)}) collective-permute-start(bf16[768,256]{1,0:T(8,128)(2,1)S(1)} %get-tuple-element.10.own_second), channel_id=1, source_target_pairs={{0,16},{1,17},{2,18},{3,19},{4,20},{5,21},{6,22},{7,23},{8,24},{9,... | collective-permute-start | bytes 1179656 | tf_op jit(solution)/shard_map/ppermute | solution.py:314
  9.5 9.0 %collective-permute-start.3 = (bf16[1184,128]{1,0:T(8,128)(2,1)S(1)}, bf16[1184,128]{1,0:T(8,128)(2,1)S(1)}, u32[]{:S(2)}, u32[]{:S(2)}) collective-permute-start(bf16[1184,128]{1,0:T(8,128)(2,1)S(1)} %merge.1.ordered_after.own), channel_id=1, source_target_pairs={{0,1},{1,0},{2,3},{3,2},{4,5},{5,4},{6,7},{7,6},{8,9},{9,8},{10,11... | collective-permute-start | bytes 909320 | tf_op jit(solution)/shard_map/ppermute | solution.py:314
  15.3 9.1 %collective-permute-start.9 = (bf16[1184,128]{1,0:T(8,128)(2,1)S(1)}, bf16[1184,128]{1,0:T(8,128)(2,1)S(1)}, u32[]{:S(2)}, u32[]{:S(2)}) collective-permute-start(bf16[1184,128]{1,0:T(8,128)(2,1)S(1)} %diagonal_forward.1.ordered_after), channel_id=1, source_target_pairs={{0,1},{1,0},{2,3},{3,2},{4,5},{5,4},{6,7},{7,6},{8,9},{9,8},{10,11... | collective-permute-start | bytes 909320 | tf_op jit(solution)/shard_map/ppermute | solution.py:314
  16.9 8.2 %collective-permute-start.7 = (bf16[1184,128]{1,0:T(8,128)(2,1)S(1)}, bf16[1184,128]{1,0:T(8,128)(2,1)S(1)}, u32[]{:S(2)}, u32[]{:S(2)}) collective-permute-start(bf16[1184,128]{1,0:T(8,128)(2,1)S(1)} %far_forward.1), channel_id=1, source_target_pairs={{0,4},{1,5},{2,0},{3,1},{4,6},{5,7},{6,2},{7,3},{8,12},{9,13},{10,... | collective-permute-start | bytes 909320 | tf_op jit(solution)/shard_map/ppermute | solution.py:314
  19.0 6.1 %collective-permute-start.6 = (bf16[7808,128]{1,0:T(8,128)(2,1)S(1)}, bf16[7808,128]{1,0:T(8,128)(2,1)S(1)}, u32[]{:S(2)}, u32[]{:S(2)}) collective-permute-start(bf16[7808,128]{1,0:T(8,128)(2,1)S(1)} %swap.1), channel_id=1, source_target_pairs={{0,8},{1,9},{2,10},{3,11},{4,12},{5,13},{6,14},{7,15},{8,0},{9,1},... | collective-permute-start | bytes 5996552 | tf_op jit(solution)/shard_map/ppermute | solution.py:314
  24.4 1.8 %collective-permute-start.10 = (bf16[1184,128]{1,0:T(8,128)(2,1)S(1)}, bf16[1184,128]{1,0:T(8,128)(2,1)S(1)}, u32[]{:S(2)}, u32[]{:S(2)}) collective-permute-start(bf16[1184,128]{1,0:T(8,128)(2,1)S(1)} %pass_diagonal.1), channel_id=1, source_target_pairs={{0,8},{1,9},{2,10},{3,11},{4,12},{5,13},{6,14},{7,15},{8,0},{9,1},... | collective-permute-start | bytes 909320 | tf_op jit(solution)/shard_map/ppermute | solution.py:314
  25.1 1.7 %collective-permute-start.8 = (bf16[1184,128]{1,0:T(8,128)(2,1)S(1)}, bf16[1184,128]{1,0:T(8,128)(2,1)S(1)}, u32[]{:S(2)}, u32[]{:S(2)}) collective-permute-start(bf16[1184,128]{1,0:T(8,128)(2,1)S(1)} %pass_far.1), channel_id=1, source_target_pairs={{0,8},{1,9},{2,10},{3,11},{4,12},{5,13},{6,14},{7,15},{8,0},{9,1},... | collective-permute-start | bytes 909320 | tf_op jit(solution)/shard_map/ppermute | solution.py:314

commit v6 on v5

--- a/solution.py
+++ b/solution.py
@@ -41,12 +41,18 @@
     return 2 if name in FARS else (i + (width if odd else 0)) % SLOTS
 
 
-def prepare_kernel(cols, p_hbm, ap_hbm, p_pattern_hbm, ap_pattern_hbm, keep_ref, send_ref, first_ref, second_ref, p_ref, ap_ref, p_pattern, ap_pattern, sems):
+def prepare_kernel(cols, p_hbm, ap_hbm, p_pattern_hbm, ap_pattern_hbm, keep_ref, send_ref, first_ref, second_ref, p_ref, p_pattern, ap_pattern, sems):
+    depth = p_ref.shape[0]
+    start = pl.multiple_of(jnp.where(lax.axis_index("row") % 2 == 1, depth, 0), depth)
     copies = [
         pltpu.make_async_copy(source, target, sems.at[i])
-        for i, (source, target) in enumerate(
-            ((p_pattern_hbm, p_pattern), (p_hbm, p_ref), (ap_pattern_hbm, ap_pattern), (ap_hbm, ap_ref))
-        )
+        for i, (source, target) in enumerate((
+            (p_pattern_hbm, p_pattern),
+            (p_hbm, p_ref),
+            (ap_pattern_hbm, ap_pattern),
+            (ap_hbm.at[pl.ds(start, depth), :], first_ref.at[pl.ds(0, depth), :]),
+            (ap_hbm.at[pl.ds(depth - start, depth), :], second_ref.at[pl.ds(0, depth), :]),
+        ))
     ]
     for copy in copies:
         copy.start()
@@ -97,16 +103,34 @@
             out[pl.ds(0, SLOTS * half), :] = jnp.zeros((SLOTS * half, TILE), p_ref.dtype)
 
     copies[2].wait()
+    rows, columns = depth // TILE, first_ref.shape[1] // TILE
+    shift = jnp.where(r % 2 == 1, rows, 0)
+    for out_ref, low in ((first_ref, shift), (second_ref, rows - shift)):
+        for b in range(columns):
+            value = jnp.zeros((META, TILE), jnp.float32)
+            for a in range(rows):
+                value = jnp.where(line == a, ap_pattern[b, low + a].astype(jnp.float32), value)
+            out_ref[pl.ds(depth, META), pl.ds(b * TILE, TILE)] = value.astype(out_ref.dtype)
     copies[3].wait()
-    count = ap_ref.shape[0] // TILE
-    shift = jnp.where(r % 2 == 1, count // 2, 0)
-    for a in range(count):
-        row = lax.rem(a + shift, count)
-        rows = pl.ds(pl.multiple_of(row * TILE, TILE), TILE)
-        for b in range(ap_ref.shape[1] // TILE):
-            tile = ap_ref[rows, pl.ds(b * TILE, TILE)]
-            out_ref = first_ref if 2 * a < count else second_ref
-            out_ref[pl.ds(a % (count // 2) * TILE, TILE), pl.ds(b * TILE, TILE)] = jnp.where(ap_pattern[b, row] > 0, tile, zeros)
+    copies[4].wait()
+
+
+def mask_applied(ref, out_ref):
+    depth = out_ref.shape[0]
+    pattern = ref[pl.ds(depth, META), :].astype(jnp.float32)
+    for a in range(depth // TILE):
+        weight = jnp.broadcast_to(pattern[a : a + 1, :], (META, out_ref.shape[1])).astype(ref.dtype)
+        rows = pl.ds(a * TILE, TILE)
+        out_ref[rows, :] = (ref[rows, :].reshape(TILE // META, META, -1) * weight[None]).reshape(TILE, -1)
+
+
+def mask_kernel(ref, ordered_after, out_ref):
+    mask_applied(ref, out_ref)
+
+
+def mask_own_kernel(first_ref, second_ref, first_out, second_out):
+    mask_applied(first_ref, first_out)
+    mask_applied(second_ref, second_out)
 
 
 def merge_kernel(keep_ref, got_ref, half_ref):
@@ -161,7 +185,7 @@
     out_ref[...] = ref[...]
 
 
-def masked_product(ref, base, flag, odd, slots, half, width, ap, transposed):
+def masked_units(ref, base, flag, odd, slots, half, width, transposed):
     note = base + SLOTS * half + (META if odd else 0)
     pattern = ref[pl.ds(pl.multiple_of(note, META), META), :].astype(jnp.float32)
     pattern = pattern * jnp.where(flag, 1.0, 0.0)
@@ -170,12 +194,16 @@
         tiles = []
         for a in range(half // TILE):
             k = a * width + i
-            weight = jnp.broadcast_to(pattern[k : k + 1, :], (TILE, TILE)).astype(ref.dtype)
-            tiles.append(ref[pl.ds(pl.multiple_of(base + slot + a * TILE, META), TILE), :] * weight)
+            weight = jnp.broadcast_to(pattern[k : k + 1, :], (META, TILE)).astype(ref.dtype)
+            tile = ref[pl.ds(pl.multiple_of(base + slot + a * TILE, META), TILE), :]
+            tiles.append((tile.reshape(TILE // META, META, TILE) * weight[None]).reshape(TILE, TILE))
         columns.append(jnp.concatenate(tiles, axis=int(transposed)))
-    lhs = jnp.concatenate(columns, axis=1 - int(transposed))
-    product = lax.dot_general(lhs, ap, (((int(transposed),), (0,)), ((), ())), preferred_element_type=jnp.float32)
-    return pl.ds(min(slots) * TILE, len(slots) * TILE), product
+    return jnp.concatenate(columns, axis=1 - int(transposed))
+
+
+def product(units, ap, transposed):
+    contract = (((int(transposed),), (0,)), ((), ()))
+    return lax.dot_general(units, ap, contract, preferred_element_type=jnp.float32)
 
 
 def present(cols, name, kind, valid=True):
@@ -197,20 +225,16 @@
     return jnp.concatenate([ref[pl.ds(start + b * depth + m * half, half), :] for b in range(2)], axis=1)
 
 
-def add_classes(cols, half, width, odd, c_ref, read, kinds, size, mine, theirs, names):
-    for name in names:
-        here = [present(cols, name, kind) for kind in kinds]
-        base = sum(jnp.where(flag, j * size, 0) for j, flag in enumerate(here))
-        there = functools.reduce(jnp.logical_or, here)
-        for m in sorted({m for m, _ in UNITS[name]}):
-            ref = mine if odd == (m == 1) else theirs
-            if ref is not None:
-                slots = {i: slot_of(name, i, odd, width) * half for mm, i in UNITS[name] if mm == m}
-                rows, product = masked_product(ref, base, there, odd, slots, half, width, read(name, m, odd), True)
-                c_ref[rows, :] += product
-
-
-def kind_product(cols, half, width, odd, read, kind, ref, m):
+def class_units(cols, half, width, odd, name, m, found, kinds, size, mine, theirs):
+    here = [present(cols, name, kind) for kind in kinds]
+    base = sum(jnp.where(flag, j * size, 0) for j, flag in enumerate(here))
+    there = functools.reduce(jnp.logical_or, here)
+    slots = {i: slot_of(name, i, odd, width) * half for i in found}
+    ref = mine if odd == (m == 1) else theirs
+    return masked_units(ref, base, there, odd, slots, half, width, True)
+
+
+def kind_units(cols, half, width, odd, read, kind, ref, m):
     here = [present(cols, name, kind) for name in range(len(UNITS))]
     there = functools.reduce(jnp.logical_or, here)
     is_far = functools.reduce(jnp.logical_or, [here[name] for name in FARS])
@@ -220,7 +244,7 @@
     slots = {
         i: jnp.where(is_far, slot_of(FARS[0], i, odd, width), slot_of(MAINS[0], i, odd, width)) * half for i in range(width)
     }
-    return masked_product(ref, 0, there, odd, slots, half, width, ap, False)[1]
+    return masked_units(ref, 0, there, odd, slots, half, width, False), ap
 
 
 def by_parity(body):
@@ -233,11 +257,12 @@
 
 def own_kernel(cols, half, width, own_first, own_second, swap, side, c_ref):
     size = side.shape[0]
-    read = lambda name, m, odd: read_applied(name, m, odd, half, size, (own_first, own_second), None, None, None)
 
     def body(odd):
-        c_ref[...] = jnp.zeros_like(c_ref)
-        add_classes(cols, half, width, odd, c_ref, read, FIRST, size, swap, None, MAINS)
+        m = int(odd)
+        units = [class_units(cols, half, width, odd, name, m, range(width), FIRST, size, swap, None) for name in MAINS]
+        ap = [read_applied(name, m, odd, half, size, (own_first, own_second), None, None, None) for name in MAINS]
+        c_ref[...] = product(jnp.concatenate(units, axis=1), jnp.concatenate(ap, axis=0), True)
 
     by_parity(body)
 
@@ -249,12 +274,22 @@
     )
 
     def body(odd):
-        mine = int(odd)
-        c_ref[...] = partial[...]
-        add_classes(cols, half, width, odd, c_ref, read, FIRST, size, None, swapped, MAINS)
-        add_classes(cols, half, width, odd, c_ref, read, FIRST, size, swap, swapped, NEARS + FARS)
-        c_ref[...] += kind_product(cols, half, width, odd, read, DIAG, diag, mine)
-        c_ref[...] += kind_product(cols, half, width, odd, read, FAR, far, mine)
+        mine, theirs = int(odd), 1 - int(odd)
+        units = lambda name, m, found: class_units(cols, half, width, odd, name, m, found, FIRST, size, swap, swapped)
+        lhs = jnp.concatenate([units(name, theirs, range(width)) for name in MAINS], axis=1)
+        rhs = jnp.concatenate([read(name, theirs, odd) for name in MAINS], axis=0)
+        c_ref[...] = partial[...] + product(lhs, rhs, True)
+        late = [kind_units(cols, half, width, odd, read, kind, ref, mine) for kind, ref in ((DIAG, diag), (FAR, far))]
+        lhs, rhs = (jnp.concatenate(x, axis=0) for x in zip(*late))
+        c_ref[...] += product(lhs, rhs, False)
+        for name in NEARS:
+            found = sorted({i for _, i in UNITS[name]})
+            lhs = jnp.concatenate([units(name, m, found) for m in range(2)], axis=1)
+            rhs = jnp.concatenate([read(name, m, odd) for m in range(2)], axis=0)
+            c_ref[pl.ds(found[0] * TILE, len(found) * TILE), :] += product(lhs, rhs, True)
+        for name in FARS:
+            for m, i in UNITS[name]:
+                c_ref[pl.ds(i * TILE, TILE), :] += product(units(name, m, [i]), read(name, m, odd), True)
 
     by_parity(body)
 
@@ -266,7 +301,7 @@
     )
 
     def body(odd):
-        c_ref[...] = partial[...] + kind_product(cols, half, width, odd, read, DIAG, diag_last, 1 - int(odd))
+        c_ref[...] = partial[...] + product(*kind_units(cols, half, width, odd, read, DIAG, diag_last, 1 - int(odd)), False)
 
     by_parity(body)
 
@@ -278,11 +313,11 @@
     )
 
     def body(odd):
-        product = kind_product(cols, half, width, odd, read, FAR, far_last, 1 - int(odd))
+        units, ap = kind_units(cols, half, width, odd, read, FAR, far_last, 1 - int(odd))
         copies = []
         for i in range(width):
             rows = pl.ds(i * TILE, TILE)
-            c_ref[rows, :] = partial[rows, :] + product[i * TILE : (i + 1) * TILE, :]
+            c_ref[rows, :] = partial[rows, :] + product(units[:, i * TILE : (i + 1) * TILE], ap, False)
             copies.append(pltpu.make_async_copy(c_ref.at[rows, :], out_hbm.at[rows, :], sems.at[i]))
             copies[-1].start()
         for copy in copies:
@@ -324,20 +359,20 @@
 
     hbm = pl.BlockSpec(memory_space=pltpu.HBM)
     half_ap = shape(depth, applied.shape[1])
-    keep, send, own_first, own_second = call(
-        functools.partial(prepare_kernel, cols), "prepare", (shape(data + META, TILE),) * 2 + (half_ap,) * 2,
+    keep, send, raw_first, raw_second = call(
+        functools.partial(prepare_kernel, cols), "prepare",
+        (shape(data + META, TILE),) * 2 + (shape(depth + META, applied.shape[1]),) * 2,
         *[pltpu.with_memory_space_constraint(x, pltpu.HBM) for x in (prolong, applied, prolong_pattern.T, applied_pattern.T)],
         specs=[hbm] * 4,
         scratch_shapes=[
             pltpu.VMEM(prolong.shape, prolong.dtype),
-            pltpu.VMEM(applied.shape, applied.dtype),
             pltpu.SMEM(prolong_pattern.shape[::-1], jnp.int32),
             pltpu.SMEM(applied_pattern.shape[::-1], jnp.int32),
-            pltpu.SemaphoreType.DMA((4,)),
+            pltpu.SemaphoreType.DMA((5,)),
         ],
     )
     got = move(send, partner)
-    far_first, far_second = move(own_first, row_pairs(opposite)), move(own_second, row_pairs(opposite))
+    far_first, far_second = move(raw_first, row_pairs(opposite)), move(raw_second, row_pairs(opposite))
     mine = call(merge_kernel, "merge", shape(size, TILE), keep, got)
     middle = lambda c: 2 <= c < cols - 2
     step = lambda c: c - 2 if (c // 2) % 2 == 0 else c + 2
@@ -357,7 +392,8 @@
         functools.partial(far_forward_kernel, cols), "far_forward", shape(size, TILE), mine, cross, cross
     )
     far = move(far_send, col_pairs(far_pairs))
-    far_first = call(pass_kernel, "settle_first", half_ap, far_first, mine, weight=FIRST_WEIGHT)
+    own_first, own_second = call(mask_own_kernel, "mask_own", (half_ap,) * 2, raw_first, raw_second)
+    far_first = call(mask_kernel, "settle_first", half_ap, far_first, mine, weight=FIRST_WEIGHT)
     swap = call(
         swap_kernel, "swap", shape(len(FIRST) * size + 4 * depth, TILE), mine, side, pair, cross, own_second, far_first
     )
@@ -365,7 +401,7 @@
     result = jax.ShapeDtypeStruct((prolong.shape[1], applied.shape[1]), jnp.float32)
     sizes = (cols, half, width)
     partial = call(functools.partial(own_kernel, *sizes), "own", result, own_first, own_second, swap, side)
-    far_second = call(pass_kernel, "settle", half_ap, far_second, partial)
+    far_second = call(mask_kernel, "settle", half_ap, far_second, partial)
     diag_last = move(call(pass_kernel, "pass_diagonal", shape(size, TILE), diag, diag_send), partner)
     far_last = move(call(pass_kernel, "pass_far", shape(size, TILE), far, far_second, weight=LAST_WEIGHT), partner)
     beyond = [(r, r + 1 if r % 2 == 1 else r - 1) for r in range(rows)]

time: 28 us -> 27.9 us (level)
    pallas_call x12 -> x13, Pallas kernels: 4.16 us -> 3.98 us  [call(): pl.pallas_call(kernel, out_shape=out_shape, in_specs=specs or [vmem] * le...]
  transfers between devices with their start and end apart: 11 -> 11, of which waited for: 5 -> 6; matrix products, arithmetic and copies ran while one was open for 0% -> 0% of each run, Pallas kernels for 9% -> 9%
where the time goes in v6:
time: 27.9 us; the launch traced here: 27.7 us
  starting transfers between devices  12.9 us (46%)
  waiting for transfers between devices  9.65 us (35%)
  Pallas kernels  5.07 us (18%)
    ppermute x11, starting transfers between devices, move(): return lax.ppermute(x, AXES, pairs)  12.9 us
    ppermute x11, waiting for transfers between devices, move(): return lax.ppermute(x, AXES, pairs)  9.65 us
    pallas_call x13, Pallas kernels, call(): pl.pallas_call(kernel, out_shape=out_shape, in_specs=specs or [vmem] * le...  3.98 us
    pallas_call x1, Pallas kernels, on_device(): pl.pallas_call(functools.partial(last_kernel, *sizes), out_shape=result,...  1.1 us
  transfers between devices with their start and end apart: 11, of which 6 were waited for; matrix products, arithmetic and copies ran while one was open for 0% of the time, Pallas kernels for 9%

profile of v6, /device:TPU:0, one launch (start us, length us, event | category | flops | bytes accessed | tf_op | source)
XLA Modules:
  0.0 27.7 jit_solution(5193085261568290465)
XLA Ops:
  0.0 1.5 %prepare.1 = (bf16[1168,128]{1,0:T(8,128)(2,1)S(1)}, bf16[1168,128]{1,0:T(8,128)(2,1)S(1)}, bf16[784,256]{1,0:T(8,128)(2,1)S(1)}, bf16[784,256]{1,0:T(8,128)(2,1)S(1)}) custom-call(bf16[768,512]{1,0:T(8,128)(2,1)} %p_hbm.1, bf16[1536,256]{1,0:T(8,128)(2,1)} %ap_hbm.1, s32[4,6]{1,0:T(4,128)} %bitcast.2, s32[2,12]{1,0:T(2,128)} %bitcast.3), custom_call_target="tpu_custom_call" | custom-call | tf_op jit(solution)/shard_map/prepare/pallas_call | solution.py:343
  1.5 0.4 %collective-permute-start.1 = (bf16[1168,128]{1,0:T(8,128)(2,1)S(1)}, bf16[1168,128]{1,0:T(8,128)(2,1)S(1)}, u32[]{:S(2)}, u32[]{:S(2)}) collective-permute-start(bf16[1168,128]{1,0:T(8,128)(2,1)S(1)} %get-tuple-element.16), channel_id=1, source_target_pairs={{0,8},{1,9},{2,10},{3,11},{4,12},{5,13},{6,14},{7,15},{8,0},{9,1},... | collective-permute-start | bytes 897032 | tf_op jit(solution)/shard_map/ppermute | solution.py:349
  1.9 2.6 %collective-permute-start = (bf16[784,256]{1,0:T(8,128)(2,1)S(1)}, bf16[784,256]{1,0:T(8,128)(2,1)S(1)}, u32[]{:S(2)}, u32[]{:S(2)}) collective-permute-start(bf16[784,256]{1,0:T(8,128)(2,1)S(1)} %get-tuple-element.11.first_ref), channel_id=1, source_target_pairs={{0,16},{1,17},{2,18},{3,19},{4,20},{5,21},{6,22},{7,23},{8,24},{9,... | collective-permute-start | bytes 1204232 | tf_op jit(solution)/shard_map/ppermute | solution.py:349
  4.5 0.1 merge.1.ordered_after.own
  4.6 0.2 collective-permute-start.5
  4.8 3.0 %collective-permute-start.4 = (bf16[1184,128]{1,0:T(8,128)(2,1)S(1)}, bf16[1184,128]{1,0:T(8,128)(2,1)S(1)}, u32[]{:S(2)}, u32[]{:S(2)}) collective-permute-start(bf16[1184,128]{1,0:T(8,128)(2,1)S(1)} %merge.1.ordered_after.own), channel_id=1, source_target_pairs={{0,2},{1,3},{2,0},{3,1},{4,6},{5,7},{6,4},{7,5},{8,10},{9,11},{10,... | collective-permute-start | bytes 909320 | tf_op jit(solution)/shard_map/ppermute | solution.py:349
  7.9 1.5 %collective-permute-start.2 = (bf16[784,256]{1,0:T(8,128)(2,1)S(1)}, bf16[784,256]{1,0:T(8,128)(2,1)S(1)}, u32[]{:S(2)}, u32[]{:S(2)}) collective-permute-start(bf16[784,256]{1,0:T(8,128)(2,1)S(1)} %get-tuple-element.12.second_ref), channel_id=1, source_target_pairs={{0,16},{1,17},{2,18},{3,19},{4,20},{5,21},{6,22},{7,23},{8,24},{9,... | collective-permute-start | bytes 1204232 | tf_op jit(solution)/shard_map/ppermute | solution.py:349
  9.4 1.6 %collective-permute-start.3 = (bf16[1184,128]{1,0:T(8,128)(2,1)S(1)}, bf16[1184,128]{1,0:T(8,128)(2,1)S(1)}, u32[]{:S(2)}, u32[]{:S(2)}) collective-permute-start(bf16[1184,128]{1,0:T(8,128)(2,1)S(1)} %merge.1.ordered_after.own), channel_id=1, source_target_pairs={{0,1},{1,0},{2,3},{3,2},{4,5},{5,4},{6,7},{7,6},{8,9},{9,8},{10,11... | collective-permute-start | bytes 909320 | tf_op jit(solution)/shard_map/ppermute | solution.py:349
  11.0 4.1 %collective-permute-done.4.pair.ordered_after = bf16[1184,128]{1,0:T(8,128)(2,1)S(1)} collective-permute-done((bf16[1184,128]{1,0:T(8,128)(2,1)S(1)}, bf16[1184,128]{1,0:T(8,128)(2,1)S(1)}, u32[]{:S(2)}, u32[]{:S(2)}) %collective-permute-start.4) | collective-permute-done | bytes 303136 | tf_op jit(solution)/shard_map/ppermute | solution.py:349
  15.1 1.6 %collective-permute-start.9 = (bf16[1184,128]{1,0:T(8,128)(2,1)S(1)}, bf16[1184,128]{1,0:T(8,128)(2,1)S(1)}, u32[]{:S(2)}, u32[]{:S(2)}) collective-permute-start(bf16[1184,128]{1,0:T(8,128)(2,1)S(1)} %diagonal_forward.1.ordered_after), channel_id=1, source_target_pairs={{0,1},{1,0},{2,3},{3,2},{4,5},{5,4},{6,7},{7,6},{8,9},{9,8},{10,11... | collective-permute-start | bytes 909320 | tf_op jit(solution)/shard_map/ppermute | solution.py:349
  16.7 1.6 %collective-permute-start.7 = (bf16[1184,128]{1,0:T(8,128)(2,1)S(1)}, bf16[1184,128]{1,0:T(8,128)(2,1)S(1)}, u32[]{:S(2)}, u32[]{:S(2)}) collective-permute-start(bf16[1184,128]{1,0:T(8,128)(2,1)S(1)} %far_forward.1), channel_id=1, source_target_pairs={{0,4},{1,5},{2,0},{3,1},{4,6},{5,7},{6,2},{7,3},{8,12},{9,13},{10,... | collective-permute-start | bytes 909320 | tf_op jit(solution)/shard_map/ppermute | solution.py:349
  18.4 0.2 collective-permute-done.3.side
  18.6 0.4 %swap.1 = bf16[7808,128]{1,0:T(8,128)(2,1)S(1)} custom-call(bf16[1184,128]{1,0:T(8,128)(2,1)S(1)} %merge.1.ordered_after.own, bf16[1184,128]{1,0:T(8,128)(2,1)S(1)} %collective-permute-done.3.side, bf16[1184,128]{1,0:T(8,128)(2,1)S(1)} %collective-permute-done.4.pair.ordered_after, bf16[1184,128]{1,0:T(8,128)(2,1)S(1)} %collective-permute-done.5.cross.ordered_after, ...), custom_call_target="tpu_custom_call" | custom-call | tf_op jit(solution)/shard_map/swap/pallas_call | solution.py:343
  19.0 0.1 collective-permute-start.6
  19.1 0.4 %own.1.ordered_after.partial = f32[512,256]{1,0:T(8,128)S(1)} custom-call(bf16[768,256]{1,0:T(8,128)(2,1)S(1)} %get-tuple-element.13.own_first, bf16[768,256]{1,0:T(8,128)(2,1)S(1)} %get-tuple-element.14.own_second, bf16[7808,128]{1,0:T(8,128)(2,1)S(1)} %swap.1, bf16[1184,128]{1,0:T(8,128)(2,1)S(1)} %collective-permute-done.3.side), custom_call_target="tpu_custom_call" | custom-call | tf_op jit(solution)/shard_map/own/pallas_call | solution.py:343
  19.5 3.5 %collective-permute-done.2.ref = bf16[784,256]{1,0:T(8,128)(2,1)S(1)} collective-permute-done((bf16[784,256]{1,0:T(8,128)(2,1)S(1)}, bf16[784,256]{1,0:T(8,128)(2,1)S(1)}, u32[]{:S(2)}, u32[]{:S(2)}) %collective-permute-start.2) | collective-permute-done | bytes 401440 | tf_op jit(solution)/shard_map/ppermute | solution.py:349
  23.0 1.3 %collective-permute-done.9.ref.diag = bf16[1184,128]{1,0:T(8,128)(2,1)S(1)} collective-permute-done((bf16[1184,128]{1,0:T(8,128)(2,1)S(1)}, bf16[1184,128]{1,0:T(8,128)(2,1)S(1)}, u32[]{:S(2)}, u32[]{:S(2)}) %collective-permute-start.9) | collective-permute-done | bytes 303136 | tf_op jit(solution)/shard_map/ppermute | solution.py:349
  24.4 0.1 collective-permute-start.10
  24.5 0.4 %collective-permute-done.7.ref.far = bf16[1184,128]{1,0:T(8,128)(2,1)S(1)} collective-permute-done((bf16[1184,128]{1,0:T(8,128)(2,1)S(1)}, bf16[1184,128]{1,0:T(8,128)(2,1)S(1)}, u32[]{:S(2)}, u32[]{:S(2)}) %collective-permute-start.7) | collective-permute-done | bytes 303136 | tf_op jit(solution)/shard_map/ppermute | solution.py:349
  24.9 0.1 collective-permute-start.8
  25.1 1.0 %near.1.partial = f32[512,256]{1,0:T(8,128)S(1)} custom-call(bf16[768,256]{1,0:T(8,128)(2,1)S(1)} %get-tuple-element.13.own_first, bf16[768,256]{1,0:T(8,128)(2,1)S(1)} %get-tuple-element.14.own_second, bf16[768,256]{1,0:T(8,128)(2,1)S(1)} %settle_first.1.far_first, bf16[768,256]{1,0:T(8,128)(2,1)S(1)} %settle.1.ordered_after.far_second, ...), custom_call_target="tpu_custom_call" | custom-call | tf_op jit(solution)/shard_map/near/pallas_call | solution.py:343
  26.1 0.4 %diagonal.1.partial = f32[512,256]{1,0:T(8,128)S(1)} custom-call(bf16[768,256]{1,0:T(8,128)(2,1)S(1)} %get-tuple-element.13.own_first, bf16[768,256]{1,0:T(8,128)(2,1)S(1)} %get-tuple-element.14.own_second, bf16[768,256]{1,0:T(8,128)(2,1)S(1)} %settle_first.1.far_first, bf16[768,256]{1,0:T(8,128)(2,1)S(1)} %settle.1.ordered_after.far_second, ...), custom_call_target="tpu_custom_call" | custom-call | tf_op jit(solution)/shard_map/diagonal/pallas_call | solution.py:343
  26.5 0.1 collective-permute-done.8.far_last
  26.6 1.1 %last.1 = f32[512,256]{1,0:T(8,128)} custom-call(bf16[768,256]{1,0:T(8,128)(2,1)S(1)} %get-tuple-element.13.own_first, bf16[768,256]{1,0:T(8,128)(2,1)S(1)} %get-tuple-element.14.own_second, bf16[768,256]{1,0:T(8,128)(2,1)S(1)} %settle_first.1.far_first, bf16[768,256]{1,0:T(8,128)(2,1)S(1)} %settle.1.ordered_after.far_second, ...), custom_call_target="tpu_custom_call" | custom-call | tf_op jit(solution)/shard_map/last/pallas_call | solution.py:419
  (12 shorter events, 0.2 us)
Async XLA Ops:
  1.5 3.1 %collective-permute-start.1 = (bf16[1168,128]{1,0:T(8,128)(2,1)S(1)}, bf16[1168,128]{1,0:T(8,128)(2,1)S(1)}, u32[]{:S(2)}, u32[]{:S(2)}) collective-permute-start(bf16[1168,128]{1,0:T(8,128)(2,1)S(1)} %get-tuple-element.16), channel_id=1, source_target_pairs={{0,8},{1,9},{2,10},{3,11},{4,12},{5,13},{6,14},{7,15},{8,0},{9,1},... | collective-permute-start | bytes 897032 | tf_op jit(solution)/shard_map/ppermute | solution.py:349
  1.9 16.4 %collective-permute-start = (bf16[784,256]{1,0:T(8,128)(2,1)S(1)}, bf16[784,256]{1,0:T(8,128)(2,1)S(1)}, u32[]{:S(2)}, u32[]{:S(2)}) collective-permute-start(bf16[784,256]{1,0:T(8,128)(2,1)S(1)} %get-tuple-element.11.first_ref), channel_id=1, source_target_pairs={{0,16},{1,17},{2,18},{3,19},{4,20},{5,21},{6,22},{7,23},{8,24},{9,... | collective-permute-start | bytes 1204232 | tf_op jit(solution)/shard_map/ppermute | solution.py:349
  4.6 6.4 %collective-permute-start.5 = (bf16[1184,128]{1,0:T(8,128)(2,1)S(1)}, bf16[1184,128]{1,0:T(8,128)(2,1)S(1)}, u32[]{:S(2)}, u32[]{:S(2)}) collective-permute-start(bf16[1184,128]{1,0:T(8,128)(2,1)S(1)} %merge.1.ordered_after.own), channel_id=1, source_target_pairs={{0,8},{1,9},{2,4},{3,5},{4,2},{5,3},{6,14},{7,15},{8,0},{9,1},{10,... | collective-permute-start | bytes 909320 | tf_op jit(solution)/shard_map/ppermute | solution.py:349
  4.8 10.3 %collective-permute-start.4 = (bf16[1184,128]{1,0:T(8,128)(2,1)S(1)}, bf16[1184,128]{1,0:T(8,128)(2,1)S(1)}, u32[]{:S(2)}, u32[]{:S(2)}) collective-permute-start(bf16[1184,128]{1,0:T(8,128)(2,1)S(1)} %merge.1.ordered_after.own), channel_id=1, source_target_pairs={{0,2},{1,3},{2,0},{3,1},{4,6},{5,7},{6,4},{7,5},{8,10},{9,11},{10,... | collective-permute-start | bytes 909320 | tf_op jit(solution)/shard_map/ppermute | solution.py:349
  7.9 15.1 %collective-permute-start.2 = (bf16[784,256]{1,0:T(8,128)(2,1)S(1)}, bf16[784,256]{1,0:T(8,128)(2,1)S(1)}, u32[]{:S(2)}, u32[]{:S(2)}) collective-permute-start(bf16[784,256]{1,0:T(8,128)(2,1)S(1)} %get-tuple-element.12.second_ref), channel_id=1, source_target_pairs={{0,16},{1,17},{2,18},{3,19},{4,20},{5,21},{6,22},{7,23},{8,24},{9,... | collective-permute-start | bytes 1204232 | tf_op jit(solution)/shard_map/ppermute | solution.py:349
  9.4 9.1 %collective-permute-start.3 = (bf16[1184,128]{1,0:T(8,128)(2,1)S(1)}, bf16[1184,128]{1,0:T(8,128)(2,1)S(1)}, u32[]{:S(2)}, u32[]{:S(2)}) collective-permute-start(bf16[1184,128]{1,0:T(8,128)(2,1)S(1)} %merge.1.ordered_after.own), channel_id=1, source_target_pairs={{0,1},{1,0},{2,3},{3,2},{4,5},{5,4},{6,7},{7,6},{8,9},{9,8},{10,11... | collective-permute-start | bytes 909320 | tf_op jit(solution)/shard_map/ppermute | solution.py:349
  15.1 9.3 %collective-permute-start.9 = (bf16[1184,128]{1,0:T(8,128)(2,1)S(1)}, bf16[1184,128]{1,0:T(8,128)(2,1)S(1)}, u32[]{:S(2)}, u32[]{:S(2)}) collective-permute-start(bf16[1184,128]{1,0:T(8,128)(2,1)S(1)} %diagonal_forward.1.ordered_after), channel_id=1, source_target_pairs={{0,1},{1,0},{2,3},{3,2},{4,5},{5,4},{6,7},{7,6},{8,9},{9,8},{10,11... | collective-permute-start | bytes 909320 | tf_op jit(solution)/shard_map/ppermute | solution.py:349
  16.7 8.2 %collective-permute-start.7 = (bf16[1184,128]{1,0:T(8,128)(2,1)S(1)}, bf16[1184,128]{1,0:T(8,128)(2,1)S(1)}, u32[]{:S(2)}, u32[]{:S(2)}) collective-permute-start(bf16[1184,128]{1,0:T(8,128)(2,1)S(1)} %far_forward.1), channel_id=1, source_target_pairs={{0,4},{1,5},{2,0},{3,1},{4,6},{5,7},{6,2},{7,3},{8,12},{9,13},{10,... | collective-permute-start | bytes 909320 | tf_op jit(solution)/shard_map/ppermute | solution.py:349
  19.0 6.0 %collective-permute-start.6 = (bf16[7808,128]{1,0:T(8,128)(2,1)S(1)}, bf16[7808,128]{1,0:T(8,128)(2,1)S(1)}, u32[]{:S(2)}, u32[]{:S(2)}) collective-permute-start(bf16[7808,128]{1,0:T(8,128)(2,1)S(1)} %swap.1), channel_id=1, source_target_pairs={{0,8},{1,9},{2,10},{3,11},{4,12},{5,13},{6,14},{7,15},{8,0},{9,1},... | collective-permute-start | bytes 5996552 | tf_op jit(solution)/shard_map/ppermute | solution.py:349
  24.4 1.7 %collective-permute-start.10 = (bf16[1184,128]{1,0:T(8,128)(2,1)S(1)}, bf16[1184,128]{1,0:T(8,128)(2,1)S(1)}, u32[]{:S(2)}, u32[]{:S(2)}) collective-permute-start(bf16[1184,128]{1,0:T(8,128)(2,1)S(1)} %pass_diagonal.1), channel_id=1, source_target_pairs={{0,8},{1,9},{2,10},{3,11},{4,12},{5,13},{6,14},{7,15},{8,0},{9,1},... | collective-permute-start | bytes 909320 | tf_op jit(solution)/shard_map/ppermute | solution.py:349
  24.9 1.7 %collective-permute-start.8 = (bf16[1184,128]{1,0:T(8,128)(2,1)S(1)}, bf16[1184,128]{1,0:T(8,128)(2,1)S(1)}, u32[]{:S(2)}, u32[]{:S(2)}) collective-permute-start(bf16[1184,128]{1,0:T(8,128)(2,1)S(1)} %pass_far.1), channel_id=1, source_target_pairs={{0,8},{1,9},{2,10},{3,11},{4,12},{5,13},{6,14},{7,15},{8,0},{9,1},... | collective-permute-start | bytes 909320 | tf_op jit(solution)/shard_map/ppermute | solution.py:349

commit v7 on v6

--- a/solution.py
+++ b/solution.py
@@ -10,6 +10,7 @@
 TILE = 128
 AXES = ("row", "col")
 LAST_WEIGHT, FIRST_WEIGHT = 20, 5
+DIAGONAL_FIRST = 0
 SLOTS = 3
 META = 16
 MAINS, NEARS, FARS = (0, 1), (2, 3), (4, 5)
@@ -142,28 +143,27 @@
     half_ref[pl.ds(size + META, META), :] = jnp.where(odd, mine, theirs)
 
 
-def far_forward_kernel(cols, own, cross, ordered_after, out_ref):
-    c = lax.axis_index("col")
+def late_kind(step, odd):
+    return DIAG if odd == (DIAGONAL_FIRST != step) else FAR
+
+
+def forward_kernel(cols, step, own, pair, cross, ordered_after, out_ref):
+    row_odd, c = lax.axis_index("row") % 2 == 1, lax.axis_index("col")
+    diagonal = row_odd == (late_kind(step, True) == DIAG)
+    by_pair = (c % 2 == 0) == ((c // 2) % 2 == 0)
     inner = (cols == 8) & (c >= 2) & (c < 6)
-
-    @pl.when(inner)
+    from_pair = diagonal & by_pair
+    from_own = jnp.logical_not(diagonal | inner)
+
+    @pl.when(from_pair)
     def _():
-        out_ref[...] = cross[...]
-
-    @pl.when(jnp.logical_not(inner))
+        out_ref[...] = pair[...]
+
+    @pl.when(from_own)
     def _():
         out_ref[...] = own[...]
 
-
-def diagonal_forward_kernel(pair, cross, ordered_after, out_ref):
-    c = lax.axis_index("col")
-    by_pair = (c % 2 == 0) == ((c // 2) % 2 == 0)
-
-    @pl.when(by_pair)
-    def _():
-        out_ref[...] = pair[...]
-
-    @pl.when(jnp.logical_not(by_pair))
+    @pl.when(jnp.logical_not(from_pair | from_own))
     def _():
         out_ref[...] = cross[...]
 
@@ -267,8 +267,8 @@
     by_parity(body)
 
 
-def near_kernel(cols, half, width, own_first, own_second, far_first, far_second, swapped, cross_ap, swap, diag, far, partial, c_ref):
-    size = far.shape[0]
+def near_kernel(cols, half, width, own_first, own_second, far_first, far_second, swapped, cross_ap, swap, late_first, late_second, partial, c_ref):
+    size = late_first.shape[0]
     read = lambda name, m, odd: read_applied(
         name, m, odd, half, size, (own_first, own_second), (far_first, far_second), swapped, cross_ap
     )
@@ -279,7 +279,10 @@
         lhs = jnp.concatenate([units(name, theirs, range(width)) for name in MAINS], axis=1)
         rhs = jnp.concatenate([read(name, theirs, odd) for name in MAINS], axis=0)
         c_ref[...] = partial[...] + product(lhs, rhs, True)
-        late = [kind_units(cols, half, width, odd, read, kind, ref, mine) for kind, ref in ((DIAG, diag), (FAR, far))]
+        late = [
+            kind_units(cols, half, width, odd, read, late_kind(step, odd), ref, mine)
+            for step, ref in enumerate((late_first, late_second))
+        ]
         lhs, rhs = (jnp.concatenate(x, axis=0) for x in zip(*late))
         c_ref[...] += product(lhs, rhs, False)
         for name in NEARS:
@@ -294,26 +297,26 @@
     by_parity(body)
 
 
-def diagonal_kernel(cols, half, width, own_first, own_second, far_first, far_second, swapped, cross_ap, diag_last, partial, c_ref):
-    size = diag_last.shape[0]
+def late_kernel(cols, half, width, own_first, own_second, far_first, far_second, swapped, cross_ap, late_first, partial, c_ref):
+    size = late_first.shape[0]
     read = lambda name, m, odd: read_applied(
         name, m, odd, half, size, (own_first, own_second), (far_first, far_second), swapped, cross_ap
     )
 
     def body(odd):
-        c_ref[...] = partial[...] + product(*kind_units(cols, half, width, odd, read, DIAG, diag_last, 1 - int(odd)), False)
+        c_ref[...] = partial[...] + product(*kind_units(cols, half, width, odd, read, late_kind(0, not odd), late_first, 1 - int(odd)), False)
 
     by_parity(body)
 
 
-def last_kernel(cols, half, width, own_first, own_second, far_first, far_second, swapped, cross_ap, far_last, partial, out_hbm, c_ref, sems):
-    size = far_last.shape[0]
+def last_kernel(cols, half, width, own_first, own_second, far_first, far_second, swapped, cross_ap, late_second, partial, out_hbm, c_ref, sems):
+    size = late_second.shape[0]
     read = lambda name, m, odd: read_applied(
         name, m, odd, half, size, (own_first, own_second), (far_first, far_second), swapped, cross_ap
     )
 
     def body(odd):
-        units, ap = kind_units(cols, half, width, odd, read, FAR, far_last, 1 - int(odd))
+        units, ap = kind_units(cols, half, width, odd, read, late_kind(1, not odd), late_second, 1 - int(odd))
         copies = []
         for i in range(width):
             rows = pl.ds(i * TILE, TILE)
@@ -386,12 +389,17 @@
         far_pairs = [(0, 4), (1, 5), (2, 0), (3, 1), (4, 6), (5, 7), (6, 2), (7, 3)]
     else:
         far_pairs = [(c, (c + cols // 2) % cols) for c in range(cols)]
-    diag_send = call(diagonal_forward_kernel, "diagonal_forward", shape(size, TILE), pair, cross, pair)
-    diag = move(diag_send, col_pairs([(c, c ^ 1) for c in range(cols)]))
-    far_send = call(
-        functools.partial(far_forward_kernel, cols), "far_forward", shape(size, TILE), mine, cross, cross
-    )
-    far = move(far_send, col_pairs(far_pairs))
+    def relay_pairs(step):
+        pairs = {DIAG: [(c, c ^ 1) for c in range(cols)], FAR: far_pairs}
+        return [(r * cols + a, r * cols + b) for r in range(rows) for a, b in pairs[late_kind(step, r % 2 == 1)]]
+
+    late, after = [], cross
+    for step in range(2):
+        send_on = call(
+            functools.partial(forward_kernel, cols, step), "forward", shape(size, TILE), mine, pair, cross, after
+        )
+        late.append(move(send_on, relay_pairs(step)))
+        after = send_on
     own_first, own_second = call(mask_own_kernel, "mask_own", (half_ap,) * 2, raw_first, raw_second)
     far_first = call(mask_kernel, "settle_first", half_ap, far_first, mine, weight=FIRST_WEIGHT)
     swap = call(
@@ -402,8 +410,8 @@
     sizes = (cols, half, width)
     partial = call(functools.partial(own_kernel, *sizes), "own", result, own_first, own_second, swap, side)
     far_second = call(mask_kernel, "settle", half_ap, far_second, partial)
-    diag_last = move(call(pass_kernel, "pass_diagonal", shape(size, TILE), diag, diag_send), partner)
-    far_last = move(call(pass_kernel, "pass_far", shape(size, TILE), far, far_second, weight=LAST_WEIGHT), partner)
+    late_first = move(call(pass_kernel, "pass_late", shape(size, TILE), late[0], mine), partner)
+    late_second = move(call(pass_kernel, "pass_late", shape(size, TILE), late[1], far_second, weight=LAST_WEIGHT), partner)
     beyond = [(r, r + 1 if r % 2 == 1 else r - 1) for r in range(rows)]
     relay = [((r + rows // 2) % rows, t) for r, t in beyond if 0 <= t < rows]
     if all(h ^ 1 == t for h, t in relay):
@@ -413,9 +421,9 @@
         cross_ap = move(first, row_pairs([(r, t) for r, t in beyond if 0 <= t < rows]))
 
     aps = (own_first, own_second, far_first, far_second, swapped, cross_ap)
-    partial = call(functools.partial(near_kernel, *sizes), "near", result, *aps, swap, diag, far, partial)
-    partial = call(functools.partial(diagonal_kernel, *sizes), "diagonal", result, *aps, diag_last, partial)
-    operands = (*aps, far_last, partial)
+    partial = call(functools.partial(near_kernel, *sizes), "near", result, *aps, swap, *late, partial)
+    partial = call(functools.partial(late_kernel, *sizes), "late", result, *aps, late_first, partial)
+    operands = (*aps, late_second, partial)
     return pl.pallas_call(
         functools.partial(last_kernel, *sizes), out_shape=result, in_specs=[vmem] * len(operands), out_specs=hbm,
         compiler_params=params, name="last",

time: 27.9 us -> 26.8 us (0.961)
  waiting for transfers between devices: 9.65 us -> 7.79 us
  starting transfers between devices: 12.9 us -> 13.5 us
    ppermute x11, waiting for transfers between devices: 9.65 us -> 7.79 us  [move(): return lax.ppermute(x, AXES, pairs)]
    ppermute x11, starting transfers between devices: 12.9 us -> 13.5 us  [move(): return lax.ppermute(x, AXES, pairs)]
  transfers between devices with their start and end apart: 11 -> 11, of which waited for: 6 -> 3; matrix products, arithmetic and copies ran while one was open for 0% -> 0% of each run, Pallas kernels for 9% -> 10%
where the time goes in v7:
time: 26.8 us; the launch traced here: 26.6 us
  starting transfers between devices  13.5 us (50%)
  waiting for transfers between devices  7.79 us (29%)
  Pallas kernels  5.14 us (19%)
    ppermute x11, starting transfers between devices, move(): return lax.ppermute(x, AXES, pairs)  13.5 us
    ppermute x11, waiting for transfers between devices, move(): return lax.ppermute(x, AXES, pairs)  7.79 us
    pallas_call x13, Pallas kernels, call(): pl.pallas_call(kernel, out_shape=out_shape, in_specs=specs or [vmem] * le...  4 us
    pallas_call x1, Pallas kernels, on_device(): pl.pallas_call(functools.partial(last_kernel, *sizes), out_shape=result,...  1.13 us
  transfers between devices with their start and end apart: 11, of which 3 were waited for; matrix products, arithmetic and copies ran while one was open for 0% of the time, Pallas kernels for 10%

profile of v7, /device:TPU:0, one launch (start us, length us, event | category | flops | bytes accessed | tf_op | source)
XLA Modules:
  0.0 26.6 jit_solution(2790552616045589338)
XLA Ops:
  0.0 1.5 %prepare.1 = (bf16[1168,128]{1,0:T(8,128)(2,1)S(1)}, bf16[1168,128]{1,0:T(8,128)(2,1)S(1)}, bf16[784,256]{1,0:T(8,128)(2,1)S(1)}, bf16[784,256]{1,0:T(8,128)(2,1)S(1)}) custom-call(bf16[768,512]{1,0:T(8,128)(2,1)} %p_hbm.1, bf16[1536,256]{1,0:T(8,128)(2,1)} %ap_hbm.1, s32[4,6]{1,0:T(4,128)} %bitcast.2, s32[2,12]{1,0:T(2,128)} %bitcast.3), custom_call_target="tpu_custom_call" | custom-call | tf_op jit(solution)/shard_map/prepare/pallas_call | solution.py:346
  1.5 0.4 %collective-permute-start.1 = (bf16[1168,128]{1,0:T(8,128)(2,1)S(1)}, bf16[1168,128]{1,0:T(8,128)(2,1)S(1)}, u32[]{:S(2)}, u32[]{:S(2)}) collective-permute-start(bf16[1168,128]{1,0:T(8,128)(2,1)S(1)} %get-tuple-element.16), channel_id=1, source_target_pairs={{0,8},{1,9},{2,10},{3,11},{4,12},{5,13},{6,14},{7,15},{8,0},{9,1},... | collective-permute-start | bytes 897032 | tf_op jit(solution)/shard_map/ppermute | solution.py:352
  1.9 2.6 %collective-permute-start = (bf16[784,256]{1,0:T(8,128)(2,1)S(1)}, bf16[784,256]{1,0:T(8,128)(2,1)S(1)}, u32[]{:S(2)}, u32[]{:S(2)}) collective-permute-start(bf16[784,256]{1,0:T(8,128)(2,1)S(1)} %get-tuple-element.11.first_ref), channel_id=1, source_target_pairs={{0,16},{1,17},{2,18},{3,19},{4,20},{5,21},{6,22},{7,23},{8,24},{9,... | collective-permute-start | bytes 1204232 | tf_op jit(solution)/shard_map/ppermute | solution.py:352
  4.5 0.0 collective-permute-done.1.got_ref
  4.5 0.1 merge.1.ordered_after.own
  4.6 1.6 %collective-permute-start.4 = (bf16[1184,128]{1,0:T(8,128)(2,1)S(1)}, bf16[1184,128]{1,0:T(8,128)(2,1)S(1)}, u32[]{:S(2)}, u32[]{:S(2)}) collective-permute-start(bf16[1184,128]{1,0:T(8,128)(2,1)S(1)} %merge.1.ordered_after.own), channel_id=1, source_target_pairs={{0,2},{1,3},{2,0},{3,1},{4,6},{5,7},{6,4},{7,5},{8,10},{9,11},{10,... | collective-permute-start | bytes 909320 | tf_op jit(solution)/shard_map/ppermute | solution.py:352
  6.2 0.0 collective-permute-start.5
  6.2 1.5 %collective-permute-start.2 = (bf16[784,256]{1,0:T(8,128)(2,1)S(1)}, bf16[784,256]{1,0:T(8,128)(2,1)S(1)}, u32[]{:S(2)}, u32[]{:S(2)}) collective-permute-start(bf16[784,256]{1,0:T(8,128)(2,1)S(1)} %get-tuple-element.12.second_ref), channel_id=1, source_target_pairs={{0,16},{1,17},{2,18},{3,19},{4,20},{5,21},{6,22},{7,23},{8,24},{9,... | collective-permute-start | bytes 1204232 | tf_op jit(solution)/shard_map/ppermute | solution.py:352
  7.7 0.1 mask_own.1
  7.8 1.6 %collective-permute-start.3 = (bf16[1184,128]{1,0:T(8,128)(2,1)S(1)}, bf16[1184,128]{1,0:T(8,128)(2,1)S(1)}, u32[]{:S(2)}, u32[]{:S(2)}) collective-permute-start(bf16[1184,128]{1,0:T(8,128)(2,1)S(1)} %merge.1.ordered_after.own), channel_id=1, source_target_pairs={{0,1},{1,0},{2,3},{3,2},{4,5},{5,4},{6,7},{7,6},{8,9},{9,8},{10,11... | collective-permute-start | bytes 909320 | tf_op jit(solution)/shard_map/ppermute | solution.py:352
  9.4 4.5 %collective-permute-done.4.pair = bf16[1184,128]{1,0:T(8,128)(2,1)S(1)} collective-permute-done((bf16[1184,128]{1,0:T(8,128)(2,1)S(1)}, bf16[1184,128]{1,0:T(8,128)(2,1)S(1)}, u32[]{:S(2)}, u32[]{:S(2)}) %collective-permute-start.4) | collective-permute-done | bytes 303136 | tf_op jit(solution)/shard_map/ppermute | solution.py:352
  14.0 1.6 %collective-permute-start.9 = (bf16[1184,128]{1,0:T(8,128)(2,1)S(1)}, bf16[1184,128]{1,0:T(8,128)(2,1)S(1)}, u32[]{:S(2)}, u32[]{:S(2)}) collective-permute-start(bf16[1184,128]{1,0:T(8,128)(2,1)S(1)} %forward.2.ordered_after), channel_id=1, source_target_pairs={{0,1},{1,0},{2,3},{3,2},{4,5},{5,4},{6,7},{7,6},{8,12},{9,13},{10,... | collective-permute-start | bytes 909320 | tf_op jit(solution)/shard_map/ppermute | solution.py:352
  15.5 3.9 %collective-permute-start.7 = (bf16[1184,128]{1,0:T(8,128)(2,1)S(1)}, bf16[1184,128]{1,0:T(8,128)(2,1)S(1)}, u32[]{:S(2)}, u32[]{:S(2)}) collective-permute-start(bf16[1184,128]{1,0:T(8,128)(2,1)S(1)} %forward.3), channel_id=1, source_target_pairs={{0,4},{1,5},{2,0},{3,1},{4,6},{5,7},{6,2},{7,3},{8,9},{9,8},{10,11... | collective-permute-start | bytes 909320 | tf_op jit(solution)/shard_map/ppermute | solution.py:352
  19.5 0.4 %swap.1 = bf16[7808,128]{1,0:T(8,128)(2,1)S(1)} custom-call(bf16[1184,128]{1,0:T(8,128)(2,1)S(1)} %merge.1.ordered_after.own, bf16[1184,128]{1,0:T(8,128)(2,1)S(1)} %collective-permute-done.3.side, bf16[1184,128]{1,0:T(8,128)(2,1)S(1)} %collective-permute-done.4.pair, bf16[1184,128]{1,0:T(8,128)(2,1)S(1)} %collective-permute-done.5.cross.ordered_after, ...), custom_call_target="tpu_custom_call" | custom-call | tf_op jit(solution)/shard_map/swap/pallas_call | solution.py:346
  19.9 0.1 collective-permute-start.6
  20.0 0.4 %own.1.ordered_after.partial = f32[512,256]{1,0:T(8,128)S(1)} custom-call(bf16[768,256]{1,0:T(8,128)(2,1)S(1)} %get-tuple-element.13.own_first, bf16[768,256]{1,0:T(8,128)(2,1)S(1)} %get-tuple-element.14.own_second, bf16[7808,128]{1,0:T(8,128)(2,1)S(1)} %swap.1, bf16[1184,128]{1,0:T(8,128)(2,1)S(1)} %collective-permute-done.3.side), custom_call_target="tpu_custom_call" | custom-call | tf_op jit(solution)/shard_map/own/pallas_call | solution.py:346
  20.4 2.6 %collective-permute-done.2.ref = bf16[784,256]{1,0:T(8,128)(2,1)S(1)} collective-permute-done((bf16[784,256]{1,0:T(8,128)(2,1)S(1)}, bf16[784,256]{1,0:T(8,128)(2,1)S(1)}, u32[]{:S(2)}, u32[]{:S(2)}) %collective-permute-start.2) | collective-permute-done | bytes 401440 | tf_op jit(solution)/shard_map/ppermute | solution.py:352
  23.1 0.1 collective-permute-start.10
  23.2 0.6 %collective-permute-done.7.ref.late_second = bf16[1184,128]{1,0:T(8,128)(2,1)S(1)} collective-permute-done((bf16[1184,128]{1,0:T(8,128)(2,1)S(1)}, bf16[1184,128]{1,0:T(8,128)(2,1)S(1)}, u32[]{:S(2)}, u32[]{:S(2)}) %collective-permute-start.7) | collective-permute-done | bytes 303136 | tf_op jit(solution)/shard_map/ppermute | solution.py:352
  23.8 0.2 collective-permute-start.8
  24.0 0.0 collective-permute-done.6.swapped.cross_ap
  24.0 1.0 %near.1.partial = f32[512,256]{1,0:T(8,128)S(1)} custom-call(bf16[768,256]{1,0:T(8,128)(2,1)S(1)} %get-tuple-element.13.own_first, bf16[768,256]{1,0:T(8,128)(2,1)S(1)} %get-tuple-element.14.own_second, bf16[768,256]{1,0:T(8,128)(2,1)S(1)} %settle_first.1.far_first, bf16[768,256]{1,0:T(8,128)(2,1)S(1)} %settle.1.ordered_after.far_second, ...), custom_call_target="tpu_custom_call" | custom-call | tf_op jit(solution)/shard_map/near/pallas_call | solution.py:346
  25.1 0.4 %late.1.partial = f32[512,256]{1,0:T(8,128)S(1)} custom-call(bf16[768,256]{1,0:T(8,128)(2,1)S(1)} %get-tuple-element.13.own_first, bf16[768,256]{1,0:T(8,128)(2,1)S(1)} %get-tuple-element.14.own_second, bf16[768,256]{1,0:T(8,128)(2,1)S(1)} %settle_first.1.far_first, bf16[768,256]{1,0:T(8,128)(2,1)S(1)} %settle.1.ordered_after.far_second, ...), custom_call_target="tpu_custom_call" | custom-call | tf_op jit(solution)/shard_map/late/pallas_call | solution.py:346
  25.5 1.1 %last.1 = f32[512,256]{1,0:T(8,128)} custom-call(bf16[768,256]{1,0:T(8,128)(2,1)S(1)} %get-tuple-element.13.own_first, bf16[768,256]{1,0:T(8,128)(2,1)S(1)} %get-tuple-element.14.own_second, bf16[768,256]{1,0:T(8,128)(2,1)S(1)} %settle_first.1.far_first, bf16[768,256]{1,0:T(8,128)(2,1)S(1)} %settle.1.ordered_after.far_second, ...), custom_call_target="tpu_custom_call" | custom-call | tf_op jit(solution)/shard_map/last/pallas_call | solution.py:427
  (12 shorter events, 0.2 us)
Async XLA Ops:
  1.5 3.1 %collective-permute-start.1 = (bf16[1168,128]{1,0:T(8,128)(2,1)S(1)}, bf16[1168,128]{1,0:T(8,128)(2,1)S(1)}, u32[]{:S(2)}, u32[]{:S(2)}) collective-permute-start(bf16[1168,128]{1,0:T(8,128)(2,1)S(1)} %get-tuple-element.16), channel_id=1, source_target_pairs={{0,8},{1,9},{2,10},{3,11},{4,12},{5,13},{6,14},{7,15},{8,0},{9,1},... | collective-permute-start | bytes 897032 | tf_op jit(solution)/shard_map/ppermute | solution.py:352
  1.9 17.5 %collective-permute-start = (bf16[784,256]{1,0:T(8,128)(2,1)S(1)}, bf16[784,256]{1,0:T(8,128)(2,1)S(1)}, u32[]{:S(2)}, u32[]{:S(2)}) collective-permute-start(bf16[784,256]{1,0:T(8,128)(2,1)S(1)} %get-tuple-element.11.first_ref), channel_id=1, source_target_pairs={{0,16},{1,17},{2,18},{3,19},{4,20},{5,21},{6,22},{7,23},{8,24},{9,... | collective-permute-start | bytes 1204232 | tf_op jit(solution)/shard_map/ppermute | solution.py:352
  4.6 9.3 %collective-permute-start.4 = (bf16[1184,128]{1,0:T(8,128)(2,1)S(1)}, bf16[1184,128]{1,0:T(8,128)(2,1)S(1)}, u32[]{:S(2)}, u32[]{:S(2)}) collective-permute-start(bf16[1184,128]{1,0:T(8,128)(2,1)S(1)} %merge.1.ordered_after.own), channel_id=1, source_target_pairs={{0,2},{1,3},{2,0},{3,1},{4,6},{5,7},{6,4},{7,5},{8,10},{9,11},{10,... | collective-permute-start | bytes 909320 | tf_op jit(solution)/shard_map/ppermute | solution.py:352
  6.2 7.7 %collective-permute-start.5 = (bf16[1184,128]{1,0:T(8,128)(2,1)S(1)}, bf16[1184,128]{1,0:T(8,128)(2,1)S(1)}, u32[]{:S(2)}, u32[]{:S(2)}) collective-permute-start(bf16[1184,128]{1,0:T(8,128)(2,1)S(1)} %merge.1.ordered_after.own), channel_id=1, source_target_pairs={{0,8},{1,9},{2,4},{3,5},{4,2},{5,3},{6,14},{7,15},{8,0},{9,1},{10,... | collective-permute-start | bytes 909320 | tf_op jit(solution)/shard_map/ppermute | solution.py:352
  6.2 16.8 %collective-permute-start.2 = (bf16[784,256]{1,0:T(8,128)(2,1)S(1)}, bf16[784,256]{1,0:T(8,128)(2,1)S(1)}, u32[]{:S(2)}, u32[]{:S(2)}) collective-permute-start(bf16[784,256]{1,0:T(8,128)(2,1)S(1)} %get-tuple-element.12.second_ref), channel_id=1, source_target_pairs={{0,16},{1,17},{2,18},{3,19},{4,20},{5,21},{6,22},{7,23},{8,24},{9,... | collective-permute-start | bytes 1204232 | tf_op jit(solution)/shard_map/ppermute | solution.py:352
  7.8 11.7 %collective-permute-start.3 = (bf16[1184,128]{1,0:T(8,128)(2,1)S(1)}, bf16[1184,128]{1,0:T(8,128)(2,1)S(1)}, u32[]{:S(2)}, u32[]{:S(2)}) collective-permute-start(bf16[1184,128]{1,0:T(8,128)(2,1)S(1)} %merge.1.ordered_after.own), channel_id=1, source_target_pairs={{0,1},{1,0},{2,3},{3,2},{4,5},{5,4},{6,7},{7,6},{8,9},{9,8},{10,11... | collective-permute-start | bytes 909320 | tf_op jit(solution)/shard_map/ppermute | solution.py:352
  14.0 9.1 %collective-permute-start.9 = (bf16[1184,128]{1,0:T(8,128)(2,1)S(1)}, bf16[1184,128]{1,0:T(8,128)(2,1)S(1)}, u32[]{:S(2)}, u32[]{:S(2)}) collective-permute-start(bf16[1184,128]{1,0:T(8,128)(2,1)S(1)} %forward.2.ordered_after), channel_id=1, source_target_pairs={{0,1},{1,0},{2,3},{3,2},{4,5},{5,4},{6,7},{7,6},{8,12},{9,13},{10,... | collective-permute-start | bytes 909320 | tf_op jit(solution)/shard_map/ppermute | solution.py:352
  15.5 8.2 %collective-permute-start.7 = (bf16[1184,128]{1,0:T(8,128)(2,1)S(1)}, bf16[1184,128]{1,0:T(8,128)(2,1)S(1)}, u32[]{:S(2)}, u32[]{:S(2)}) collective-permute-start(bf16[1184,128]{1,0:T(8,128)(2,1)S(1)} %forward.3), channel_id=1, source_target_pairs={{0,4},{1,5},{2,0},{3,1},{4,6},{5,7},{6,2},{7,3},{8,9},{9,8},{10,11... | collective-permute-start | bytes 909320 | tf_op jit(solution)/shard_map/ppermute | solution.py:352
  19.9 4.1 %collective-permute-start.6 = (bf16[7808,128]{1,0:T(8,128)(2,1)S(1)}, bf16[7808,128]{1,0:T(8,128)(2,1)S(1)}, u32[]{:S(2)}, u32[]{:S(2)}) collective-permute-start(bf16[7808,128]{1,0:T(8,128)(2,1)S(1)} %swap.1), channel_id=1, source_target_pairs={{0,8},{1,9},{2,10},{3,11},{4,12},{5,13},{6,14},{7,15},{8,0},{9,1},... | collective-permute-start | bytes 5996552 | tf_op jit(solution)/shard_map/ppermute | solution.py:352
  23.1 2.0 %collective-permute-start.10 = (bf16[1184,128]{1,0:T(8,128)(2,1)S(1)}, bf16[1184,128]{1,0:T(8,128)(2,1)S(1)}, u32[]{:S(2)}, u32[]{:S(2)}) collective-permute-start(bf16[1184,128]{1,0:T(8,128)(2,1)S(1)} %pass_late.3), channel_id=1, source_target_pairs={{0,8},{1,9},{2,10},{3,11},{4,12},{5,13},{6,14},{7,15},{8,0},{9,1},... | collective-permute-start | bytes 909320 | tf_op jit(solution)/shard_map/ppermute | solution.py:352
  23.8 1.7 %collective-permute-start.8 = (bf16[1184,128]{1,0:T(8,128)(2,1)S(1)}, bf16[1184,128]{1,0:T(8,128)(2,1)S(1)}, u32[]{:S(2)}, u32[]{:S(2)}) collective-permute-start(bf16[1184,128]{1,0:T(8,128)(2,1)S(1)} %pass_late.2), channel_id=1, source_target_pairs={{0,8},{1,9},{2,10},{3,11},{4,12},{5,13},{6,14},{7,15},{8,0},{9,1},... | collective-permute-start | bytes 909320 | tf_op jit(solution)/shard_map/ppermute | solution.py:352

commit v8 on v7

--- a/solution.py
+++ b/solution.py
@@ -409,8 +409,9 @@
     result = jax.ShapeDtypeStruct((prolong.shape[1], applied.shape[1]), jnp.float32)
     sizes = (cols, half, width)
     partial = call(functools.partial(own_kernel, *sizes), "own", result, own_first, own_second, swap, side)
-    far_second = call(mask_kernel, "settle", half_ap, far_second, partial)
-    late_first = move(call(pass_kernel, "pass_late", shape(size, TILE), late[0], mine), partner)
+    passed = call(pass_kernel, "pass_late", shape(size, TILE), late[0], partial)
+    late_first = move(passed, partner)
+    far_second = call(mask_kernel, "settle", half_ap, far_second, passed)
     late_second = move(call(pass_kernel, "pass_late", shape(size, TILE), late[1], far_second, weight=LAST_WEIGHT), partner)
     beyond = [(r, r + 1 if r % 2 == 1 else r - 1) for r in range(rows)]
     relay = [((r + rows // 2) % rows, t) for r, t in beyond if 0 <= t < rows]

time: 26.8 us -> 26.7 us (level)
  transfers between devices with their start and end apart: 11 -> 11, of which waited for: 3 -> 4; matrix products, arithmetic and copies ran while one was open for 0% -> 0% of each run, Pallas kernels for 10% -> 10%
where the time goes in v8:
time: 26.7 us; the launch traced here: 26.6 us
  starting transfers between devices  13.5 us (51%)
  waiting for transfers between devices  7.81 us (29%)
  Pallas kernels  5.12 us (19%)
    ppermute x11, starting transfers between devices, move(): return lax.ppermute(x, AXES, pairs)  13.5 us
    ppermute x11, waiting for transfers between devices, move(): return lax.ppermute(x, AXES, pairs)  7.81 us
    pallas_call x13, Pallas kernels, call(): pl.pallas_call(kernel, out_shape=out_shape, in_specs=specs or [vmem] * le...  3.99 us
    pallas_call x1, Pallas kernels, on_device(): pl.pallas_call(functools.partial(last_kernel, *sizes), out_shape=result,...  1.12 us
  transfers between devices with their start and end apart: 11, of which 4 were waited for; matrix products, arithmetic and copies ran while one was open for 0% of the time, Pallas kernels for 10%

profile of v8, /device:TPU:0, one launch (start us, length us, event | category | flops | bytes accessed | tf_op | source)
XLA Modules:
  0.0 26.6 jit_solution(13796499982135701306)
XLA Ops:
  0.0 1.5 %prepare.1 = (bf16[1168,128]{1,0:T(8,128)(2,1)S(1)}, bf16[1168,128]{1,0:T(8,128)(2,1)S(1)}, bf16[784,256]{1,0:T(8,128)(2,1)S(1)}, bf16[784,256]{1,0:T(8,128)(2,1)S(1)}) custom-call(bf16[768,512]{1,0:T(8,128)(2,1)} %p_hbm.1, bf16[1536,256]{1,0:T(8,128)(2,1)} %ap_hbm.1, s32[4,6]{1,0:T(4,128)} %bitcast.2, s32[2,12]{1,0:T(2,128)} %bitcast.3), custom_call_target="tpu_custom_call" | custom-call | tf_op jit(solution)/shard_map/prepare/pallas_call | solution.py:346
  1.5 0.4 %collective-permute-start.1 = (bf16[1168,128]{1,0:T(8,128)(2,1)S(1)}, bf16[1168,128]{1,0:T(8,128)(2,1)S(1)}, u32[]{:S(2)}, u32[]{:S(2)}) collective-permute-start(bf16[1168,128]{1,0:T(8,128)(2,1)S(1)} %get-tuple-element.16), channel_id=1, source_target_pairs={{0,8},{1,9},{2,10},{3,11},{4,12},{5,13},{6,14},{7,15},{8,0},{9,1},... | collective-permute-start | bytes 897032 | tf_op jit(solution)/shard_map/ppermute | solution.py:352
  1.9 2.6 %collective-permute-start = (bf16[784,256]{1,0:T(8,128)(2,1)S(1)}, bf16[784,256]{1,0:T(8,128)(2,1)S(1)}, u32[]{:S(2)}, u32[]{:S(2)}) collective-permute-start(bf16[784,256]{1,0:T(8,128)(2,1)S(1)} %get-tuple-element.11.first_ref), channel_id=1, source_target_pairs={{0,16},{1,17},{2,18},{3,19},{4,20},{5,21},{6,22},{7,23},{8,24},{9,... | collective-permute-start | bytes 1204232 | tf_op jit(solution)/shard_map/ppermute | solution.py:352
  4.5 0.1 merge.1.ordered_after.own
  4.6 1.6 %collective-permute-start.3 = (bf16[1184,128]{1,0:T(8,128)(2,1)S(1)}, bf16[1184,128]{1,0:T(8,128)(2,1)S(1)}, u32[]{:S(2)}, u32[]{:S(2)}) collective-permute-start(bf16[1184,128]{1,0:T(8,128)(2,1)S(1)} %merge.1.ordered_after.own), channel_id=1, source_target_pairs={{0,2},{1,3},{2,0},{3,1},{4,6},{5,7},{6,4},{7,5},{8,10},{9,11},{10,... | collective-permute-start | bytes 909320 | tf_op jit(solution)/shard_map/ppermute | solution.py:352
  6.2 1.5 %collective-permute-start.2 = (bf16[784,256]{1,0:T(8,128)(2,1)S(1)}, bf16[784,256]{1,0:T(8,128)(2,1)S(1)}, u32[]{:S(2)}, u32[]{:S(2)}) collective-permute-start(bf16[784,256]{1,0:T(8,128)(2,1)S(1)} %get-tuple-element.12.second_ref), channel_id=1, source_target_pairs={{0,16},{1,17},{2,18},{3,19},{4,20},{5,21},{6,22},{7,23},{8,24},{9,... | collective-permute-start | bytes 1204232 | tf_op jit(solution)/shard_map/ppermute | solution.py:352
  7.7 0.1 mask_own.1
  7.8 1.6 %collective-permute-start.6 = (bf16[1184,128]{1,0:T(8,128)(2,1)S(1)}, bf16[1184,128]{1,0:T(8,128)(2,1)S(1)}, u32[]{:S(2)}, u32[]{:S(2)}) collective-permute-start(bf16[1184,128]{1,0:T(8,128)(2,1)S(1)} %merge.1.ordered_after.own), channel_id=1, source_target_pairs={{0,1},{1,0},{2,3},{3,2},{4,5},{5,4},{6,7},{7,6},{8,9},{9,8},{10,11... | collective-permute-start | bytes 909320 | tf_op jit(solution)/shard_map/ppermute | solution.py:352
  9.4 4.5 %collective-permute-done.3.pair = bf16[1184,128]{1,0:T(8,128)(2,1)S(1)} collective-permute-done((bf16[1184,128]{1,0:T(8,128)(2,1)S(1)}, bf16[1184,128]{1,0:T(8,128)(2,1)S(1)}, u32[]{:S(2)}, u32[]{:S(2)}) %collective-permute-start.3) | collective-permute-done | bytes 303136 | tf_op jit(solution)/shard_map/ppermute | solution.py:352
  14.0 1.6 %collective-permute-start.5 = (bf16[1184,128]{1,0:T(8,128)(2,1)S(1)}, bf16[1184,128]{1,0:T(8,128)(2,1)S(1)}, u32[]{:S(2)}, u32[]{:S(2)}) collective-permute-start(bf16[1184,128]{1,0:T(8,128)(2,1)S(1)} %forward.2.ordered_after), channel_id=1, source_target_pairs={{0,1},{1,0},{2,3},{3,2},{4,5},{5,4},{6,7},{7,6},{8,12},{9,13},{10,... | collective-permute-start | bytes 909320 | tf_op jit(solution)/shard_map/ppermute | solution.py:352
  15.5 3.9 %collective-permute-start.8 = (bf16[1184,128]{1,0:T(8,128)(2,1)S(1)}, bf16[1184,128]{1,0:T(8,128)(2,1)S(1)}, u32[]{:S(2)}, u32[]{:S(2)}) collective-permute-start(bf16[1184,128]{1,0:T(8,128)(2,1)S(1)} %forward.3), channel_id=1, source_target_pairs={{0,4},{1,5},{2,0},{3,1},{4,6},{5,7},{6,2},{7,3},{8,9},{9,8},{10,11... | collective-permute-start | bytes 909320 | tf_op jit(solution)/shard_map/ppermute | solution.py:352
  19.5 0.0 collective-permute-done.6.side
  19.5 0.4 %swap.1 = bf16[7808,128]{1,0:T(8,128)(2,1)S(1)} custom-call(bf16[1184,128]{1,0:T(8,128)(2,1)S(1)} %merge.1.ordered_after.own, bf16[1184,128]{1,0:T(8,128)(2,1)S(1)} %collective-permute-done.6.side, bf16[1184,128]{1,0:T(8,128)(2,1)S(1)} %collective-permute-done.3.pair, bf16[1184,128]{1,0:T(8,128)(2,1)S(1)} %collective-permute-done.4.cross.ordered_after, ...), custom_call_target="tpu_custom_call" | custom-call | tf_op jit(solution)/shard_map/swap/pallas_call | solution.py:346
  19.9 0.1 collective-permute-start.7
  20.0 0.4 %own.1.ordered_after.partial = f32[512,256]{1,0:T(8,128)S(1)} custom-call(bf16[768,256]{1,0:T(8,128)(2,1)S(1)} %get-tuple-element.13.own_first, bf16[768,256]{1,0:T(8,128)(2,1)S(1)} %get-tuple-element.14.own_second, bf16[7808,128]{1,0:T(8,128)(2,1)S(1)} %swap.1, bf16[1184,128]{1,0:T(8,128)(2,1)S(1)} %collective-permute-done.6.side), custom_call_target="tpu_custom_call" | custom-call | tf_op jit(solution)/shard_map/own/pallas_call | solution.py:346
  20.4 1.8 %collective-permute-done.5.ref.late_first = bf16[1184,128]{1,0:T(8,128)(2,1)S(1)} collective-permute-done((bf16[1184,128]{1,0:T(8,128)(2,1)S(1)}, bf16[1184,128]{1,0:T(8,128)(2,1)S(1)}, u32[]{:S(2)}, u32[]{:S(2)}) %collective-permute-start.5) | collective-permute-done | bytes 303136 | tf_op jit(solution)/shard_map/ppermute | solution.py:352
  22.3 0.1 collective-permute-start.10
  22.4 0.6 %collective-permute-done.2.ref = bf16[784,256]{1,0:T(8,128)(2,1)S(1)} collective-permute-done((bf16[784,256]{1,0:T(8,128)(2,1)S(1)}, bf16[784,256]{1,0:T(8,128)(2,1)S(1)}, u32[]{:S(2)}, u32[]{:S(2)}) %collective-permute-start.2) | collective-permute-done | bytes 401440 | tf_op jit(solution)/shard_map/ppermute | solution.py:352
  23.0 0.7 %collective-permute-done.8.ref.late_second = bf16[1184,128]{1,0:T(8,128)(2,1)S(1)} collective-permute-done((bf16[1184,128]{1,0:T(8,128)(2,1)S(1)}, bf16[1184,128]{1,0:T(8,128)(2,1)S(1)}, u32[]{:S(2)}, u32[]{:S(2)}) %collective-permute-start.8) | collective-permute-done | bytes 303136 | tf_op jit(solution)/shard_map/ppermute | solution.py:352
  23.8 0.2 collective-permute-start.9
  24.0 0.0 collective-permute-done.7.swapped.cross_ap
  24.0 1.0 %near.1.partial = f32[512,256]{1,0:T(8,128)S(1)} custom-call(bf16[768,256]{1,0:T(8,128)(2,1)S(1)} %get-tuple-element.13.own_first, bf16[768,256]{1,0:T(8,128)(2,1)S(1)} %get-tuple-element.14.own_second, bf16[768,256]{1,0:T(8,128)(2,1)S(1)} %settle_first.1.far_first, bf16[768,256]{1,0:T(8,128)(2,1)S(1)} %settle.1.ordered_after.far_second, ...), custom_call_target="tpu_custom_call" | custom-call | tf_op jit(solution)/shard_map/near/pallas_call | solution.py:346
  25.1 0.4 %late.1.partial = f32[512,256]{1,0:T(8,128)S(1)} custom-call(bf16[768,256]{1,0:T(8,128)(2,1)S(1)} %get-tuple-element.13.own_first, bf16[768,256]{1,0:T(8,128)(2,1)S(1)} %get-tuple-element.14.own_second, bf16[768,256]{1,0:T(8,128)(2,1)S(1)} %settle_first.1.far_first, bf16[768,256]{1,0:T(8,128)(2,1)S(1)} %settle.1.ordered_after.far_second, ...), custom_call_target="tpu_custom_call" | custom-call | tf_op jit(solution)/shard_map/late/pallas_call | solution.py:346
  25.5 1.1 %last.1 = f32[512,256]{1,0:T(8,128)} custom-call(bf16[768,256]{1,0:T(8,128)(2,1)S(1)} %get-tuple-element.13.own_first, bf16[768,256]{1,0:T(8,128)(2,1)S(1)} %get-tuple-element.14.own_second, bf16[768,256]{1,0:T(8,128)(2,1)S(1)} %settle_first.1.far_first, bf16[768,256]{1,0:T(8,128)(2,1)S(1)} %settle.1.ordered_after.far_second, ...), custom_call_target="tpu_custom_call" | custom-call | tf_op jit(solution)/shard_map/last/pallas_call | solution.py:428
  (12 shorter events, 0.2 us)
Async XLA Ops:
  1.5 3.1 %collective-permute-start.1 = (bf16[1168,128]{1,0:T(8,128)(2,1)S(1)}, bf16[1168,128]{1,0:T(8,128)(2,1)S(1)}, u32[]{:S(2)}, u32[]{:S(2)}) collective-permute-start(bf16[1168,128]{1,0:T(8,128)(2,1)S(1)} %get-tuple-element.16), channel_id=1, source_target_pairs={{0,8},{1,9},{2,10},{3,11},{4,12},{5,13},{6,14},{7,15},{8,0},{9,1},... | collective-permute-start | bytes 897032 | tf_op jit(solution)/shard_map/ppermute | solution.py:352
  1.9 17.5 %collective-permute-start = (bf16[784,256]{1,0:T(8,128)(2,1)S(1)}, bf16[784,256]{1,0:T(8,128)(2,1)S(1)}, u32[]{:S(2)}, u32[]{:S(2)}) collective-permute-start(bf16[784,256]{1,0:T(8,128)(2,1)S(1)} %get-tuple-element.11.first_ref), channel_id=1, source_target_pairs={{0,16},{1,17},{2,18},{3,19},{4,20},{5,21},{6,22},{7,23},{8,24},{9,... | collective-permute-start | bytes 1204232 | tf_op jit(solution)/shard_map/ppermute | solution.py:352
  4.6 9.3 %collective-permute-start.3 = (bf16[1184,128]{1,0:T(8,128)(2,1)S(1)}, bf16[1184,128]{1,0:T(8,128)(2,1)S(1)}, u32[]{:S(2)}, u32[]{:S(2)}) collective-permute-start(bf16[1184,128]{1,0:T(8,128)(2,1)S(1)} %merge.1.ordered_after.own), channel_id=1, source_target_pairs={{0,2},{1,3},{2,0},{3,1},{4,6},{5,7},{6,4},{7,5},{8,10},{9,11},{10,... | collective-permute-start | bytes 909320 | tf_op jit(solution)/shard_map/ppermute | solution.py:352
  6.2 7.7 %collective-permute-start.4 = (bf16[1184,128]{1,0:T(8,128)(2,1)S(1)}, bf16[1184,128]{1,0:T(8,128)(2,1)S(1)}, u32[]{:S(2)}, u32[]{:S(2)}) collective-permute-start(bf16[1184,128]{1,0:T(8,128)(2,1)S(1)} %merge.1.ordered_after.own), channel_id=1, source_target_pairs={{0,8},{1,9},{2,4},{3,5},{4,2},{5,3},{6,14},{7,15},{8,0},{9,1},{10,... | collective-permute-start | bytes 909320 | tf_op jit(solution)/shard_map/ppermute | solution.py:352
  6.2 16.8 %collective-permute-start.2 = (bf16[784,256]{1,0:T(8,128)(2,1)S(1)}, bf16[784,256]{1,0:T(8,128)(2,1)S(1)}, u32[]{:S(2)}, u32[]{:S(2)}) collective-permute-start(bf16[784,256]{1,0:T(8,128)(2,1)S(1)} %get-tuple-element.12.second_ref), channel_id=1, source_target_pairs={{0,16},{1,17},{2,18},{3,19},{4,20},{5,21},{6,22},{7,23},{8,24},{9,... | collective-permute-start | bytes 1204232 | tf_op jit(solution)/shard_map/ppermute | solution.py:352
  7.8 11.7 %collective-permute-start.6 = (bf16[1184,128]{1,0:T(8,128)(2,1)S(1)}, bf16[1184,128]{1,0:T(8,128)(2,1)S(1)}, u32[]{:S(2)}, u32[]{:S(2)}) collective-permute-start(bf16[1184,128]{1,0:T(8,128)(2,1)S(1)} %merge.1.ordered_after.own), channel_id=1, source_target_pairs={{0,1},{1,0},{2,3},{3,2},{4,5},{5,4},{6,7},{7,6},{8,9},{9,8},{10,11... | collective-permute-start | bytes 909320 | tf_op jit(solution)/shard_map/ppermute | solution.py:352
  14.0 8.3 %collective-permute-start.5 = (bf16[1184,128]{1,0:T(8,128)(2,1)S(1)}, bf16[1184,128]{1,0:T(8,128)(2,1)S(1)}, u32[]{:S(2)}, u32[]{:S(2)}) collective-permute-start(bf16[1184,128]{1,0:T(8,128)(2,1)S(1)} %forward.2.ordered_after), channel_id=1, source_target_pairs={{0,1},{1,0},{2,3},{3,2},{4,5},{5,4},{6,7},{7,6},{8,12},{9,13},{10,... | collective-permute-start | bytes 909320 | tf_op jit(solution)/shard_map/ppermute | solution.py:352
  15.5 8.2 %collective-permute-start.8 = (bf16[1184,128]{1,0:T(8,128)(2,1)S(1)}, bf16[1184,128]{1,0:T(8,128)(2,1)S(1)}, u32[]{:S(2)}, u32[]{:S(2)}) collective-permute-start(bf16[1184,128]{1,0:T(8,128)(2,1)S(1)} %forward.3), channel_id=1, source_target_pairs={{0,4},{1,5},{2,0},{3,1},{4,6},{5,7},{6,2},{7,3},{8,9},{9,8},{10,11... | collective-permute-start | bytes 909320 | tf_op jit(solution)/shard_map/ppermute | solution.py:352
  19.9 4.1 %collective-permute-start.7 = (bf16[7808,128]{1,0:T(8,128)(2,1)S(1)}, bf16[7808,128]{1,0:T(8,128)(2,1)S(1)}, u32[]{:S(2)}, u32[]{:S(2)}) collective-permute-start(bf16[7808,128]{1,0:T(8,128)(2,1)S(1)} %swap.1), channel_id=1, source_target_pairs={{0,8},{1,9},{2,10},{3,11},{4,12},{5,13},{6,14},{7,15},{8,0},{9,1},... | collective-permute-start | bytes 5996552 | tf_op jit(solution)/shard_map/ppermute | solution.py:352
  22.3 2.8 %collective-permute-start.10 = (bf16[1184,128]{1,0:T(8,128)(2,1)S(1)}, bf16[1184,128]{1,0:T(8,128)(2,1)S(1)}, u32[]{:S(2)}, u32[]{:S(2)}) collective-permute-start(bf16[1184,128]{1,0:T(8,128)(2,1)S(1)} %pass_late.2.ordered_after), channel_id=1, source_target_pairs={{0,8},{1,9},{2,10},{3,11},{4,12},{5,13},{6,14},{7,15},{8,0},{9,1},... | collective-permute-start | bytes 909320 | tf_op jit(solution)/shard_map/ppermute | solution.py:352
  23.8 1.7 %collective-permute-start.9 = (bf16[1184,128]{1,0:T(8,128)(2,1)S(1)}, bf16[1184,128]{1,0:T(8,128)(2,1)S(1)}, u32[]{:S(2)}, u32[]{:S(2)}) collective-permute-start(bf16[1184,128]{1,0:T(8,128)(2,1)S(1)} %pass_late.3), channel_id=1, source_target_pairs={{0,8},{1,9},{2,10},{3,11},{4,12},{5,13},{6,14},{7,15},{8,0},{9,1},... | collective-permute-start | bytes 909320 | tf_op jit(solution)/shard_map/ppermute | solution.py:352

commit v9 on v8

--- a/solution.py
+++ b/solution.py
@@ -9,7 +9,8 @@
 
 TILE = 128
 AXES = ("row", "col")
-LAST_WEIGHT, FIRST_WEIGHT = 20, 5
+SIDE_WEIGHT = 2
+LAST_WEIGHT, FIRST_WEIGHT = 20, 3
 DIAGONAL_FIRST = 0
 SLOTS = 3
 META = 16
@@ -376,7 +377,7 @@
     )
     got = move(send, partner)
     far_first, far_second = move(raw_first, row_pairs(opposite)), move(raw_second, row_pairs(opposite))
-    mine = call(merge_kernel, "merge", shape(size, TILE), keep, got)
+    mine = call(merge_kernel, "merge", shape(size, TILE), keep, got, weight=SIDE_WEIGHT)
     middle = lambda c: 2 <= c < cols - 2
     step = lambda c: c - 2 if (c // 2) % 2 == 0 else c + 2
     cross = move(mine, [
@@ -401,6 +402,7 @@
         late.append(move(send_on, relay_pairs(step)))
         after = send_on
     own_first, own_second = call(mask_own_kernel, "mask_own", (half_ap,) * 2, raw_first, raw_second)
+    side = call(pass_kernel, "pass_side", shape(size, TILE), side, mine, weight=SIDE_WEIGHT)
     far_first = call(mask_kernel, "settle_first", half_ap, far_first, mine, weight=FIRST_WEIGHT)
     swap = call(
         swap_kernel, "swap", shape(len(FIRST) * size + 4 * depth, TILE), mine, side, pair, cross, own_second, far_first

time: 26.7 us -> 26.8 us (level)
    pallas_call x13 -> x14, Pallas kernels: 3.99 us -> 4.03 us  [call(): pl.pallas_call(kernel, out_shape=out_shape, in_specs=specs or [vmem] * le...]
  transfers between devices with their start and end apart: 11 -> 11, of which waited for: 4 -> 5; matrix products, arithmetic and copies ran while one was open for 0% -> 0% of each run, Pallas kernels for 10% -> 10%
where the time goes in v9:
time: 26.8 us; the launch traced here: 26.6 us
  starting transfers between devices  13.5 us (50%)
  waiting for transfers between devices  7.87 us (29%)
  Pallas kernels  5.15 us (19%)
    ppermute x11, starting transfers between devices, move(): return lax.ppermute(x, AXES, pairs)  13.5 us
    ppermute x11, waiting for transfers between devices, move(): return lax.ppermute(x, AXES, pairs)  7.87 us
    pallas_call x14, Pallas kernels, call(): pl.pallas_call(kernel, out_shape=out_shape, in_specs=specs or [vmem] * le...  4.03 us
    pallas_call x1, Pallas kernels, on_device(): pl.pallas_call(functools.partial(last_kernel, *sizes), out_shape=result,...  1.12 us
  transfers between devices with their start and end apart: 11, of which 5 were waited for; matrix products, arithmetic and copies ran while one was open for 0% of the time, Pallas kernels for 10%

profile of v9, /device:TPU:0, one launch (start us, length us, event | category | flops | bytes accessed | tf_op | source)
XLA Modules:
  0.0 26.6 jit_solution(12329492943126592110)
XLA Ops:
  0.0 1.5 %prepare.1 = (bf16[1168,128]{1,0:T(8,128)(2,1)S(1)}, bf16[1168,128]{1,0:T(8,128)(2,1)S(1)}, bf16[784,256]{1,0:T(8,128)(2,1)S(1)}, bf16[784,256]{1,0:T(8,128)(2,1)S(1)}) custom-call(bf16[768,512]{1,0:T(8,128)(2,1)} %p_hbm.1, bf16[1536,256]{1,0:T(8,128)(2,1)} %ap_hbm.1, s32[4,6]{1,0:T(4,128)} %bitcast.2, s32[2,12]{1,0:T(2,128)} %bitcast.3), custom_call_target="tpu_custom_call" | custom-call | tf_op jit(solution)/shard_map/prepare/pallas_call | solution.py:347
  1.5 0.4 %collective-permute-start.1 = (bf16[1168,128]{1,0:T(8,128)(2,1)S(1)}, bf16[1168,128]{1,0:T(8,128)(2,1)S(1)}, u32[]{:S(2)}, u32[]{:S(2)}) collective-permute-start(bf16[1168,128]{1,0:T(8,128)(2,1)S(1)} %get-tuple-element.16), channel_id=1, source_target_pairs={{0,8},{1,9},{2,10},{3,11},{4,12},{5,13},{6,14},{7,15},{8,0},{9,1},... | collective-permute-start | bytes 897032 | tf_op jit(solution)/shard_map/ppermute | solution.py:353
  1.9 2.6 %collective-permute-start = (bf16[784,256]{1,0:T(8,128)(2,1)S(1)}, bf16[784,256]{1,0:T(8,128)(2,1)S(1)}, u32[]{:S(2)}, u32[]{:S(2)}) collective-permute-start(bf16[784,256]{1,0:T(8,128)(2,1)S(1)} %get-tuple-element.11.first_ref), channel_id=1, source_target_pairs={{0,16},{1,17},{2,18},{3,19},{4,20},{5,21},{6,22},{7,23},{8,24},{9,... | collective-permute-start | bytes 1204232 | tf_op jit(solution)/shard_map/ppermute | solution.py:353
  4.5 0.1 merge.1.ordered_after.own
  4.6 1.6 %collective-permute-start.3 = (bf16[1184,128]{1,0:T(8,128)(2,1)S(1)}, bf16[1184,128]{1,0:T(8,128)(2,1)S(1)}, u32[]{:S(2)}, u32[]{:S(2)}) collective-permute-start(bf16[1184,128]{1,0:T(8,128)(2,1)S(1)} %merge.1.ordered_after.own), channel_id=1, source_target_pairs={{0,2},{1,3},{2,0},{3,1},{4,6},{5,7},{6,4},{7,5},{8,10},{9,11},{10,... | collective-permute-start | bytes 909320 | tf_op jit(solution)/shard_map/ppermute | solution.py:353
  6.2 0.0 collective-permute-start.4
  6.2 1.5 %collective-permute-start.6 = (bf16[1184,128]{1,0:T(8,128)(2,1)S(1)}, bf16[1184,128]{1,0:T(8,128)(2,1)S(1)}, u32[]{:S(2)}, u32[]{:S(2)}) collective-permute-start(bf16[1184,128]{1,0:T(8,128)(2,1)S(1)} %merge.1.ordered_after.own), channel_id=1, source_target_pairs={{0,1},{1,0},{2,3},{3,2},{4,5},{5,4},{6,7},{7,6},{8,9},{9,8},{10,11... | collective-permute-start | bytes 909320 | tf_op jit(solution)/shard_map/ppermute | solution.py:353
  7.7 1.5 %collective-permute-start.2 = (bf16[784,256]{1,0:T(8,128)(2,1)S(1)}, bf16[784,256]{1,0:T(8,128)(2,1)S(1)}, u32[]{:S(2)}, u32[]{:S(2)}) collective-permute-start(bf16[784,256]{1,0:T(8,128)(2,1)S(1)} %get-tuple-element.12.second_ref), channel_id=1, source_target_pairs={{0,16},{1,17},{2,18},{3,19},{4,20},{5,21},{6,22},{7,23},{8,24},{9,... | collective-permute-start | bytes 1204232 | tf_op jit(solution)/shard_map/ppermute | solution.py:353
  9.3 0.1 mask_own.1
  9.3 4.6 %collective-permute-done.3.pair = bf16[1184,128]{1,0:T(8,128)(2,1)S(1)} collective-permute-done((bf16[1184,128]{1,0:T(8,128)(2,1)S(1)}, bf16[1184,128]{1,0:T(8,128)(2,1)S(1)}, u32[]{:S(2)}, u32[]{:S(2)}) %collective-permute-start.3) | collective-permute-done | bytes 303136 | tf_op jit(solution)/shard_map/ppermute | solution.py:353
  14.0 1.6 %collective-permute-start.5 = (bf16[1184,128]{1,0:T(8,128)(2,1)S(1)}, bf16[1184,128]{1,0:T(8,128)(2,1)S(1)}, u32[]{:S(2)}, u32[]{:S(2)}) collective-permute-start(bf16[1184,128]{1,0:T(8,128)(2,1)S(1)} %forward.2.ordered_after), channel_id=1, source_target_pairs={{0,1},{1,0},{2,3},{3,2},{4,5},{5,4},{6,7},{7,6},{8,12},{9,13},{10,... | collective-permute-start | bytes 909320 | tf_op jit(solution)/shard_map/ppermute | solution.py:353
  15.5 3.9 %collective-permute-start.8 = (bf16[1184,128]{1,0:T(8,128)(2,1)S(1)}, bf16[1184,128]{1,0:T(8,128)(2,1)S(1)}, u32[]{:S(2)}, u32[]{:S(2)}) collective-permute-start(bf16[1184,128]{1,0:T(8,128)(2,1)S(1)} %forward.3), channel_id=1, source_target_pairs={{0,4},{1,5},{2,0},{3,1},{4,6},{5,7},{6,2},{7,3},{8,9},{9,8},{10,11... | collective-permute-start | bytes 909320 | tf_op jit(solution)/shard_map/ppermute | solution.py:353
  19.5 0.4 %swap.1 = bf16[7808,128]{1,0:T(8,128)(2,1)S(1)} custom-call(bf16[1184,128]{1,0:T(8,128)(2,1)S(1)} %merge.1.ordered_after.own, bf16[1184,128]{1,0:T(8,128)(2,1)S(1)} %pass_side.1.side, bf16[1184,128]{1,0:T(8,128)(2,1)S(1)} %collective-permute-done.3.pair, bf16[1184,128]{1,0:T(8,128)(2,1)S(1)} %collective-permute-done.4.cross.ordered_after, ...), custom_call_target="tpu_custom_call" | custom-call | tf_op jit(solution)/shard_map/swap/pallas_call | solution.py:347
  20.0 0.1 collective-permute-start.7
  20.0 0.4 %own.1.ordered_after.partial = f32[512,256]{1,0:T(8,128)S(1)} custom-call(bf16[768,256]{1,0:T(8,128)(2,1)S(1)} %get-tuple-element.13.own_first, bf16[768,256]{1,0:T(8,128)(2,1)S(1)} %get-tuple-element.14.own_second, bf16[7808,128]{1,0:T(8,128)(2,1)S(1)} %swap.1, bf16[1184,128]{1,0:T(8,128)(2,1)S(1)} %pass_side.1.side), custom_call_target="tpu_custom_call" | custom-call | tf_op jit(solution)/shard_map/own/pallas_call | solution.py:347
  20.5 1.8 %collective-permute-done.5.ref.late_first = bf16[1184,128]{1,0:T(8,128)(2,1)S(1)} collective-permute-done((bf16[1184,128]{1,0:T(8,128)(2,1)S(1)}, bf16[1184,128]{1,0:T(8,128)(2,1)S(1)}, u32[]{:S(2)}, u32[]{:S(2)}) %collective-permute-start.5) | collective-permute-done | bytes 303136 | tf_op jit(solution)/shard_map/ppermute | solution.py:353
  22.3 0.1 collective-permute-start.10
  22.4 0.6 %collective-permute-done.2.ref = bf16[784,256]{1,0:T(8,128)(2,1)S(1)} collective-permute-done((bf16[784,256]{1,0:T(8,128)(2,1)S(1)}, bf16[784,256]{1,0:T(8,128)(2,1)S(1)}, u32[]{:S(2)}, u32[]{:S(2)}) %collective-permute-start.2) | collective-permute-done | bytes 401440 | tf_op jit(solution)/shard_map/ppermute | solution.py:353
  23.0 0.7 %collective-permute-done.8.ref.late_second = bf16[1184,128]{1,0:T(8,128)(2,1)S(1)} collective-permute-done((bf16[1184,128]{1,0:T(8,128)(2,1)S(1)}, bf16[1184,128]{1,0:T(8,128)(2,1)S(1)}, u32[]{:S(2)}, u32[]{:S(2)}) %collective-permute-start.8) | collective-permute-done | bytes 303136 | tf_op jit(solution)/shard_map/ppermute | solution.py:353
  23.8 0.2 collective-permute-start.9
  24.0 0.1 collective-permute-done.7.swapped.cross_ap
  24.1 1.0 %near.1.partial = f32[512,256]{1,0:T(8,128)S(1)} custom-call(bf16[768,256]{1,0:T(8,128)(2,1)S(1)} %get-tuple-element.13.own_first, bf16[768,256]{1,0:T(8,128)(2,1)S(1)} %get-tuple-element.14.own_second, bf16[768,256]{1,0:T(8,128)(2,1)S(1)} %settle_first.1.far_first, bf16[768,256]{1,0:T(8,128)(2,1)S(1)} %settle.1.ordered_after.far_second, ...), custom_call_target="tpu_custom_call" | custom-call | tf_op jit(solution)/shard_map/near/pallas_call | solution.py:347
  25.1 0.4 %late.1.partial = f32[512,256]{1,0:T(8,128)S(1)} custom-call(bf16[768,256]{1,0:T(8,128)(2,1)S(1)} %get-tuple-element.13.own_first, bf16[768,256]{1,0:T(8,128)(2,1)S(1)} %get-tuple-element.14.own_second, bf16[768,256]{1,0:T(8,128)(2,1)S(1)} %settle_first.1.far_first, bf16[768,256]{1,0:T(8,128)(2,1)S(1)} %settle.1.ordered_after.far_second, ...), custom_call_target="tpu_custom_call" | custom-call | tf_op jit(solution)/shard_map/late/pallas_call | solution.py:347
  25.5 1.1 %last.1 = f32[512,256]{1,0:T(8,128)} custom-call(bf16[768,256]{1,0:T(8,128)(2,1)S(1)} %get-tuple-element.13.own_first, bf16[768,256]{1,0:T(8,128)(2,1)S(1)} %get-tuple-element.14.own_second, bf16[768,256]{1,0:T(8,128)(2,1)S(1)} %settle_first.1.far_first, bf16[768,256]{1,0:T(8,128)(2,1)S(1)} %settle.1.ordered_after.far_second, ...), custom_call_target="tpu_custom_call" | custom-call | tf_op jit(solution)/shard_map/last/pallas_call | solution.py:430
  (13 shorter events, 0.2 us)
Async XLA Ops:
  1.5 3.1 %collective-permute-start.1 = (bf16[1168,128]{1,0:T(8,128)(2,1)S(1)}, bf16[1168,128]{1,0:T(8,128)(2,1)S(1)}, u32[]{:S(2)}, u32[]{:S(2)}) collective-permute-start(bf16[1168,128]{1,0:T(8,128)(2,1)S(1)} %get-tuple-element.16), channel_id=1, source_target_pairs={{0,8},{1,9},{2,10},{3,11},{4,12},{5,13},{6,14},{7,15},{8,0},{9,1},... | collective-permute-start | bytes 897032 | tf_op jit(solution)/shard_map/ppermute | solution.py:353
  1.9 17.5 %collective-permute-start = (bf16[784,256]{1,0:T(8,128)(2,1)S(1)}, bf16[784,256]{1,0:T(8,128)(2,1)S(1)}, u32[]{:S(2)}, u32[]{:S(2)}) collective-permute-start(bf16[784,256]{1,0:T(8,128)(2,1)S(1)} %get-tuple-element.11.first_ref), channel_id=1, source_target_pairs={{0,16},{1,17},{2,18},{3,19},{4,20},{5,21},{6,22},{7,23},{8,24},{9,... | collective-permute-start | bytes 1204232 | tf_op jit(solution)/shard_map/ppermute | solution.py:353
  4.6 9.3 %collective-permute-start.3 = (bf16[1184,128]{1,0:T(8,128)(2,1)S(1)}, bf16[1184,128]{1,0:T(8,128)(2,1)S(1)}, u32[]{:S(2)}, u32[]{:S(2)}) collective-permute-start(bf16[1184,128]{1,0:T(8,128)(2,1)S(1)} %merge.1.ordered_after.own), channel_id=1, source_target_pairs={{0,2},{1,3},{2,0},{3,1},{4,6},{5,7},{6,4},{7,5},{8,10},{9,11},{10,... | collective-permute-start | bytes 909320 | tf_op jit(solution)/shard_map/ppermute | solution.py:353
  6.2 7.7 %collective-permute-start.4 = (bf16[1184,128]{1,0:T(8,128)(2,1)S(1)}, bf16[1184,128]{1,0:T(8,128)(2,1)S(1)}, u32[]{:S(2)}, u32[]{:S(2)}) collective-permute-start(bf16[1184,128]{1,0:T(8,128)(2,1)S(1)} %merge.1.ordered_after.own), channel_id=1, source_target_pairs={{0,8},{1,9},{2,4},{3,5},{4,2},{5,3},{6,14},{7,15},{8,0},{9,1},{10,... | collective-permute-start | bytes 909320 | tf_op jit(solution)/shard_map/ppermute | solution.py:353
  6.2 13.2 %collective-permute-start.6 = (bf16[1184,128]{1,0:T(8,128)(2,1)S(1)}, bf16[1184,128]{1,0:T(8,128)(2,1)S(1)}, u32[]{:S(2)}, u32[]{:S(2)}) collective-permute-start(bf16[1184,128]{1,0:T(8,128)(2,1)S(1)} %merge.1.ordered_after.own), channel_id=1, source_target_pairs={{0,1},{1,0},{2,3},{3,2},{4,5},{5,4},{6,7},{7,6},{8,9},{9,8},{10,11... | collective-permute-start | bytes 909320 | tf_op jit(solution)/shard_map/ppermute | solution.py:353
  7.7 15.3 %collective-permute-start.2 = (bf16[784,256]{1,0:T(8,128)(2,1)S(1)}, bf16[784,256]{1,0:T(8,128)(2,1)S(1)}, u32[]{:S(2)}, u32[]{:S(2)}) collective-permute-start(bf16[784,256]{1,0:T(8,128)(2,1)S(1)} %get-tuple-element.12.second_ref), channel_id=1, source_target_pairs={{0,16},{1,17},{2,18},{3,19},{4,20},{5,21},{6,22},{7,23},{8,24},{9,... | collective-permute-start | bytes 1204232 | tf_op jit(solution)/shard_map/ppermute | solution.py:353
  14.0 8.3 %collective-permute-start.5 = (bf16[1184,128]{1,0:T(8,128)(2,1)S(1)}, bf16[1184,128]{1,0:T(8,128)(2,1)S(1)}, u32[]{:S(2)}, u32[]{:S(2)}) collective-permute-start(bf16[1184,128]{1,0:T(8,128)(2,1)S(1)} %forward.2.ordered_after), channel_id=1, source_target_pairs={{0,1},{1,0},{2,3},{3,2},{4,5},{5,4},{6,7},{7,6},{8,12},{9,13},{10,... | collective-permute-start | bytes 909320 | tf_op jit(solution)/shard_map/ppermute | solution.py:353
  15.5 8.2 %collective-permute-start.8 = (bf16[1184,128]{1,0:T(8,128)(2,1)S(1)}, bf16[1184,128]{1,0:T(8,128)(2,1)S(1)}, u32[]{:S(2)}, u32[]{:S(2)}) collective-permute-start(bf16[1184,128]{1,0:T(8,128)(2,1)S(1)} %forward.3), channel_id=1, source_target_pairs={{0,4},{1,5},{2,0},{3,1},{4,6},{5,7},{6,2},{7,3},{8,9},{9,8},{10,11... | collective-permute-start | bytes 909320 | tf_op jit(solution)/shard_map/ppermute | solution.py:353
  20.0 4.1 %collective-permute-start.7 = (bf16[7808,128]{1,0:T(8,128)(2,1)S(1)}, bf16[7808,128]{1,0:T(8,128)(2,1)S(1)}, u32[]{:S(2)}, u32[]{:S(2)}) collective-permute-start(bf16[7808,128]{1,0:T(8,128)(2,1)S(1)} %swap.1), channel_id=1, source_target_pairs={{0,8},{1,9},{2,10},{3,11},{4,12},{5,13},{6,14},{7,15},{8,0},{9,1},... | collective-permute-start | bytes 5996552 | tf_op jit(solution)/shard_map/ppermute | solution.py:353
  22.3 2.8 %collective-permute-start.10 = (bf16[1184,128]{1,0:T(8,128)(2,1)S(1)}, bf16[1184,128]{1,0:T(8,128)(2,1)S(1)}, u32[]{:S(2)}, u32[]{:S(2)}) collective-permute-start(bf16[1184,128]{1,0:T(8,128)(2,1)S(1)} %pass_late.2.ordered_after), channel_id=1, source_target_pairs={{0,8},{1,9},{2,10},{3,11},{4,12},{5,13},{6,14},{7,15},{8,0},{9,1},... | collective-permute-start | bytes 909320 | tf_op jit(solution)/shard_map/ppermute | solution.py:353
  23.8 1.7 %collective-permute-start.9 = (bf16[1184,128]{1,0:T(8,128)(2,1)S(1)}, bf16[1184,128]{1,0:T(8,128)(2,1)S(1)}, u32[]{:S(2)}, u32[]{:S(2)}) collective-permute-start(bf16[1184,128]{1,0:T(8,128)(2,1)S(1)} %pass_late.3), channel_id=1, source_target_pairs={{0,8},{1,9},{2,10},{3,11},{4,12},{5,13},{6,14},{7,15},{8,0},{9,1},... | collective-permute-start | bytes 909320 | tf_op jit(solution)/shard_map/ppermute | solution.py:353

commit v10 on v7

--- a/solution.py
+++ b/solution.py
@@ -106,32 +106,37 @@
     copies[2].wait()
     rows, columns = depth // TILE, first_ref.shape[1] // TILE
     shift = jnp.where(r % 2 == 1, rows, 0)
-    for out_ref, low in ((first_ref, shift), (second_ref, rows - shift)):
-        for b in range(columns):
-            value = jnp.zeros((META, TILE), jnp.float32)
-            for a in range(rows):
-                value = jnp.where(line == a, ap_pattern[b, low + a].astype(jnp.float32), value)
-            out_ref[pl.ds(depth, META), pl.ds(b * TILE, TILE)] = value.astype(out_ref.dtype)
+    for b in range(columns):
+        value = jnp.zeros((META, TILE), jnp.float32)
+        for a in range(2 * rows):
+            row = lax.rem(shift + a, 2 * rows)
+            value = jnp.where(line == a, ap_pattern[b, row].astype(jnp.float32), value)
+        first_ref[pl.ds(depth, META), pl.ds(b * TILE, TILE)] = value.astype(first_ref.dtype)
     copies[3].wait()
     copies[4].wait()
 
 
-def mask_applied(ref, out_ref):
+def mask_applied(ref, first_ref, second, out_ref):
     depth = out_ref.shape[0]
-    pattern = ref[pl.ds(depth, META), :].astype(jnp.float32)
+    pattern = first_ref[pl.ds(depth, META), :].astype(jnp.float32)
     for a in range(depth // TILE):
-        weight = jnp.broadcast_to(pattern[a : a + 1, :], (META, out_ref.shape[1])).astype(ref.dtype)
+        k = a + second * (depth // TILE)
+        weight = jnp.broadcast_to(pattern[k : k + 1, :], (META, out_ref.shape[1])).astype(ref.dtype)
         rows = pl.ds(a * TILE, TILE)
         out_ref[rows, :] = (ref[rows, :].reshape(TILE // META, META, -1) * weight[None]).reshape(TILE, -1)
 
 
-def mask_kernel(ref, ordered_after, out_ref):
-    mask_applied(ref, out_ref)
+def mask_first_kernel(ref, ordered_after, out_ref):
+    mask_applied(ref, ref, 0, out_ref)
+
+
+def mask_second_kernel(ref, first_ref, ordered_after, out_ref):
+    mask_applied(ref, first_ref, 1, out_ref)
 
 
 def mask_own_kernel(first_ref, second_ref, first_out, second_out):
-    mask_applied(first_ref, first_out)
-    mask_applied(second_ref, second_out)
+    mask_applied(first_ref, first_ref, 0, first_out)
+    mask_applied(second_ref, first_ref, 1, second_out)
 
 
 def merge_kernel(keep_ref, got_ref, half_ref):
@@ -364,7 +369,7 @@
     half_ap = shape(depth, applied.shape[1])
     keep, send, raw_first, raw_second = call(
         functools.partial(prepare_kernel, cols), "prepare",
-        (shape(data + META, TILE),) * 2 + (shape(depth + META, applied.shape[1]),) * 2,
+        (shape(data + META, TILE),) * 2 + (shape(depth + META, applied.shape[1]), half_ap),
         *[pltpu.with_memory_space_constraint(x, pltpu.HBM) for x in (prolong, applied, prolong_pattern.T, applied_pattern.T)],
         specs=[hbm] * 4,
         scratch_shapes=[
@@ -401,7 +406,8 @@
         late.append(move(send_on, relay_pairs(step)))
         after = send_on
     own_first, own_second = call(mask_own_kernel, "mask_own", (half_ap,) * 2, raw_first, raw_second)
-    far_first = call(mask_kernel, "settle_first", half_ap, far_first, mine, weight=FIRST_WEIGHT)
+    far_raw = far_first
+    far_first = call(mask_first_kernel, "settle_first", half_ap, far_first, mine, weight=FIRST_WEIGHT)
     swap = call(
         swap_kernel, "swap", shape(len(FIRST) * size + 4 * depth, TILE), mine, side, pair, cross, own_second, far_first
     )
@@ -409,7 +415,7 @@
     result = jax.ShapeDtypeStruct((prolong.shape[1], applied.shape[1]), jnp.float32)
     sizes = (cols, half, width)
     partial = call(functools.partial(own_kernel, *sizes), "own", result, own_first, own_second, swap, side)
-    far_second = call(mask_kernel, "settle", half_ap, far_second, partial)
+    far_second = call(mask_second_kernel, "settle", half_ap, far_second, far_raw, partial)
     late_first = move(call(pass_kernel, "pass_late", shape(size, TILE), late[0], mine), partner)
     late_second = move(call(pass_kernel, "pass_late", shape(size, TILE), late[1], far_second, weight=LAST_WEIGHT), partner)
     beyond = [(r, r + 1 if r % 2 == 1 else r - 1) for r in range(rows)]

time: 26.8 us -> 26.8 us (level)
  no operation moved by 1% of the time
where the time goes in v10:
time: 26.8 us; the launch traced here: 26.6 us
  starting transfers between devices  13.5 us (50%)
  waiting for transfers between devices  7.79 us (29%)
  Pallas kernels  5.15 us (19%)
    ppermute x11, starting transfers between devices, move(): return lax.ppermute(x, AXES, pairs)  13.5 us
    ppermute x11, waiting for transfers between devices, move(): return lax.ppermute(x, AXES, pairs)  7.79 us
    pallas_call x13, Pallas kernels, call(): pl.pallas_call(kernel, out_shape=out_shape, in_specs=specs or [vmem] * le...  4.02 us
    pallas_call x1, Pallas kernels, on_device(): pl.pallas_call(functools.partial(last_kernel, *sizes), out_shape=result,...  1.13 us
  transfers between devices with their start and end apart: 11, of which 3 were waited for; matrix products, arithmetic and copies ran while one was open for 0% of the time, Pallas kernels for 10%

profile of v10, /device:TPU:0, one launch (start us, length us, event | category | flops | bytes accessed | tf_op | source)
XLA Modules:
  0.0 26.6 jit_solution(16675297393491196344)
XLA Ops:
  0.0 1.5 %prepare.1 = (bf16[1168,128]{1,0:T(8,128)(2,1)S(1)}, bf16[1168,128]{1,0:T(8,128)(2,1)S(1)}, bf16[784,256]{1,0:T(8,128)(2,1)S(1)}, bf16[768,256]{1,0:T(8,128)(2,1)S(1)}) custom-call(bf16[768,512]{1,0:T(8,128)(2,1)} %p_hbm.1, bf16[1536,256]{1,0:T(8,128)(2,1)} %ap_hbm.1, s32[4,6]{1,0:T(4,128)} %bitcast.2, s32[2,12]{1,0:T(2,128)} %bitcast.3), custom_call_target="tpu_custom_call" | custom-call | tf_op jit(solution)/shard_map/prepare/pallas_call | solution.py:351
  1.5 0.4 %collective-permute-start.1 = (bf16[1168,128]{1,0:T(8,128)(2,1)S(1)}, bf16[1168,128]{1,0:T(8,128)(2,1)S(1)}, u32[]{:S(2)}, u32[]{:S(2)}) collective-permute-start(bf16[1168,128]{1,0:T(8,128)(2,1)S(1)} %get-tuple-element.16), channel_id=1, source_target_pairs={{0,8},{1,9},{2,10},{3,11},{4,12},{5,13},{6,14},{7,15},{8,0},{9,1},... | collective-permute-start | bytes 897032 | tf_op jit(solution)/shard_map/ppermute | solution.py:357
  1.9 2.6 %collective-permute-start = (bf16[784,256]{1,0:T(8,128)(2,1)S(1)}, bf16[784,256]{1,0:T(8,128)(2,1)S(1)}, u32[]{:S(2)}, u32[]{:S(2)}) collective-permute-start(bf16[784,256]{1,0:T(8,128)(2,1)S(1)} %get-tuple-element.11.first_ref), channel_id=1, source_target_pairs={{0,16},{1,17},{2,18},{3,19},{4,20},{5,21},{6,22},{7,23},{8,24},{9,... | collective-permute-start | bytes 1204232 | tf_op jit(solution)/shard_map/ppermute | solution.py:357
  4.5 0.0 collective-permute-done.1.got_ref
  4.5 0.1 merge.1.ordered_after.own
  4.6 1.6 %collective-permute-start.4 = (bf16[1184,128]{1,0:T(8,128)(2,1)S(1)}, bf16[1184,128]{1,0:T(8,128)(2,1)S(1)}, u32[]{:S(2)}, u32[]{:S(2)}) collective-permute-start(bf16[1184,128]{1,0:T(8,128)(2,1)S(1)} %merge.1.ordered_after.own), channel_id=1, source_target_pairs={{0,2},{1,3},{2,0},{3,1},{4,6},{5,7},{6,4},{7,5},{8,10},{9,11},{10,... | collective-permute-start | bytes 909320 | tf_op jit(solution)/shard_map/ppermute | solution.py:357
  6.2 0.0 collective-permute-start.5
  6.3 1.5 %collective-permute-start.2 = (bf16[768,256]{1,0:T(8,128)(2,1)S(1)}, bf16[768,256]{1,0:T(8,128)(2,1)S(1)}, u32[]{:S(2)}, u32[]{:S(2)}) collective-permute-start(bf16[768,256]{1,0:T(8,128)(2,1)S(1)} %get-tuple-element.12.second_ref), channel_id=1, source_target_pairs={{0,16},{1,17},{2,18},{3,19},{4,20},{5,21},{6,22},{7,23},{8,24},{9,... | collective-permute-start | bytes 1179656 | tf_op jit(solution)/shard_map/ppermute | solution.py:357
  7.8 0.1 mask_own.1
  7.8 1.6 %collective-permute-start.3 = (bf16[1184,128]{1,0:T(8,128)(2,1)S(1)}, bf16[1184,128]{1,0:T(8,128)(2,1)S(1)}, u32[]{:S(2)}, u32[]{:S(2)}) collective-permute-start(bf16[1184,128]{1,0:T(8,128)(2,1)S(1)} %merge.1.ordered_after.own), channel_id=1, source_target_pairs={{0,1},{1,0},{2,3},{3,2},{4,5},{5,4},{6,7},{7,6},{8,9},{9,8},{10,11... | collective-permute-start | bytes 909320 | tf_op jit(solution)/shard_map/ppermute | solution.py:357
  9.4 4.5 %collective-permute-done.4.pair = bf16[1184,128]{1,0:T(8,128)(2,1)S(1)} collective-permute-done((bf16[1184,128]{1,0:T(8,128)(2,1)S(1)}, bf16[1184,128]{1,0:T(8,128)(2,1)S(1)}, u32[]{:S(2)}, u32[]{:S(2)}) %collective-permute-start.4) | collective-permute-done | bytes 303136 | tf_op jit(solution)/shard_map/ppermute | solution.py:357
  14.0 1.6 %collective-permute-start.9 = (bf16[1184,128]{1,0:T(8,128)(2,1)S(1)}, bf16[1184,128]{1,0:T(8,128)(2,1)S(1)}, u32[]{:S(2)}, u32[]{:S(2)}) collective-permute-start(bf16[1184,128]{1,0:T(8,128)(2,1)S(1)} %forward.2.ordered_after), channel_id=1, source_target_pairs={{0,1},{1,0},{2,3},{3,2},{4,5},{5,4},{6,7},{7,6},{8,12},{9,13},{10,... | collective-permute-start | bytes 909320 | tf_op jit(solution)/shard_map/ppermute | solution.py:357
  15.6 3.9 %collective-permute-start.7 = (bf16[1184,128]{1,0:T(8,128)(2,1)S(1)}, bf16[1184,128]{1,0:T(8,128)(2,1)S(1)}, u32[]{:S(2)}, u32[]{:S(2)}) collective-permute-start(bf16[1184,128]{1,0:T(8,128)(2,1)S(1)} %forward.3), channel_id=1, source_target_pairs={{0,4},{1,5},{2,0},{3,1},{4,6},{5,7},{6,2},{7,3},{8,9},{9,8},{10,11... | collective-permute-start | bytes 909320 | tf_op jit(solution)/shard_map/ppermute | solution.py:357
  19.5 0.4 %swap.1 = bf16[7808,128]{1,0:T(8,128)(2,1)S(1)} custom-call(bf16[1184,128]{1,0:T(8,128)(2,1)S(1)} %merge.1.ordered_after.own, bf16[1184,128]{1,0:T(8,128)(2,1)S(1)} %collective-permute-done.3.side, bf16[1184,128]{1,0:T(8,128)(2,1)S(1)} %collective-permute-done.4.pair, bf16[1184,128]{1,0:T(8,128)(2,1)S(1)} %collective-permute-done.5.cross.ordered_after, ...), custom_call_target="tpu_custom_call" | custom-call | tf_op jit(solution)/shard_map/swap/pallas_call | solution.py:351
  19.9 0.1 collective-permute-start.6
  20.0 0.4 %own.1.ordered_after.partial = f32[512,256]{1,0:T(8,128)S(1)} custom-call(bf16[768,256]{1,0:T(8,128)(2,1)S(1)} %get-tuple-element.13.own_first, bf16[768,256]{1,0:T(8,128)(2,1)S(1)} %get-tuple-element.14.own_second, bf16[7808,128]{1,0:T(8,128)(2,1)S(1)} %swap.1, bf16[1184,128]{1,0:T(8,128)(2,1)S(1)} %collective-permute-done.3.side), custom_call_target="tpu_custom_call" | custom-call | tf_op jit(solution)/shard_map/own/pallas_call | solution.py:351
  20.4 2.4 %collective-permute-done.2.ref = bf16[768,256]{1,0:T(8,128)(2,1)S(1)} collective-permute-done((bf16[768,256]{1,0:T(8,128)(2,1)S(1)}, bf16[768,256]{1,0:T(8,128)(2,1)S(1)}, u32[]{:S(2)}, u32[]{:S(2)}) %collective-permute-start.2) | collective-permute-done | bytes 393248 | tf_op jit(solution)/shard_map/ppermute | solution.py:357
  22.9 0.1 collective-permute-start.10
  23.0 0.8 %collective-permute-done.7.ref.late_second = bf16[1184,128]{1,0:T(8,128)(2,1)S(1)} collective-permute-done((bf16[1184,128]{1,0:T(8,128)(2,1)S(1)}, bf16[1184,128]{1,0:T(8,128)(2,1)S(1)}, u32[]{:S(2)}, u32[]{:S(2)}) %collective-permute-start.7) | collective-permute-done | bytes 303136 | tf_op jit(solution)/shard_map/ppermute | solution.py:357
  23.8 0.2 collective-permute-start.8
  24.0 0.0 collective-permute-done.6.swapped.cross_ap
  24.0 1.0 %near.1.partial = f32[512,256]{1,0:T(8,128)S(1)} custom-call(bf16[768,256]{1,0:T(8,128)(2,1)S(1)} %get-tuple-element.13.own_first, bf16[768,256]{1,0:T(8,128)(2,1)S(1)} %get-tuple-element.14.own_second, bf16[768,256]{1,0:T(8,128)(2,1)S(1)} %settle_first.1.far_first, bf16[768,256]{1,0:T(8,128)(2,1)S(1)} %settle.1.ordered_after.far_second, ...), custom_call_target="tpu_custom_call" | custom-call | tf_op jit(solution)/shard_map/near/pallas_call | solution.py:351
  25.1 0.4 %late.1.partial = f32[512,256]{1,0:T(8,128)S(1)} custom-call(bf16[768,256]{1,0:T(8,128)(2,1)S(1)} %get-tuple-element.13.own_first, bf16[768,256]{1,0:T(8,128)(2,1)S(1)} %get-tuple-element.14.own_second, bf16[768,256]{1,0:T(8,128)(2,1)S(1)} %settle_first.1.far_first, bf16[768,256]{1,0:T(8,128)(2,1)S(1)} %settle.1.ordered_after.far_second, ...), custom_call_target="tpu_custom_call" | custom-call | tf_op jit(solution)/shard_map/late/pallas_call | solution.py:351
  25.5 1.1 %last.1 = f32[512,256]{1,0:T(8,128)} custom-call(bf16[768,256]{1,0:T(8,128)(2,1)S(1)} %get-tuple-element.13.own_first, bf16[768,256]{1,0:T(8,128)(2,1)S(1)} %get-tuple-element.14.own_second, bf16[768,256]{1,0:T(8,128)(2,1)S(1)} %settle_first.1.far_first, bf16[768,256]{1,0:T(8,128)(2,1)S(1)} %settle.1.ordered_after.far_second, ...), custom_call_target="tpu_custom_call" | custom-call | tf_op jit(solution)/shard_map/last/pallas_call | solution.py:433
  (12 shorter events, 0.2 us)
Async XLA Ops:
  1.5 3.1 %collective-permute-start.1 = (bf16[1168,128]{1,0:T(8,128)(2,1)S(1)}, bf16[1168,128]{1,0:T(8,128)(2,1)S(1)}, u32[]{:S(2)}, u32[]{:S(2)}) collective-permute-start(bf16[1168,128]{1,0:T(8,128)(2,1)S(1)} %get-tuple-element.16), channel_id=1, source_target_pairs={{0,8},{1,9},{2,10},{3,11},{4,12},{5,13},{6,14},{7,15},{8,0},{9,1},... | collective-permute-start | bytes 897032 | tf_op jit(solution)/shard_map/ppermute | solution.py:357
  1.9 17.5 %collective-permute-start = (bf16[784,256]{1,0:T(8,128)(2,1)S(1)}, bf16[784,256]{1,0:T(8,128)(2,1)S(1)}, u32[]{:S(2)}, u32[]{:S(2)}) collective-permute-start(bf16[784,256]{1,0:T(8,128)(2,1)S(1)} %get-tuple-element.11.first_ref), channel_id=1, source_target_pairs={{0,16},{1,17},{2,18},{3,19},{4,20},{5,21},{6,22},{7,23},{8,24},{9,... | collective-permute-start | bytes 1204232 | tf_op jit(solution)/shard_map/ppermute | solution.py:357
  4.6 9.3 %collective-permute-start.4 = (bf16[1184,128]{1,0:T(8,128)(2,1)S(1)}, bf16[1184,128]{1,0:T(8,128)(2,1)S(1)}, u32[]{:S(2)}, u32[]{:S(2)}) collective-permute-start(bf16[1184,128]{1,0:T(8,128)(2,1)S(1)} %merge.1.ordered_after.own), channel_id=1, source_target_pairs={{0,2},{1,3},{2,0},{3,1},{4,6},{5,7},{6,4},{7,5},{8,10},{9,11},{10,... | collective-permute-start | bytes 909320 | tf_op jit(solution)/shard_map/ppermute | solution.py:357
  6.2 7.7 %collective-permute-start.5 = (bf16[1184,128]{1,0:T(8,128)(2,1)S(1)}, bf16[1184,128]{1,0:T(8,128)(2,1)S(1)}, u32[]{:S(2)}, u32[]{:S(2)}) collective-permute-start(bf16[1184,128]{1,0:T(8,128)(2,1)S(1)} %merge.1.ordered_after.own), channel_id=1, source_target_pairs={{0,8},{1,9},{2,4},{3,5},{4,2},{5,3},{6,14},{7,15},{8,0},{9,1},{10,... | collective-permute-start | bytes 909320 | tf_op jit(solution)/shard_map/ppermute | solution.py:357
  6.3 16.6 %collective-permute-start.2 = (bf16[768,256]{1,0:T(8,128)(2,1)S(1)}, bf16[768,256]{1,0:T(8,128)(2,1)S(1)}, u32[]{:S(2)}, u32[]{:S(2)}) collective-permute-start(bf16[768,256]{1,0:T(8,128)(2,1)S(1)} %get-tuple-element.12.second_ref), channel_id=1, source_target_pairs={{0,16},{1,17},{2,18},{3,19},{4,20},{5,21},{6,22},{7,23},{8,24},{9,... | collective-permute-start | bytes 1179656 | tf_op jit(solution)/shard_map/ppermute | solution.py:357
  7.8 11.7 %collective-permute-start.3 = (bf16[1184,128]{1,0:T(8,128)(2,1)S(1)}, bf16[1184,128]{1,0:T(8,128)(2,1)S(1)}, u32[]{:S(2)}, u32[]{:S(2)}) collective-permute-start(bf16[1184,128]{1,0:T(8,128)(2,1)S(1)} %merge.1.ordered_after.own), channel_id=1, source_target_pairs={{0,1},{1,0},{2,3},{3,2},{4,5},{5,4},{6,7},{7,6},{8,9},{9,8},{10,11... | collective-permute-start | bytes 909320 | tf_op jit(solution)/shard_map/ppermute | solution.py:357
  14.0 8.9 %collective-permute-start.9 = (bf16[1184,128]{1,0:T(8,128)(2,1)S(1)}, bf16[1184,128]{1,0:T(8,128)(2,1)S(1)}, u32[]{:S(2)}, u32[]{:S(2)}) collective-permute-start(bf16[1184,128]{1,0:T(8,128)(2,1)S(1)} %forward.2.ordered_after), channel_id=1, source_target_pairs={{0,1},{1,0},{2,3},{3,2},{4,5},{5,4},{6,7},{7,6},{8,12},{9,13},{10,... | collective-permute-start | bytes 909320 | tf_op jit(solution)/shard_map/ppermute | solution.py:357
  15.6 8.2 %collective-permute-start.7 = (bf16[1184,128]{1,0:T(8,128)(2,1)S(1)}, bf16[1184,128]{1,0:T(8,128)(2,1)S(1)}, u32[]{:S(2)}, u32[]{:S(2)}) collective-permute-start(bf16[1184,128]{1,0:T(8,128)(2,1)S(1)} %forward.3), channel_id=1, source_target_pairs={{0,4},{1,5},{2,0},{3,1},{4,6},{5,7},{6,2},{7,3},{8,9},{9,8},{10,11... | collective-permute-start | bytes 909320 | tf_op jit(solution)/shard_map/ppermute | solution.py:357
  19.9 4.1 %collective-permute-start.6 = (bf16[7808,128]{1,0:T(8,128)(2,1)S(1)}, bf16[7808,128]{1,0:T(8,128)(2,1)S(1)}, u32[]{:S(2)}, u32[]{:S(2)}) collective-permute-start(bf16[7808,128]{1,0:T(8,128)(2,1)S(1)} %swap.1), channel_id=1, source_target_pairs={{0,8},{1,9},{2,10},{3,11},{4,12},{5,13},{6,14},{7,15},{8,0},{9,1},... | collective-permute-start | bytes 5996552 | tf_op jit(solution)/shard_map/ppermute | solution.py:357
  22.9 2.1 %collective-permute-start.10 = (bf16[1184,128]{1,0:T(8,128)(2,1)S(1)}, bf16[1184,128]{1,0:T(8,128)(2,1)S(1)}, u32[]{:S(2)}, u32[]{:S(2)}) collective-permute-start(bf16[1184,128]{1,0:T(8,128)(2,1)S(1)} %pass_late.3), channel_id=1, source_target_pairs={{0,8},{1,9},{2,10},{3,11},{4,12},{5,13},{6,14},{7,15},{8,0},{9,1},... | collective-permute-start | bytes 909320 | tf_op jit(solution)/shard_map/ppermute | solution.py:357
  23.8 1.7 %collective-permute-start.8 = (bf16[1184,128]{1,0:T(8,128)(2,1)S(1)}, bf16[1184,128]{1,0:T(8,128)(2,1)S(1)}, u32[]{:S(2)}, u32[]{:S(2)}) collective-permute-start(bf16[1184,128]{1,0:T(8,128)(2,1)S(1)} %pass_late.2), channel_id=1, source_target_pairs={{0,8},{1,9},{2,10},{3,11},{4,12},{5,13},{6,14},{7,15},{8,0},{9,1},... | collective-permute-start | bytes 909320 | tf_op jit(solution)/shard_map/ppermute | solution.py:357
